TPU v7x, 128 devices: a whole 4x4x4 slice. The times are simulated.
128 devices in a mesh: gx: 4 (over z), gy: 4 (over y), gz: 8 (over x, core).
Axes of the slice: x: 4, y: 4, z: 4, core: 2. Of those that a mesh axis runs over, the one named last changes fastest.
Arguments:
- source: float32 [64, 128, 1024], P('gx', 'gy', 'gz'), may hold values from -6 to 6
- conductance: float32 [64, 128, 1024], P('gx', 'gy', 'gz'), may hold values from 0.25 to 4
Outputs:
- solution_field: float32 [64, 128, 1024], P('gx', 'gy', 'gz')
- residual: float32 [64, 128, 1024], P('gx', 'gy', 'gz')
All inputs are finite; a program needn't handle non-finite values.
Results may differ from a plain program's by a relative error of at most 0.0003.
Values sent between devices are 32-bit elements; how exact they have to be, the bound alone decides.
No kernel may reach another device: no remote copies, remote signals or barrier semaphores. Data moves between devices by JAX's collectives and lax.ppermute only.
A program may use at most 128 MiB of HBM per device.

v0:
```python
import jax
import jax.numpy as jnp
from jax import lax
from jax.sharding import PartitionSpec as P

LEVELS = 4
SWEEPS = 2
COARSE_ITERS = 20


def with_halo(cells, sides, width):
    for axis, dim in sides:
        count = lax.axis_size(axis)
        ends = count - 1
        head = lax.slice_in_dim(cells, 0, width, axis=dim)
        tail = lax.slice_in_dim(cells, cells.shape[dim] - width, cells.shape[dim], axis=dim)
        cells = jnp.concatenate(
            [
                lax.ppermute(tail, axis, [(i, (i + 1) % count) for i in range(ends)]),
                cells,
                lax.ppermute(head, axis, [((i + 1) % count, i) for i in range(ends)]),
            ],
            axis=dim,
        )
    return cells


def coefficients(padded_b):
    center = padded_b[1:-1, 1:-1, 1:-1]
    return (
        0.5 * (center + padded_b[:-2, 1:-1, 1:-1]),
        0.5 * (center + padded_b[2:, 1:-1, 1:-1]),
        0.5 * (center + padded_b[1:-1, :-2, 1:-1]),
        0.5 * (center + padded_b[1:-1, 2:, 1:-1]),
        0.5 * (center + padded_b[1:-1, 1:-1, :-2]),
        0.5 * (center + padded_b[1:-1, 1:-1, 2:]),
    )


def operate(padded, face_coef, factor):
    center = padded[1:-1, 1:-1, 1:-1]
    beside = (
        padded[:-2, 1:-1, 1:-1],
        padded[2:, 1:-1, 1:-1],
        padded[1:-1, :-2, 1:-1],
        padded[1:-1, 2:, 1:-1],
        padded[1:-1, 1:-1, :-2],
        padded[1:-1, 1:-1, 2:],
    )
    summed = face_coef[0] * (center - beside[0])
    for which in range(1, 6):
        summed = summed + face_coef[which] * (center - beside[which])
    return factor * summed


def diagonal_of(face_coef, factor):
    summed = face_coef[0]
    for which in range(1, 6):
        summed = summed + face_coef[which]
    return factor * summed


def checker(shape):
    parity = (
        lax.broadcasted_iota(jnp.int32, shape, 0)
        + lax.broadcasted_iota(jnp.int32, shape, 1)
        + lax.broadcasted_iota(jnp.int32, shape, 2)
    )
    return parity % 2 == 0


def coarsen(field):
    sx, sy, sz = field.shape
    return jnp.sum(field.reshape(sx // 2, 2, sy // 2, 2, sz // 2, 2), axis=(1, 3, 5)) * 0.125


def refine(field):
    return jnp.repeat(jnp.repeat(jnp.repeat(field, 2, 0), 2, 1), 2, 2)


def coef_halo(beta):
    return with_halo(beta, (("gx", 0), ("gy", 1), ("gz", 2)), 2)


def outer_layer(field):
    return with_halo(field, (("gx", 0), ("gy", 1), ("gz", 2)), 1)


def residual_layer(field):
    return with_halo(field, (("gx", 0), ("gy", 1), ("gz", 2)), 1)


def make_level(beta, current, factor):
    coef_ext = coefficients(coef_halo(beta))
    coef_int = tuple((part[1:-1, 1:-1, 1:-1] for part in coef_ext))
    setup = {
        "coef_int": coef_int,
        "diag_int": diagonal_of(coef_int, factor),
        "red_int": checker(current.shape),
        "factor": factor,
        "source": current,
    }
    return setup


def local_sweep(field, setup):
    factor = setup["factor"]
    for chosen in (setup["red_int"], jnp.logical_not(setup["red_int"])):
        applied = operate(outer_layer(field), setup["coef_int"], factor)
        field = jnp.where(chosen, field + (setup["source"] - applied) / setup["diag_int"], field)
    return field


def whole_sweep(field, source, face_coef, diagonal, red_cells, factor):
    for chosen in (red_cells, jnp.logical_not(red_cells)):
        applied = operate(jnp.pad(field, 1), face_coef, factor)
        field = jnp.where(chosen, field + (source - applied) / diagonal, field)
    return field


def gather_whole(current, local_b):
    whole_s, whole_b = (
        lax.all_gather(current, "gz", axis=2, tiled=True),
        lax.all_gather(local_b, "gz", axis=2, tiled=True),
    )
    whole_s, whole_b = (
        lax.all_gather(whole_s, "gy", axis=1, tiled=True),
        lax.all_gather(whole_b, "gy", axis=1, tiled=True),
    )
    return (
        lax.all_gather(whole_s, "gx", axis=0, tiled=True),
        lax.all_gather(whole_b, "gx", axis=0, tiled=True),
    )


def body(source, conductance):
    split = LEVELS
    betas = [conductance]
    for level in range(split):
        betas.append(coarsen(betas[-1]))
    stored = []
    current = source
    for level in range(split):
        setup = make_level(betas[level], current, 0.25**level)
        field = jnp.zeros_like(current)
        for count in range(SWEEPS):
            field = local_sweep(field, setup)
        applied = operate(residual_layer(field), setup["coef_int"], setup["factor"])
        stored.append((field, setup))
        current = coarsen(current - applied)
    bx, by, bz = current.shape
    whole_s, whole_b = gather_whole(current, betas[split])
    factor = 0.25**LEVELS
    face_coef = coefficients(jnp.pad(whole_b, 1))
    diagonal = diagonal_of(face_coef, factor)
    red_cells = checker(whole_s.shape)

    def coarse_step(count, field):
        return whole_sweep(field, whole_s, face_coef, diagonal, red_cells, factor)

    solved = lax.fori_loop(0, COARSE_ITERS, coarse_step, jnp.zeros_like(whole_s))
    coarse = lax.dynamic_slice(
        solved,
        (lax.axis_index("gx") * bx, lax.axis_index("gy") * by, lax.axis_index("gz") * bz),
        (bx, by, bz),
    )
    for level in range(split - 1, -1, -1):
        field, setup = stored[level]
        field = field + refine(coarse)
        for count in range(SWEEPS):
            field = local_sweep(field, setup)
        coarse = field
    setup = stored[0][1]
    residual = source - operate(residual_layer(coarse), setup["coef_int"], 1.0)
    return (coarse, residual)


def solution(mesh):
    placed = (P("gx", "gy", "gz"), P("gx", "gy", "gz"))
    return jax.shard_map(
        body,
        mesh=mesh,
        in_specs=placed,
        out_specs=(P("gx", "gy", "gz"), P("gx", "gy", "gz")),
        check_vma=False,
    )
```

profile of v0, /device:TPU:1, one launch (start us, length us, event | category | flops | bytes accessed | tf_op | source)
XLA Modules:
  0.0 1058.2 jit_solution(4312362867558506428)
XLA Ops:
  16.7 18.9 %reshape.85 = f32[8,2,16,2,64,2]{5,4,3,2,1,0:T(8,128)} reshape(f32[16,32,128]{2,1,0:T(8,128)} %param.5) | data formatting | bytes 524288 | tf_op jit(solution)/shard_map/reshape | solution.py:74
  35.6 7.0 reduce_sum.87
  49.0 13.0 %all-gather.6 = f32[8,8,2]{1,2,0:T(2,128)} all-gather(f32[1,8,2]{1,2,0:T(2,128)S(1)} %multiply_bitcast_fusion.1), channel_id=2, replica_groups=mesh['gx'=4,'gy'=4,'gz'=8] {'gz'}, dimensions={0}, use_global_device_ids=true | all-gather | bytes 576 | tf_op jit(solution)/shard_map/all_gather | solution.py:124
  124.5 4.9 collective-permute-start.16
  243.4 18.1 %reshape.84 = f32[8,2,16,2,64,2]{5,4,3,2,1,0:T(8,128)} reshape(f32[16,32,128]{2,1,0:T(8,128)S(1)} %fusion.154) | data formatting | bytes 524288 | tf_op jit(solution)/shard_map/reshape | solution.py:74
  261.5 7.0 reduce_sum.86
  285.1 5.6 collective-permute-start.82
  321.2 6.2 collective-permute-start.58
  373.6 6.4 collective-permute-start.70
  396.3 5.2 all-gather.7
  411.1 6.0 collective-permute-start.88
  440.6 7.1 collective-permute-start.94
  464.8 5.9 collective-permute-start.118
  477.1 4.8 collective-permute-start.100
  518.0 9.1 all-gather.2
  533.1 6.5 collective-permute-start.124
  558.3 4.8 collective-permute-start.130
  604.9 4.8 collective-permute-start.142
  615.0 8.1 all-gather.8
  623.2 5.2 all-gather.9
  628.5 9.0 all-gather.5
  655.4 9.6 collective-permute-start.148
  707.7 4.8 collective-permute-start.160
  752.0 4.8 collective-permute-start.172
  (877 shorter events, 873.6 us)
Async XLA Ops:
  0.6 61.4 %collective-permute-start.6 = (f32[1,32,128]{2,1,0:T(8,128)S(1)}, f32[1,32,128]{2,1,0:T(8,128)S(1)}, u32[]{:S(2)}, u32[]{:S(2)}) collective-permute-start(f32[1,32,128]{2,1,0:T(8,128)S(1)} %broadcast.146), channel_id=1, source_target_pairs={{0,32},{32,64},{64,96},{1,33},{33,65},{65,97},{2,34},{34,66},{66,9... | collective-permute-start | bytes 49160 | tf_op jit(solution)/shard_map/ppermute | solution.py:19
  5.0 58.3 %collective-permute-start.7 = (f32[1,32,128]{2,1,0:T(8,128)S(1)}, f32[1,32,128]{2,1,0:T(8,128)S(1)}, u32[]{:S(2)}, u32[]{:S(2)}) collective-permute-start(f32[1,32,128]{2,1,0:T(8,128)S(1)} %broadcast.146), channel_id=1, source_target_pairs={{32,0},{64,32},{96,64},{33,1},{65,33},{97,65},{34,2},{66,34},{98,6... | collective-permute-start | bytes 49160 | tf_op jit(solution)/shard_map/ppermute | solution.py:21
  6.3 143.0 %collective-permute-start.42 = (f32[1,16,64]{2,1,0:T(8,128)S(1)}, f32[1,16,64]{2,1,0:T(8,128)S(1)}, u32[]{:S(2)}, u32[]{:S(2)}) collective-permute-start(f32[1,16,64]{2,1,0:T(8,128)S(1)} %broadcast.150), channel_id=1, source_target_pairs={{0,32},{32,64},{64,96},{1,33},{33,65},{65,97},{2,34},{34,66},{66,9... | collective-permute-start | bytes 12296 | tf_op jit(solution)/shard_map/ppermute | solution.py:19
  10.5 141.7 %collective-permute-start.43 = (f32[1,16,64]{2,1,0:T(8,128)S(1)}, f32[1,16,64]{2,1,0:T(8,128)S(1)}, u32[]{:S(2)}, u32[]{:S(2)}) collective-permute-start(f32[1,16,64]{2,1,0:T(8,128)S(1)} %broadcast.150), channel_id=1, source_target_pairs={{32,0},{64,32},{96,64},{33,1},{65,33},{97,65},{34,2},{66,34},{98,6... | collective-permute-start | bytes 12296 | tf_op jit(solution)/shard_map/ppermute | solution.py:21
  12.6 55.0 %collective-permute-start = (f32[2,32,128]{2,1,0:T(8,128)S(1)}, f32[2,32,128]{2,1,0:T(8,128)S(1)}, u32[]{:S(2)}, u32[]{:S(2)}) collective-permute-start(f32[2,32,128]{2,1,0:T(8,128)S(1)} %get-tuple-element.335), channel_id=1, source_target_pairs={{0,32},{32,64},{64,96},{1,33},{33,65},{65,97},{2,34},{34,66},{66,9... | collective-permute-start | bytes 98312 | tf_op jit(solution)/shard_map/ppermute | solution.py:19
  63.4 44.0 %collective-permute-start.78 = (f32[1,8,32]{2,1,0:T(8,128)S(1)}, f32[1,8,32]{2,1,0:T(8,128)S(1)}, u32[]{:S(2)}, u32[]{:S(2)}) collective-permute-start(f32[1,8,32]{2,1,0:T(8,128)S(1)} %broadcast.155), channel_id=1, source_target_pairs={{0,32},{32,64},{64,96},{1,33},{33,65},{65,97},{2,34},{34,66},{66,9... | collective-permute-start | bytes 3080 | tf_op jit(solution)/shard_map/ppermute | solution.py:19
  98.4 12.3 %collective-permute-start.79 = (f32[1,8,32]{2,1,0:T(8,128)S(1)}, f32[1,8,32]{2,1,0:T(8,128)S(1)}, u32[]{:S(2)}, u32[]{:S(2)}) collective-permute-start(f32[1,8,32]{2,1,0:T(8,128)S(1)} %broadcast.155), channel_id=1, source_target_pairs={{32,0},{64,32},{96,64},{33,1},{65,33},{97,65},{34,2},{66,34},{98,6... | collective-permute-start | bytes 3080 | tf_op jit(solution)/shard_map/ppermute | solution.py:21
  102.8 325.0 %collective-permute-start.108 = (f32[2,4,16]{2,1,0:T(4,128)S(1)}, f32[2,4,16]{2,1,0:T(4,128)S(1)}, u32[]{:S(2)}, u32[]{:S(2)}) collective-permute-start(f32[2,4,16]{2,1,0:T(4,128)S(1)} %get-tuple-element.538), channel_id=1, source_target_pairs={{0,32},{32,64},{64,96},{1,33},{33,65},{65,97},{2,34},{34,66},{66,9... | collective-permute-start | bytes 1544 | tf_op jit(solution)/shard_map/ppermute | solution.py:19
  143.3 285.8 %collective-permute-start.109 = (f32[2,4,16]{2,1,0:T(4,128)S(1)}, f32[2,4,16]{2,1,0:T(4,128)}, u32[]{:S(2)}, u32[]{:S(2)}) collective-permute-start(f32[2,4,16]{2,1,0:T(4,128)S(1)} %get-tuple-element.538), channel_id=1, source_target_pairs={{32,0},{64,32},{96,64},{33,1},{65,33},{97,65},{34,2},{66,34},{98,6... | collective-permute-start | bytes 1544 | tf_op jit(solution)/shard_map/ppermute | solution.py:21
  146.5 38.3 %collective-permute-start.36 = (f32[2,16,64]{2,1,0:T(8,128)S(1)}, f32[2,16,64]{2,1,0:T(8,128)S(1)}, u32[]{:S(2)}, u32[]{:S(2)}) collective-permute-start(f32[2,16,64]{2,1,0:T(8,128)S(1)} %get-tuple-element.397), channel_id=1, source_target_pairs={{0,32},{32,64},{64,96},{1,33},{33,65},{65,97},{2,34},{34,66},{66,9... | collective-permute-start | bytes 24584 | tf_op jit(solution)/shard_map/ppermute | solution.py:19
  180.6 124.9 %collective-permute-start.72 = (f32[2,8,32]{2,1,0:T(8,128)}, f32[2,8,32]{2,1,0:T(8,128)}, u32[]{:S(2)}, u32[]{:S(2)}) collective-permute-start(f32[2,8,32]{2,1,0:T(8,128)} %get-tuple-element.505), channel_id=1, source_target_pairs={{0,32},{32,64},{64,96},{1,33},{33,65},{65,97},{2,34},{34,66},{66,9... | collective-permute-start | bytes 6152 | tf_op jit(solution)/shard_map/ppermute | solution.py:19
  236.6 31.8 %collective-permute-start.46 = (f32[10,18,1]{2,1,0:T(8,128)}, f32[10,18,1]{2,1,0:T(8,128)}, u32[]{:S(2)}, u32[]{:S(2)}) collective-permute-start(f32[10,18,1]{2,1,0:T(8,128)} %get-tuple-element.359), channel_id=1, source_target_pairs={{0,1},{1,2},{2,3},{3,4},{4,5},{5,6},{6,7},{8,9},{9,10},{10,11},{11... | collective-permute-start | bytes 2168 | tf_op jit(solution)/shard_map/ppermute | solution.py:19
  241.0 28.8 %collective-permute-start.47 = (f32[10,18,1]{2,1,0:T(8,128)}, f32[10,18,1]{2,1,0:T(8,128)}, u32[]{:S(2)}, u32[]{:S(2)}) collective-permute-start(f32[10,18,1]{2,1,0:T(8,128)} %get-tuple-element.360), channel_id=1, source_target_pairs={{1,0},{2,1},{3,2},{4,3},{5,4},{6,5},{7,6},{9,8},{10,9},{11,10},{12... | collective-permute-start | bytes 2168 | tf_op jit(solution)/shard_map/ppermute | solution.py:21
  303.1 103.1 %collective-permute-start.114 = (f32[1,4,16]{2,1,0:T(4,128)S(1)}, f32[1,4,16]{2,1,0:T(4,128)S(1)}, u32[]{:S(2)}, u32[]{:S(2)}) collective-permute-start(f32[1,4,16]{2,1,0:T(4,128)S(1)} %broadcast.160), channel_id=1, source_target_pairs={{0,32},{32,64},{64,96},{1,33},{33,65},{65,97},{2,34},{34,66},{66,9... | collective-permute-start | bytes 776 | tf_op jit(solution)/shard_map/ppermute | solution.py:19
  411.1 11.6 %collective-permute-start.88 = (f32[6,10,1]{2,0,1:T(8,128)S(1)}, f32[6,10,1]{2,0,1:T(8,128)S(1)}, u32[]{:S(2)}, u32[]{:S(2)}) collective-permute-start(f32[6,10,1]{2,0,1:T(8,128)S(1)} %get-tuple-element.438), channel_id=1, source_target_pairs={{0,1},{1,2},{2,3},{3,4},{4,5},{5,6},{6,7},{8,9},{9,10},{10,11},{11... | collective-permute-start | bytes 728 | tf_op jit(solution)/shard_map/ppermute | solution.py:19
  419.0 37.4 %collective-permute-start.116 = (f32[4,1,16]{2,1,0:T(1,128)S(1)}, f32[4,1,16]{2,1,0:T(1,128)S(1)}, u32[]{:S(2)}, u32[]{:S(2)}) collective-permute-start(f32[4,1,16]{2,1,0:T(1,128)S(1)} %get-tuple-element.525), channel_id=1, source_target_pairs={{0,8},{8,16},{16,24},{1,9},{9,17},{17,25},{2,10},{10,18},{18,26},{... | collective-permute-start | bytes 776 | tf_op jit(solution)/shard_map/ppermute | solution.py:19
  422.7 35.0 %collective-permute-start.117 = (f32[4,1,16]{2,1,0:T(1,128)S(1)}, f32[4,1,16]{2,1,0:T(1,128)S(1)}, u32[]{:S(2)}, u32[]{:S(2)}) collective-permute-start(f32[4,1,16]{2,1,0:T(1,128)S(1)} %get-tuple-element.526), channel_id=1, source_target_pairs={{8,0},{16,8},{24,16},{9,1},{17,9},{25,17},{10,2},{18,10},{26,18},{... | collective-permute-start | bytes 776 | tf_op jit(solution)/shard_map/ppermute | solution.py:21
  449.6 32.3 %collective-permute-start.110 = (f32[6,2,16]{2,1,0:T(2,128)S(1)}, f32[6,2,16]{2,1,0:T(2,128)S(1)}, u32[]{:S(2)}, u32[]{:S(2)}) collective-permute-start(f32[6,2,16]{2,1,0:T(2,128)S(1)} %get-tuple-element.507), channel_id=1, source_target_pairs={{0,8},{8,16},{16,24},{1,9},{9,17},{17,25},{2,10},{10,18},{18,26},{... | collective-permute-start | bytes 2312 | tf_op jit(solution)/shard_map/ppermute | solution.py:19
  451.2 32.6 %collective-permute-start.111 = (f32[6,2,16]{2,1,0:T(2,128)S(1)}, f32[6,2,16]{2,1,0:T(2,128)S(1)}, u32[]{:S(2)}, u32[]{:S(2)}) collective-permute-start(f32[6,2,16]{2,1,0:T(2,128)S(1)} %get-tuple-element.508), channel_id=1, source_target_pairs={{8,0},{16,8},{24,16},{9,1},{17,9},{25,17},{10,2},{18,10},{26,18},{... | collective-permute-start | bytes 2312 | tf_op jit(solution)/shard_map/ppermute | solution.py:21
  460.8 11.9 %collective-permute-start.98 = (f32[6,1,32]{2,1,0:T(1,128)S(1)}, f32[6,1,32]{2,1,0:T(1,128)S(1)}, u32[]{:S(2)}, u32[]{:S(2)}) collective-permute-start(f32[6,1,32]{2,1,0:T(1,128)S(1)} %get-tuple-element.463), channel_id=1, source_target_pairs={{0,8},{8,16},{16,24},{1,9},{9,17},{17,25},{2,10},{10,18},{18,26},{... | collective-permute-start | bytes 2312 | tf_op jit(solution)/shard_map/ppermute | solution.py:19
  464.8 47.4 %collective-permute-start.118 = (f32[4,6,1]{2,1,0:T(8,128)S(1)}, f32[4,6,1]{2,1,0:T(8,128)S(1)}, u32[]{:S(2)}, u32[]{:S(2)}) collective-permute-start(f32[4,6,1]{2,1,0:T(8,128)S(1)} %get-tuple-element.497), channel_id=1, source_target_pairs={{0,1},{1,2},{2,3},{3,4},{4,5},{5,6},{6,7},{8,9},{9,10},{10,11},{11... | collective-permute-start | bytes 296 | tf_op jit(solution)/shard_map/ppermute | solution.py:19
  470.7 41.5 %collective-permute-start.119 = (f32[4,6,1]{2,1,0:T(8,128)S(1)}, f32[4,6,1]{2,1,0:T(8,128)S(1)}, u32[]{:S(2)}, u32[]{:S(2)}) collective-permute-start(f32[4,6,1]{2,1,0:T(8,128)S(1)} %get-tuple-element.498), channel_id=1, source_target_pairs={{1,0},{2,1},{3,2},{4,3},{5,4},{6,5},{7,6},{9,8},{10,9},{11,10},{12... | collective-permute-start | bytes 296 | tf_op jit(solution)/shard_map/ppermute | solution.py:21
  512.4 14.6 %collective-permute-start.120 = (f32[1,4,16]{2,1,0:T(4,128)S(1)}, f32[1,4,16]{2,1,0:T(4,128)S(1)}, u32[]{:S(2)}, u32[]{:S(2)}) collective-permute-start(f32[1,4,16]{2,1,0:T(4,128)S(1)} %get-tuple-element.543), channel_id=1, source_target_pairs={{0,32},{32,64},{64,96},{1,33},{33,65},{65,97},{2,34},{34,66},{66,9... | collective-permute-start | bytes 776 | tf_op jit(solution)/shard_map/ppermute | solution.py:19
  655.4 11.6 %collective-permute-start.148 = (f32[4,6,1]{2,1,0:T(8,128)S(1)}, f32[4,6,1]{2,1,0:T(8,128)S(1)}, u32[]{:S(2)}, u32[]{:S(2)}) collective-permute-start(f32[4,6,1]{2,1,0:T(8,128)S(1)} %get-tuple-element.485), channel_id=1, source_target_pairs={{0,1},{1,2},{2,3},{3,4},{4,5},{5,6},{6,7},{8,9},{9,10},{10,11},{11... | collective-permute-start | bytes 296 | tf_op jit(solution)/shard_map/ppermute | solution.py:19
  (237 other events, 2183.3 us)
where the time goes:
time: 1070 us; the launch traced here: 1060 us
  starting transfers between devices  592 us (55%)
  waiting for transfers between devices  313 us (29%)
  local copies, waits for them, and re-layouts  58.4 us (5%)
  blocking collectives  49.7 us (5%)
  other arithmetic  38.5 us (4%)
    ppermute x123, starting transfers between devices, with_halo(): lax.ppermute(tail, axis, [(i, (i + 1) % count) for i in range(ends)])  406 us
    ppermute x123, waiting for transfers between devices, with_halo(): lax.ppermute(head, axis, [((i + 1) % count, i) for i in range(ends)])  288 us
    ppermute x123, starting transfers between devices, with_halo(): lax.ppermute(head, axis, [((i + 1) % count, i) for i in range(ends)])  186 us
    reshape x4, local copies, waits for them, and re-layouts, coarsen(): field.reshape(sx // 2, 2, sy // 2, 2, sz // 2, 2)  40.6 us
    ppermute x123, waiting for transfers between devices, with_halo(): lax.ppermute(tail, axis, [(i, (i + 1) % count) for i in range(ends)])  25.5 us
  transfers between devices with their start and end apart: 246, of which 104 were waited for; matrix products, arithmetic and copies ran while one was open for 8% of the time, Pallas kernels for 0%

commit v1 on v0

v1 whole, which is shorter than its diff:
```python
import functools

import jax
import jax.numpy as jnp
from jax import lax
from jax.experimental import pallas as pl
from jax.experimental.pallas import tpu as pltpu
from jax.sharding import PartitionSpec as P

F32 = jnp.float32
COARSE_ITERS = 20
MIB = 1 << 20


def lanes(rows):
    return lax.broadcasted_iota(jnp.int32, (rows, 128), 1)


def sublanes(rows):
    return lax.broadcasted_iota(jnp.int32, (rows, 128), 0)


def pick(x, idx):
    return jnp.take_along_axis(x, idx, axis=1, mode="promise_in_bounds")


def turn(x, shift):
    shift = shift % 128
    return pltpu.roll(x, shift, 1) if shift else x


def side_index(rows, parity, period):
    lane, row = lanes(rows), sublanes(rows)
    step = 2 * ((row + parity) % 2) - 1
    within = (lane % period + step + period) % period
    return lane - lane % period + within


def call(kernel, out, args, specs=None, scratch=(), limit=40):
    vmem = pl.BlockSpec(memory_space=pltpu.VMEM)
    return pl.pallas_call(
        kernel,
        out_shape=out[0],
        in_specs=specs or [vmem] * len(args),
        out_specs=out[1] if len(out) > 1 else jax.tree.map(lambda _: vmem, out[0]),
        scratch_shapes=scratch,
        compiler_params=pltpu.CompilerParams(vmem_limit_bytes=limit * MIB),
        name=kernel.__name__,
    )(*args)


def arr(*shape):
    return jax.ShapeDtypeStruct(shape, F32)


def split_fine(f_ref, b_ref, wf_ref, wb_ref, lo_ref, hi_ref):
    lane, row = lanes(32), sublanes(32)
    index = []
    for parity in range(2):
        odd = (row + parity) % 2
        index.append(2 * (lane % 64) + jnp.where(lane < 64, odd, 1 - odd))
    for i in range(16):
        wf = pick(f_ref[i], index[i % 2])
        wb = pick(b_ref[i], index[i % 2])
        wf_ref[i] = wf
        wb_ref[i] = wb
        if i < 8:
            lo_ref[i] = wf
        else:
            hi_ref[i - 8] = wf
        if i < 9:
            lo_ref[8 + i] = wb
        if i > 6:
            hi_ref[1 + i] = wb


def plane_f(wf, xl, xu, p):
    return xl.at[p] if p < 8 else wf.at[p - 8] if p < 24 else xu.at[p - 24]


def plane_b(wb, xl, xu, p):
    return xl.at[9 + p] if p < 8 else wb.at[p - 8] if p < 24 else xu.at[8 + p - 24]


def pack_rows(wf, wb, xl, xu, lo_ref, hi_ref):
    for p in range(32):
        f, b = plane_f(wf, xl, xu, p), plane_b(wb, xl, xu, p)
        lo_ref[p] = f[0:8]
        hi_ref[p] = f[24:32]
        lo_ref[32 + p] = b[0:8]
        hi_ref[32 + p] = b[24:32]
    for i in range(16):
        lo_ref[64 + i // 8, i % 8 : i % 8 + 1] = wb[i, 8:9]
        hi_ref[64 + i // 8, i % 8 : i % 8 + 1] = wb[i, 23:24]


def slab(plane, yl, yu, which, p):
    return jnp.concatenate([yl[32 * which + p], plane[...], yu[32 * which + p]], axis=0)


def pack_lanes(wf, wb, xl, xu, yl, yu, lo_ref, hi_ref):
    slot_of = lanes(48) % 64
    for which, width, base in ((0, 4, 0), (1, 8, 12)):
        count = 64 // width
        slot = slot_of // width
        for group in range(32 // count):
            for s in range(count):
                p = group * count + s
                plane = plane_b(wb, xl, xu, p) if which else plane_f(wf, xl, xu, p)
                v = turn(slab(plane, yl, yu, which, p), width * s)
                if s == 0:
                    low = high = v
                else:
                    low = jnp.where(slot == s, v, low)
                    high = jnp.where(slot == s - 1, v, high)
            start = base + 6 * group
            lo_ref[start : start + 6] = low.reshape(6, 8, 128)
            hi_ref[start : start + 6] = high.reshape(6, 8, 128)


def make_coefs(mine, other, f, coef, p, index, scale, rows, inside=None):
    r = slice(8, 8 + rows)
    centre = mine[p + 1, r]
    mid = other[p + 1, r]
    side = pick(mid, index)
    if inside is not None:
        side = jnp.where(inside, side, 0.0)
    beside = (other[p, r], other[p + 2, r], other[p + 1, 7 : 7 + rows], other[p + 1, 9 : 9 + rows], mid, side)
    weights = [centre + b for b in beside]
    total = weights[0]
    for w in weights[1:]:
        total = total + w
    inverse = jnp.where(centre > 0.0, 1.0 / jnp.where(centre > 0.0, total, 1.0), 0.0)
    for which in range(6):
        w = weights[which] * inverse
        if which == 5 and inside is not None:
            w = jnp.where(inside, w, 0.0)
        coef[which, p] = w
    coef[6, p] = f * (inverse * (2.0 / scale))
    coef[7, p] = total * (0.5 * scale)


def relaxed(other, coef, p, index, rows, first=0, shift=0):
    a = 8 + first
    r = slice(a, a + rows)
    c = slice(first, first + rows)
    q = p - shift
    mid = other[p + 1, r]
    out = coef[6, q, c] + coef[0, q, c] * other[p, r]
    out = out + coef[1, q, c] * other[p + 2, r]
    out = out + coef[2, q, c] * other[p + 1, a - 1 : a - 1 + rows]
    out = out + coef[3, q, c] * other[p + 1, a + 1 : a + 1 + rows]
    out = out + coef[4, q, c] * mid
    return out + coef[5, q, c] * pick(mid, index)


def pairs(start, stop, body):
    def step(t, carry):
        for parity in range(2):
            body(2 * t + parity, parity)
        return carry

    lax.fori_loop(start // 2, stop // 2, step, 0)


def update(mine, other, coef, index, start, stop, rows, flip, shift=0):
    def body(p, parity):
        mine[p + 1, 8 : 8 + rows] = relaxed(other, coef, p, index[(parity + flip) % 2], rows, 0, shift)

    pairs(start, stop, body)


def defect(red, black, cr, cb, p, parity, index, rows, first=0, shift=0):
    r = slice(8 + first, 8 + first + rows)
    c = slice(first, first + rows)
    er = cr[7, p - shift, c] * (relaxed(black, cr, p, index[parity], rows, first, shift) - red[p + 1, r])
    eb = cb[7, p - shift, c] * (relaxed(red, cb, p, index[1 - parity], rows, first, shift) - black[p + 1, r])
    return er, eb


def halve_rows(tmp, value, rows):
    tmp[0:rows] = value
    return 0.125 * (tmp[pl.ds(0, rows // 2, 2)] + tmp[pl.ds(1, rows // 2, 2)])


def double_rows(tmp, value, rows):
    tmp[pl.ds(0, rows, 2)] = value
    tmp[pl.ds(1, rows, 2)] = value


def fine_down(
    at, wf, wb, xl, xu, yl, yu, zl, zu, g_ref, cr_out, cb_out, vb_out, br, bb, fr, fb, cr, cb, vr, vb, tmp, sems
):
    gx, gy, gz = at[0], at[1], at[2]
    lane, row = lanes(48), sublanes(48)
    own = lane < 64
    keep = own | ((lane < 96) & (gz < 7)) | ((lane >= 96) & (gz > 0))
    keep = keep & ((row >= 8) | (gy > 0)) & ((row < 40) | (gy < 3))
    kept = jnp.where(keep, 1.0, 0.0).astype(F32)
    below = jnp.where(gx > 0, 1.0, 0.0).astype(F32)
    above = jnp.where(gx < 3, 1.0, 0.0).astype(F32)
    left = jnp.where(gy > 0, 1.0, 0.0).astype(F32)
    right = jnp.where(gy < 3, 1.0, 0.0).astype(F32)
    vr[...] = jnp.zeros_like(vr)
    vb[...] = jnp.zeros_like(vb)
    edge = jnp.zeros((8, 128), F32)
    for b in (br, bb):
        for q in range(34):
            b[q, 0:8] = edge
            b[q, 56:64] = edge
        for q in (0, 33):
            b[q, 8:56] = jnp.zeros((48, 128), F32)
    for which, width, base in ((0, 4, 0), (1, 8, 12)):
        count = 64 // width
        slot = (lane % 64) // width
        for p in range(32):
            plane = plane_b(wb, xl, xu, p) if which else plane_f(wf, xl, xu, p)
            w = slab(plane, yl, yu, which, p)
            s = p % count
            start = base + 6 * (p // count)
            up = zu[start : start + 6].reshape(48, 128)
            low = zl[start : start + 6].reshape(48, 128)
            both = jnp.where(slot == s, up, low)
            red = jnp.where(own, w, turn(both, 64 - width * s))
            black = jnp.where(own, turn(w, 64), turn(both, -width * s))
            if which:
                k = kept * below if p < 8 else kept * above if p >= 24 else kept
                br[p + 1, 8:56] = red * k
                bb[p + 1, 8:56] = black * k
            else:
                fr[p] = red
                fb[p] = black
    for a in range(2):
        for src, r, ok in ((yl, 7, left), (yu, 56, right)):
            v = src[64 + a] * ok
            t = turn(v, 64)
            for s in range(8):
                br[9 + 8 * a + s, r : r + 1] = v[s : s + 1]
                bb[9 + 8 * a + s, r : r + 1] = t[s : s + 1]
    for v, q in ((xl[8] * below, 0), (xu[16] * above, 33)):
        br[q, 16:48] = v
        bb[q, 16:48] = turn(v, 64)

    index = [side_index(48, parity, 128) for parity in range(2)]

    def coefs(p, parity):
        make_coefs(br, bb, fr[p], cr, p, index[parity], 1.0, 48)
        make_coefs(bb, br, fb[p], cb, p, index[1 - parity], 1.0, 48)
        vr[p + 1, 8:56] = cr[6, p]

    pairs(0, 32, coefs)
    copies = [
        pltpu.make_async_copy(cr.at[:, pl.ds(4, 24)], cr_out, sems.at[0]),
        pltpu.make_async_copy(cb.at[:, pl.ds(4, 24)], cb_out, sems.at[1]),
        pltpu.make_async_copy(vb, vb_out, sems.at[2]),
    ]
    copies[0].start()
    copies[1].start()
    update(vb, vr, cb, index, 0, 32, 48, 1)
    update(vr, vb, cr, index, 2, 30, 48, 0)
    update(vb, vr, cb, index, 2, 30, 48, 1)
    copies[2].start()

    lane, row = lanes(16), sublanes(16)
    inner = [side_index(32, parity, 128) for parity in range(2)]
    swap = jnp.where(gx >= 2, 64, 0)
    for n in range(8):
        total = coarse = None
        for parity in range(2):
            p = 8 + 2 * n + parity
            er, eb = defect(vr, vb, cr, cb, p, parity, inner, 32, 8)
            e = er + eb
            b = br[p + 1, 16:48] + bb[p + 1, 16:48]
            total = e if total is None else total + e
            coarse = b if coarse is None else coarse + b
        f1 = halve_rows(tmp, total, 32)
        b1 = halve_rows(tmp, coarse, 32)
        odd = (row + n) % 2
        idx = 64 * (lane // 64) + 2 * (lane % 32) + jnp.where(lane % 64 < 32, odd, 1 - odd)
        w1 = pick(jnp.where(lane < 64, f1, turn(b1, 64)), idx ^ swap)
        for copy in range(16):
            g_ref[copy, n] = w1
    for c in copies:
        c.wait()


def joined(g, p):
    a, i = p // 8, p % 8
    wa = jnp.concatenate([g[4 * a + y, i] for y in range(4)], axis=0)
    wb = jnp.concatenate([g[4 * (a + 2) + y, i] for y in range(4)], axis=0)
    half = lanes(64) < 64
    return jnp.where(half, wa, wb), jnp.where(half, wb, wa)


def pack_mid(g, lo_ref, hi_ref):
    slot = (lanes(64) % 32) // 8
    for group in range(4):
        low, high = [None] * 2, [None] * 2
        for s in range(4):
            for which, v in enumerate(joined(g, 4 * group + s)):
                v = turn(v, 8 * s)
                low[which] = v if s == 0 else jnp.where(slot == s, v, low[which])
                high[which] = v if s == 0 else jnp.where(slot == s - 1, v, high[which])
        for which in range(2):
            lo_ref[which, group] = low[which]
            hi_ref[which, group] = high[which]


def seam(v, rows):
    r = slice(8, 8 + rows)
    half = lanes(rows) < 64
    v[0, r] = jnp.where(half, 0.0, turn(v[16, r], 64))
    v[17, r] = jnp.where(half, turn(v[1, r], 64), 0.0)


def mid_down(at, g, zl, zu, w2_ref, cr_out, cb_out, vb_out, br, bb, fr, fb, cr, cb, vr, vb, tmp, sems):
    gy, gz = at[1], at[2]
    lane = lanes(64)
    own = lane % 64 < 32
    keep = own | ((lane % 64 < 48) & (gz < 7)) | ((lane % 64 >= 48) & (gz > 0))
    kept = jnp.where(keep, 1.0, 0.0).astype(F32)
    slot = (lane % 32) // 8
    for v in (vr, vb):
        v[...] = jnp.zeros_like(v)
    for b in (br, bb):
        b[:, 0:8] = jnp.zeros((18, 8, 128), F32)
        b[:, 72:80] = jnp.zeros((18, 8, 128), F32)
    for p in range(16):
        mf, mb = joined(g, p)
        s, group = p % 4, p // 4
        both = jnp.where(slot == s, zu[0, group], zl[0, group])
        fr[p] = jnp.where(own, mf, turn(both, 32 - 8 * s))
        fb[p] = jnp.where(own, turn(mf, 96), turn(both, -8 * s))
        both = jnp.where(slot == s, zu[1, group], zl[1, group])
        br[p + 1, 8:72] = kept * jnp.where(own, turn(mb, 64), turn(both, 96 - 8 * s))
        bb[p + 1, 8:72] = kept * jnp.where(own, turn(mb, 32), turn(both, 64 - 8 * s))
    seam(br, 64)
    seam(bb, 64)
    index = [side_index(64, parity, 64) for parity in range(2)]

    def coefs(p, parity):
        make_coefs(br, bb, fr[p], cr, p, index[parity], 0.25, 64)
        make_coefs(bb, br, fb[p], cb, p, index[1 - parity], 0.25, 64)
        vr[p + 1, 8:72] = cr[6, p]

    pairs(0, 16, coefs)
    seam(vr, 64)
    window = pl.multiple_of(jnp.clip(gy * 16 - 8, 0, 32), 8)
    copies = [
        pltpu.make_async_copy(cr.at[:, :, pl.ds(window, 32)], cr_out, sems.at[0]),
        pltpu.make_async_copy(cb.at[:, :, pl.ds(window, 32)], cb_out, sems.at[1]),
        pltpu.make_async_copy(vb.at[:, pl.ds(window + 8, 32)], vb_out, sems.at[2]),
    ]
    copies[0].start()
    copies[1].start()
    update(vb, vr, cb, index, 0, 16, 64, 1)
    seam(vb, 64)
    update(vr, vb, cr, index, 0, 16, 64, 0)
    seam(vr, 64)
    update(vb, vr, cb, index, 0, 16, 64, 1)
    seam(vb, 64)
    copies[2].start()
    lane, row = lanes(32), sublanes(32)
    for n in range(8):
        total = coarse = None
        for parity in range(2):
            p = 2 * n + parity
            er, eb = defect(vr, vb, cr, cb, p, parity, index, 64)
            e = er + eb
            b = br[p + 1, 8:72] + bb[p + 1, 8:72]
            total = e if total is None else total + e
            coarse = b if coarse is None else coarse + b
        f2 = halve_rows(tmp, total, 64)
        b2 = halve_rows(tmp, coarse, 64)
        odd = (row + n) % 2
        idx = 64 * ((lane % 64) // 32) + 2 * (lane % 16) + jnp.where(lane % 32 < 16, odd, 1 - odd)
        w2 = jnp.where(lane < 64, pick(f2, idx), pick(b2, idx))
        for copy in range(4):
            w2_ref[copy, n] = w2
    for c in copies:
        c.wait()


def transposed(blocks):
    slot = lanes(32) // 16
    for bit in (1, 2, 4):
        out = list(blocks)
        for i in range(8):
            if not i & bit:
                x, y = blocks[i], blocks[i + bit]
                out[i] = jnp.where(slot & bit == 0, x, turn(y, 16 * bit))
                out[i + bit] = jnp.where(slot & bit == 0, turn(x, -16 * bit), y)
        blocks = out
    return blocks


def level_scratch(planes, rows):
    return [pltpu.VMEM((planes + 2, rows + 16, 128), F32)] * 4 + [pltpu.VMEM((8, planes, rows, 128), F32)] * 2


def clear(refs):
    for v in refs:
        v[...] = jnp.zeros_like(v)


def smooth_down(br, bb, vr, vb, cr, cb, f_of, index, scale, planes, rows, inside):
    def coefs(p, parity):
        fr, fb = f_of(p)
        make_coefs(br, bb, fr, cr, p, index[parity], scale, rows, inside and inside[parity])
        make_coefs(bb, br, fb, cb, p, index[1 - parity], scale, rows, inside and inside[1 - parity])
        vr[p + 1, 8 : 8 + rows] = cr[6, p]

    pairs(0, planes, coefs)
    update(vb, vr, cb, index, 0, planes, rows, 1)
    update(vr, vb, cr, index, 0, planes, rows, 0)
    update(vb, vr, cb, index, 0, planes, rows, 1)


def smooth_up(vr, vb, cr, cb, index, planes, rows):
    for _ in range(2):
        update(vr, vb, cr, index, 0, planes, rows, 0)
        update(vb, vr, cb, index, 0, planes, rows, 1)


def restrict(level, tmp, index, planes, rows, cells, put):
    br, bb, vr, vb, cr, cb = level
    lane, row = lanes(rows // 2), sublanes(rows // 2)
    for n in range(planes // 2):
        total = coarse = None
        for parity in range(2):
            p = 2 * n + parity
            er, eb = defect(vr, vb, cr, cb, p, parity, index, rows)
            b = br[p + 1, 8 : 8 + rows] + bb[p + 1, 8 : 8 + rows]
            total = er + eb if total is None else total + (er + eb)
            coarse = b if coarse is None else coarse + b
        f = halve_rows(tmp, total, rows)
        b = halve_rows(tmp, coarse, rows)
        odd = (row + n) % 2
        red = 2 * (lane % 64) + odd
        black = 2 * (lane % 64) + 1 - odd
        inside = lane < cells
        put(n, *[jnp.where(inside, pick(x, i), 0.0) for x in (f, b) for i in (red, black)])


def prolong(vr, vb, out, tmp, planes, rows):
    lane, row = lanes(rows), sublanes(rows)
    r = slice(8, 8 + rows)
    for n in range(planes):
        even = (row + lane + n) % 2 == 0
        c = jnp.where(even, pick(vr[n + 1, r], lane // 2), pick(vb[n + 1, r], lane // 2))
        double_rows(tmp, c, rows)
        for p in (2 * n, 2 * n + 1):
            out[p + 1, 8 : 8 + 2 * rows] += tmp[0 : 2 * rows]


def coarse_up(
    at, mine, pair, c1r_in, c1b_in, v1b_in, c0r_in, c0b_in, v0b_in, u_ref, res_ref,
    b2r, b2b, v2r, v2b, c2r, c2b, f2,
    b3r, b3b, v3r, v3b, c3r, c3b, f3,
    b4r, b4b, v4r, v4b, c4r, c4b, f4,
    v1r, v1b, c1r, c1b, v0r, v0b, c0r, c0b, tmp, sems,
):
    gx, gy, gz = at[0], at[1], at[2]
    copies = [
        pltpu.make_async_copy(c1r_in, c1r, sems.at[0]),
        pltpu.make_async_copy(c1b_in, c1b, sems.at[1]),
        pltpu.make_async_copy(v1b_in, v1b.at[:, pl.ds(8, 32)], sems.at[2]),
        pltpu.make_async_copy(c0r_in, c0r, sems.at[3]),
        pltpu.make_async_copy(c0b_in, c0b, sems.at[4]),
        pltpu.make_async_copy(v0b_in, v0b, sems.at[5]),
    ]
    for c in copies:
        c.start()
    clear((b2r, b2b, v2r, v2b, b3r, b3b, v3r, v3b, b4r, b4b, v4r, v4b, v1r, v0r))
    v1b[:, 0:8] = jnp.zeros((18, 8, 128), F32)
    v1b[:, 40:48] = jnp.zeros((18, 8, 128), F32)

    first = gz % 2 == 0
    for n in range(8):
        blocks = []
        for chip in range(4):
            a, b = mine[chip, n], pair[chip, n]
            blocks += [jnp.where(first, a, b), jnp.where(first, b, a)]
        out = transposed(blocks)
        for h in range(2):
            p = n + 8 * h
            f2[0, p] = out[2 * h]
            f2[1, p] = out[2 * h + 1]
            b2r[p + 1, 8:40] = out[4 + 2 * h]
            b2b[p + 1, 8:40] = out[5 + 2 * h]
    lane = lanes(32)
    index2 = [side_index(32, parity, 128) for parity in range(2)]
    inside2 = [jnp.abs(index2[parity] - lane) < 64 for parity in range(2)]
    smooth_down(b2r, b2b, v2r, v2b, c2r, c2b, lambda p: (f2[0, p], f2[1, p]), index2, 0.25**2, 16, 32, inside2)

    def put3(n, fr, fb, br, bb):
        f3[0, n], f3[1, n] = fr, fb
        b3r[n + 1, 8:24], b3b[n + 1, 8:24] = br, bb

    restrict((b2r, b2b, v2r, v2b, c2r, c2b), tmp, index2, 16, 32, 64, put3)

    index3 = [side_index(16, parity, 128) for parity in range(2)]
    smooth_down(b3r, b3b, v3r, v3b, c3r, c3b, lambda p: (f3[0, p], f3[1, p]), index3, 0.25**3, 8, 16, None)

    def put4(n, fr, fb, br, bb):
        f4[0, n], f4[1, n] = fr, fb
        b4r[n + 1, 8:16], b4b[n + 1, 8:16] = br, bb

    restrict((b3r, b3b, v3r, v3b, c3r, c3b), tmp, index3, 8, 16, 32, put4)

    index4 = [side_index(8, parity, 128) for parity in range(2)]

    for p in range(4):
        make_coefs(b4r, b4b, f4[0, p], c4r, p, index4[p % 2], 0.25**4, 8)
        make_coefs(b4b, b4r, f4[1, p], c4b, p, index4[1 - p % 2], 0.25**4, 8)
    row8 = sublanes(8)
    inner = (row8 > 0, row8 < 7)
    cr4 = [[c4r[w, p] for w in range(7)] for p in range(4)]
    cb4 = [[c4b[w, p] for w in range(7)] for p in range(4)]
    for c in cr4 + cb4:
        c[2] = jnp.where(inner[0], c[2], 0.0)
        c[3] = jnp.where(inner[1], c[3], 0.0)

    def half(other, coefs, flip):
        out = []
        for p in range(4):
            c, v = coefs[p], other[p]
            w = c[6] + c[4] * v
            if p > 0:
                w = w + c[0] * other[p - 1]
            if p < 3:
                w = w + c[1] * other[p + 1]
            w = w + c[2] * pltpu.roll(v, 1, 0) + c[3] * pltpu.roll(v, 7, 0)
            out.append(w + c[5] * pick(v, index4[(p + flip) % 2]))
        return out

    def coarse_step(count, state):
        black = list(state)
        red = half(black, cr4, 0)
        return tuple(half(red, cb4, 1))

    black = lax.fori_loop(0, COARSE_ITERS - 1, coarse_step, (jnp.zeros((8, 128), F32),) * 4)
    red = half(black, cr4, 0)
    black = half(red, cb4, 1)
    for p in range(4):
        v4r[p + 1, 8:16] = red[p]
        v4b[p + 1, 8:16] = black[p]

    prolong(v4r, v4b, v3b, tmp, 4, 8)
    smooth_up(v3r, v3b, c3r, c3b, index3, 8, 16)
    prolong(v3r, v3b, v2b, tmp, 8, 16)
    smooth_up(v2r, v2b, c2r, c2b, index2, 16, 32)

    for c in copies[:3]:
        c.wait()
    lane, row = lanes(32), sublanes(32)
    near = lane % 64 - jnp.where(lane % 64 < 48, 0, 64)
    cell = gz * 32 + near
    valid = (cell >= 0) & (cell < 256)
    idx = jnp.clip(cell, 0, 255) // 2
    window = pl.multiple_of(jnp.clip(gy * 16 - 8, 0, 32), 8)
    for n in range(8):
        even = (row + lane + n) % 2 == 0
        parts = []
        for p in (n, n + 8):
            parts.append(jnp.where(even, pick(v2r[p + 1, 8:40], idx), pick(v2b[p + 1, 8:40], idx)))
        c = jnp.where(valid, jnp.where(lane < 64, parts[0], parts[1]), 0.0)
        double_rows(tmp, c, 32)
        for p in (2 * n, 2 * n + 1):
            v1b[p + 1, 8:40] += tmp[pl.ds(window, 32)]
    seam(v1b, 32)
    index1 = [side_index(32, parity, 64) for parity in range(2)]
    for _ in range(2):
        update(v1r, v1b, c1r, index1, 0, 16, 32, 0)
        seam(v1r, 32)
        update(v1b, v1r, c1b, index1, 0, 16, 32, 1)
        seam(v1b, 32)

    for c in copies[3:]:
        c.wait()
    start = pl.multiple_of(gy * 16 - window, 8)
    cell = lane - jnp.where(lane < 96, 0, 128)
    idx = (cell // 2) % 64
    for n in range(-3, 11):
        plane = gx * 8 + n
        held = jnp.clip(plane, 0, 31)
        at_half = idx + 64 * (held // 16)
        even = (row + lane + n) % 2 == 0
        red = v1r[held % 16 + 1, pl.ds(start, 32)]
        black = v1b[held % 16 + 1, pl.ds(start, 32)]
        c = jnp.where(even, pick(red, at_half), pick(black, at_half))
        c = c * jnp.where((plane >= 0) & (plane < 32), 1.0, 0.0).astype(F32)
        tmp[64:96] = c
        double_rows(tmp, tmp[68:92], 24)
        for p in (2 * n + 8, 2 * n + 9):
            v0b[p + 1, 8:56] += tmp[0:48]
    index0 = [side_index(48, parity, 128) for parity in range(2)]
    update(v0r, v0b, c0r, index0, 4, 28, 48, 0, 4)
    update(v0b, v0r, c0b, index0, 4, 28, 48, 1, 4)
    update(v0r, v0b, c0r, index0, 6, 26, 48, 0, 4)
    update(v0b, v0r, c0b, index0, 6, 26, 48, 1, 4)

    def finish(p, parity):
        even = (row + lane + parity) % 2 == 0
        er, eb = defect(v0r, v0b, c0r, c0b, p, parity, index1_0, 32, 8, 4)
        res_ref[p - 8] = jnp.where(even, pick(er, lane // 2), pick(eb, lane // 2))
        red, black = v0r[p + 1, 16:48], v0b[p + 1, 16:48]
        u_ref[p - 8] = jnp.where(even, pick(red, lane // 2), pick(black, lane // 2))

    index1_0 = [side_index(32, parity, 128) for parity in range(2)]
    pairs(8, 24, finish)


def around(lo, hi, axis):
    count = lax.axis_size(axis)
    from_above = lax.ppermute(lo, axis, [((i + 1) % count, i) for i in range(count)])
    from_below = lax.ppermute(hi, axis, [(i, (i + 1) % count) for i in range(count)])
    return from_below, from_above


def body(source, conductance):
    vmem, smem, anywhere = (pl.BlockSpec(memory_space=m) for m in (pltpu.VMEM, pltpu.SMEM, pl.ANY))
    at = jnp.stack([lax.axis_index(a) for a in ("gx", "gy", "gz")]).astype(jnp.int32)
    dma = pltpu.SemaphoreType.DMA

    block, x_slab = arr(16, 32, 128), arr(17, 32, 128)
    wf, wb, lo, hi = call(split_fine, [(block, block, x_slab, x_slab)], (source, conductance))
    xl, xu = around(lo, hi, "gx")
    lo, hi = call(pack_rows, [(arr(66, 8, 128),) * 2], (wf, wb, xl, xu))
    yl, yu = around(lo, hi, "gy")
    lo, hi = call(pack_lanes, [(arr(36, 8, 128),) * 2], (wf, wb, xl, xu, yl, yu))
    zl, zu = around(lo, hi, "gz")

    state0 = (arr(8, 24, 48, 128), arr(8, 24, 48, 128), arr(34, 64, 128))
    colour0 = pltpu.VMEM((34, 64, 128), F32)
    right0 = pltpu.VMEM((32, 48, 128), F32)
    coef0 = pltpu.VMEM((8, 32, 48, 128), F32)
    g, c0r, c0b, v0b = call(
        fine_down,
        [(arr(16, 8, 16, 128),) + state0, (vmem, anywhere, anywhere, anywhere)],
        (at, wf, wb, xl, xu, yl, yu, zl, zu),
        [smem] + [vmem] * 8,
        [colour0, colour0, right0, right0, coef0, coef0, colour0, colour0, pltpu.VMEM((32, 128), F32), dma((3,))],
    )
    g = lax.all_to_all(g, ("gx", "gy"), 0, 0, tiled=True)
    lo, hi = call(pack_mid, [(arr(2, 4, 64, 128),) * 2], (g,))
    zl, zu = around(lo, hi, "gz")

    state1 = (arr(8, 16, 32, 128), arr(8, 16, 32, 128), arr(18, 32, 128))
    colour1 = pltpu.VMEM((18, 80, 128), F32)
    right1 = pltpu.VMEM((16, 64, 128), F32)
    coef1 = pltpu.VMEM((8, 16, 64, 128), F32)
    w2, c1r, c1b, v1b = call(
        mid_down,
        [(arr(4, 8, 32, 128),) + state1, (vmem, anywhere, anywhere, anywhere)],
        (at, g, zl, zu),
        [smem] + [vmem] * 3,
        [colour1, colour1, right1, right1, coef1, coef1, colour1, colour1, pltpu.VMEM((64, 128), F32), dma((3,))],
    )
    mine = lax.all_to_all(w2, "gz", 0, 0, axis_index_groups=[[0, 2, 4, 6], [1, 3, 5, 7]], tiled=True)
    pair = lax.ppermute(mine, "gz", [(i, i ^ 1) for i in range(8)])

    scratch = []
    for planes, rows in ((16, 32), (8, 16), (4, 8)):
        scratch += level_scratch(planes, rows) + [pltpu.VMEM((2, planes, rows, 128), F32)]
    scratch += [pltpu.VMEM((18, 48, 128), F32)] * 2 + [pltpu.VMEM((8, 16, 32, 128), F32)] * 2
    scratch += [colour0] * 2 + [pltpu.VMEM((8, 24, 48, 128), F32)] * 2
    scratch += [pltpu.VMEM((96, 128), F32), dma((6,))]
    return call(
        coarse_up,
        [(block, block)],
        (at, mine, pair, c1r, c1b, v1b, c0r, c0b, v0b),
        [smem, vmem, vmem] + [anywhere] * 6,
        scratch,
    )


def solution(mesh):
    placed = (P("gx", "gy", "gz"), P("gx", "gy", "gz"))
    return jax.shard_map(body, mesh=mesh, in_specs=placed, out_specs=placed, check_vma=False)
```

time: 1070 us -> 125 us (0.12); the launches traced: 1060 us -> 125 us
  starting transfers between devices: 592 us -> 13.4 us
  waiting for transfers between devices: 313 us -> 23.6 us
  local copies, waits for them, and re-layouts: 58.4 us -> 4.01 us
  Pallas kernels: 0 us -> 46.5 us
  other arithmetic: 38.5 us -> 0.08 us
  blocking collectives: 49.7 us -> 36.7 us
    ppermute x246 -> x9, starting transfers between devices: 592 us -> 13.4 us  [the longest x4 9.3 us: around(): lax.ppermute(hi, axis, [(i, (i + 1) % count) for i in range(count)])]
    ppermute x246 -> x9, waiting for transfers between devices: 313 us -> 23.6 us  [the longest x4 16.9 us: around(): lax.ppermute(hi, axis, [(i, (i + 1) % count) for i in range(count)])]
    all_gather x6 -> x0, blocking collectives: 49.7 us -> none  [the longest x1 13 us: gather_whole(): lax.all_gather(local_b, 'gz', axis=2, tiled=True)]
    pallas_call x0 -> x7, Pallas kernels: none -> 46.5 us  [call(): pl.pallas_call(kernel, out_shape=out[0], in_specs=specs or [vmem] * len(a...]
    reshape x10 -> x0, local copies, waits for them, and re-layouts: 42.5 us -> none  [the longest x4 40.6 us: coarsen(): field.reshape(sx // 2, 2, sy // 2, 2, sz // 2, 2)]
    all_to_all x0 -> x2, blocking collectives: none -> 36.7 us  [the longest x1 22.6 us: body(): g = lax.all_to_all(g, ('gx', 'gy'), 0, 0, tiled=True)]
    reduce_sum x10 -> x0, other arithmetic: 18.2 us -> none  [coarsen(): jnp.sum(field.reshape(sx // 2, 2, sy // 2, 2, sz // 2, 2), axis=(1, 3, 5))]
    select_n x72 -> x0, other arithmetic: 12.5 us -> none  [the longest x32 8.97 us: local_sweep(): jnp.where(chosen, field + (setup['source'] - applied) / setup['diag_int']...]
  transfers between devices with their start and end apart: 246 -> 9, of which waited for: 104 -> 7; matrix products, arithmetic and copies ran while one was open for 8% -> 0% of each run, Pallas kernels for 0% -> 0%
where the time goes in v1:
time: 125 us
  Pallas kernels  46.5 us (37%)
  blocking collectives  36.7 us (29%)
  waiting for transfers between devices  23.6 us (19%)
  starting transfers between devices  13.4 us (11%)
  local copies, waits for them, and re-layouts  4.01 us (3%)
    pallas_call x7, Pallas kernels, call(): pl.pallas_call(kernel, out_shape=out[0], in_specs=specs or [vmem] * len(a...  46.5 us
    all_to_all x1, blocking collectives, body(): g = lax.all_to_all(g, ('gx', 'gy'), 0, 0, tiled=True)  22.6 us
    ppermute x4, waiting for transfers between devices, around(): lax.ppermute(hi, axis, [(i, (i + 1) % count) for i in range(count)])  16.9 us
    all_to_all x1, blocking collectives, body(): lax.all_to_all(w2, 'gz', 0, 0, axis_index_groups=[[0, 2, 4, 6], [1, 3, 5,...  14 us
    ppermute x4, starting transfers between devices, around(): lax.ppermute(hi, axis, [(i, (i + 1) % count) for i in range(count)])  9.3 us
    ppermute x4, waiting for transfers between devices, around(): lax.ppermute(lo, axis, [((i + 1) % count, i) for i in range(count)])  5.14 us
    unnamed x6, local copies, waits for them, and re-layouts  4.01 us
    ppermute x4, starting transfers between devices, around(): lax.ppermute(lo, axis, [((i + 1) % count, i) for i in range(count)])  3.73 us
  transfers between devices with their start and end apart: 9, of which 7 were waited for; matrix products, arithmetic and copies ran while one was open for 0% of the time, Pallas kernels for 0%

profile of v1, /device:TPU:1, one launch (start us, length us, event | category | flops | bytes accessed | tf_op | source)
XLA Modules:
  0.0 125.1 jit_solution(2628541221914088726)
XLA Ops:
  0.6 0.9 copy-done.1
  1.6 0.9 copy-done.2
  2.5 0.4 split_fine.1
  2.9 2.5 %collective-permute-start = (f32[17,32,128]{2,1,0:T(8,128)S(1)}, f32[17,32,128]{2,1,0:T(8,128)S(1)}, u32[]{:S(2)}, u32[]{:S(2)}) collective-permute-start(f32[17,32,128]{2,1,0:T(8,128)S(1)} %get-tuple-element.22), channel_id=1, source_target_pairs={{0,32},{32,64},{64,96},{96,0},{1,33},{33,65},{65,97},{97,1},{2,34}... | collective-permute-start | bytes 835592 | tf_op jit(solution)/shard_map/ppermute | solution.py:617
  5.5 2.2 %collective-permute-start.1 = (f32[17,32,128]{2,1,0:T(8,128)S(1)}, f32[17,32,128]{2,1,0:T(8,128)S(1)}, u32[]{:S(2)}, u32[]{:S(2)}) collective-permute-start(f32[17,32,128]{2,1,0:T(8,128)S(1)} %get-tuple-element.23), channel_id=1, source_target_pairs={{32,0},{64,32},{96,64},{0,96},{33,1},{65,33},{97,65},{1,97},{34,2}... | collective-permute-start | bytes 835592 | tf_op jit(solution)/shard_map/ppermute | solution.py:616
  7.7 6.3 %collective-permute-done.xl = f32[17,32,128]{2,1,0:T(8,128)S(1)} collective-permute-done((f32[17,32,128]{2,1,0:T(8,128)S(1)}, f32[17,32,128]{2,1,0:T(8,128)S(1)}, u32[]{:S(2)}, u32[]{:S(2)}) %collective-permute-start) | collective-permute-done | bytes 278560 | tf_op jit(solution)/shard_map/ppermute | solution.py:617
  14.0 1.4 %collective-permute-start.2 = (f32[66,8,128]{2,1,0:T(8,128)S(1)}, f32[66,8,128]{2,1,0:T(8,128)S(1)}, u32[]{:S(2)}, u32[]{:S(2)}) collective-permute-start(f32[66,8,128]{2,1,0:T(8,128)S(1)} %get-tuple-element.24), channel_id=1, source_target_pairs={{0,8},{8,16},{16,24},{24,0},{1,9},{9,17},{17,25},{25,1},{2,10},{10... | collective-permute-start | bytes 811016 | tf_op jit(solution)/shard_map/ppermute | solution.py:617
  15.4 1.5 %collective-permute-start.3 = (f32[66,8,128]{2,1,0:T(8,128)S(1)}, f32[66,8,128]{2,1,0:T(8,128)S(1)}, u32[]{:S(2)}, u32[]{:S(2)}) collective-permute-start(f32[66,8,128]{2,1,0:T(8,128)S(1)} %get-tuple-element.25), channel_id=1, source_target_pairs={{8,0},{16,8},{24,16},{0,24},{9,1},{17,9},{25,17},{1,25},{10,2},{18... | collective-permute-start | bytes 811016 | tf_op jit(solution)/shard_map/ppermute | solution.py:616
  16.9 5.3 %collective-permute-done.2.yl = f32[66,8,128]{2,1,0:T(8,128)S(1)} collective-permute-done((f32[66,8,128]{2,1,0:T(8,128)S(1)}, f32[66,8,128]{2,1,0:T(8,128)S(1)}, u32[]{:S(2)}, u32[]{:S(2)}) %collective-permute-start.2) | collective-permute-done | bytes 270368 | tf_op jit(solution)/shard_map/ppermute | solution.py:617
  22.2 0.4 pack_lanes.1
  22.6 3.2 %collective-permute-start.4 = (f32[36,8,128]{2,1,0:T(8,128)S(1)}, f32[36,8,128]{2,1,0:T(8,128)S(1)}, u32[]{:S(2)}, u32[]{:S(2)}) collective-permute-start(f32[36,8,128]{2,1,0:T(8,128)S(1)} %get-tuple-element.26), channel_id=1, source_target_pairs={{0,1},{1,2},{2,3},{3,4},{4,5},{5,6},{6,7},{7,0},{8,9},{9,10},{10,1... | collective-permute-start | bytes 442376 | tf_op jit(solution)/shard_map/ppermute | solution.py:617
  25.9 2.0 %collective-permute-done.4.zl = f32[36,8,128]{2,1,0:T(8,128)S(1)} collective-permute-done((f32[36,8,128]{2,1,0:T(8,128)S(1)}, f32[36,8,128]{2,1,0:T(8,128)S(1)}, u32[]{:S(2)}, u32[]{:S(2)}) %collective-permute-start.4) | collective-permute-done | bytes 147488 | tf_op jit(solution)/shard_map/ppermute | solution.py:617
  27.9 2.5 %collective-permute-done.5.zu = f32[36,8,128]{2,1,0:T(8,128)S(1)} collective-permute-done((f32[36,8,128]{2,1,0:T(8,128)S(1)}, f32[36,8,128]{2,1,0:T(8,128)S(1)}, u32[]{:S(2)}, u32[]{:S(2)}) %collective-permute-start.5) | collective-permute-done | bytes 147488 | tf_op jit(solution)/shard_map/ppermute | solution.py:616
  30.4 10.3 %fine_down.1 = (f32[16,8,16,128]{3,2,1,0:T(8,128)S(1)}, f32[8,24,48,128]{3,2,1,0:T(8,128)S(1)}, f32[8,24,48,128]{3,2,1,0:T(8,128)S(1)}, f32[34,64,128]{2,1,0:T(8,128)S(1)}) custom-call(s32[3]{0:T(128)S(1)} %pad_add_fusion.at, f32[16,32,128]{2,1,0:T(8,128)S(1)} %get-tuple-element.20.wf, f32[16,32,128]{2,1,0:T(8,128)S(1)} %get-tuple-element.21.wb, ...), custom_call_target="tpu_custom_call" | custom-call | tf_op jit(solution)/shard_map/fine_down/pallas_call | solution.py:41
  40.7 2.1 %copy-done = f32[8,24,48,128]{3,2,1,0:T(8,128)} copy-done((f32[8,24,48,128]{3,2,1,0:T(8,128)}, f32[8,24,48,128]{3,2,1,0:T(8,128)S(1)}, u32[]{:S(2)}) %copy-start) | copy-done | bytes 4718616
  42.8 22.6 %all_to_all.10.g = f32[16,8,16,128]{3,2,1,0:T(8,128)S(1)} all-to-all(f32[16,8,16,128]{3,2,1,0:T(8,128)S(1)} %get-tuple-element.28), channel_id=1, replica_groups=mesh['gx'=4,'gy'=4,'gz'=8] {'gx','gy'}, dimensions={0} | all-to-all | bytes 2097152 | tf_op jit(solution)/shard_map/all_to_all | solution.py:645
  65.7 2.2 %collective-permute-start.6 = (f32[2,4,64,128]{3,2,1,0:T(8,128)S(1)}, f32[2,4,64,128]{3,2,1,0:T(8,128)S(1)}, u32[]{:S(2)}, u32[]{:S(2)}) collective-permute-start(f32[2,4,64,128]{3,2,1,0:T(8,128)S(1)} %get-tuple-element.29), channel_id=1, source_target_pairs={{0,1},{1,2},{2,3},{3,4},{4,5},{5,6},{6,7},{7,0},{8,9},{9,10},{10,1... | collective-permute-start | bytes 786440 | tf_op jit(solution)/shard_map/ppermute | solution.py:617
  67.9 3.3 %collective-permute-done.6.zl = f32[2,4,64,128]{3,2,1,0:T(8,128)S(1)} collective-permute-done((f32[2,4,64,128]{3,2,1,0:T(8,128)S(1)}, f32[2,4,64,128]{3,2,1,0:T(8,128)S(1)}, u32[]{:S(2)}, u32[]{:S(2)}) %collective-permute-start.6) | collective-permute-done | bytes 262176 | tf_op jit(solution)/shard_map/ppermute | solution.py:617
  71.2 2.7 %collective-permute-done.7.zu = f32[2,4,64,128]{3,2,1,0:T(8,128)S(1)} collective-permute-done((f32[2,4,64,128]{3,2,1,0:T(8,128)S(1)}, f32[2,4,64,128]{3,2,1,0:T(8,128)S(1)}, u32[]{:S(2)}, u32[]{:S(2)}) %collective-permute-start.7) | collective-permute-done | bytes 262176 | tf_op jit(solution)/shard_map/ppermute | solution.py:616
  73.9 8.4 %mid_down.1 = (f32[4,8,32,128]{3,2,1,0:T(8,128)S(1)}, f32[8,16,32,128]{3,2,1,0:T(8,128)S(1)}, f32[8,16,32,128]{3,2,1,0:T(8,128)S(1)}, f32[18,32,128]{2,1,0:T(8,128)S(1)}) custom-call(s32[3]{0:T(128)S(1)} %pad_add_fusion.at, f32[16,8,16,128]{3,2,1,0:T(8,128)S(1)} %all_to_all.10.g, f32[2,4,64,128]{3,2,1,0:T(8,128)S(1)} %collective-permute-done.6.zl, ...), custom_call_target="tpu_custom_call" | custom-call | tf_op jit(solution)/shard_map/mid_down/pallas_call | solution.py:41
  82.3 14.0 %all_to_all.11.mine = f32[4,8,32,128]{3,2,1,0:T(8,128)S(1)} all-to-all(f32[4,8,32,128]{3,2,1,0:T(8,128)S(1)} %get-tuple-element.31), channel_id=1, replica_groups={{0,2,4,6},{1,3,5,7},{8,10,12,14},{9,11,13,15},{16,18,20,22},{17,19,21,2..., dimensions={0} | all-to-all | bytes 1048576 | tf_op jit(solution)/shard_map/all_to_all | solution.py:660
  96.3 0.4 collective-permute-start.8
  96.7 1.5 %collective-permute-done.8.pair = f32[4,8,32,128]{3,2,1,0:T(8,128)S(1)} collective-permute-done((f32[4,8,32,128]{3,2,1,0:T(8,128)S(1)}, f32[4,8,32,128]{3,2,1,0:T(8,128)S(1)}, u32[]{:S(2)}, u32[]{:S(2)}) %collective-permute-start.8) | collective-permute-done | bytes 524320 | tf_op jit(solution)/shard_map/ppermute | solution.py:661
  98.3 26.7 %coarse_up.1 = (f32[16,32,128]{2,1,0:T(8,128)}, f32[16,32,128]{2,1,0:T(8,128)}) custom-call(s32[3]{0:T(128)S(1)} %pad_add_fusion.at, f32[4,8,32,128]{3,2,1,0:T(8,128)S(1)} %all_to_all.11.mine, f32[4,8,32,128]{3,2,1,0:T(8,128)S(1)} %collective-permute-done.8.pair, f32[8,16,32,128]{3,2,1,0:T(8,128)S(1)} %get-tuple-element.32.c1r_in, ...), custom_call_target="tpu_custom_call" | custom-call | tf_op jit(solution)/shard_map/coarse_up/pallas_call | solution.py:41
  (10 shorter events, 0.4 us)
Async XLA Ops:
  0.6 1.0 copy-start.1
  1.6 0.9 copy-start.2
  2.9 11.0 %collective-permute-start = (f32[17,32,128]{2,1,0:T(8,128)S(1)}, f32[17,32,128]{2,1,0:T(8,128)S(1)}, u32[]{:S(2)}, u32[]{:S(2)}) collective-permute-start(f32[17,32,128]{2,1,0:T(8,128)S(1)} %get-tuple-element.22), channel_id=1, source_target_pairs={{0,32},{32,64},{64,96},{96,0},{1,33},{33,65},{65,97},{97,1},{2,34}... | collective-permute-start | bytes 835592 | tf_op jit(solution)/shard_map/ppermute | solution.py:617
  5.5 8.5 %collective-permute-start.1 = (f32[17,32,128]{2,1,0:T(8,128)S(1)}, f32[17,32,128]{2,1,0:T(8,128)S(1)}, u32[]{:S(2)}, u32[]{:S(2)}) collective-permute-start(f32[17,32,128]{2,1,0:T(8,128)S(1)} %get-tuple-element.23), channel_id=1, source_target_pairs={{32,0},{64,32},{96,64},{0,96},{33,1},{65,33},{97,65},{1,97},{34,2}... | collective-permute-start | bytes 835592 | tf_op jit(solution)/shard_map/ppermute | solution.py:616
  14.0 8.2 %collective-permute-start.2 = (f32[66,8,128]{2,1,0:T(8,128)S(1)}, f32[66,8,128]{2,1,0:T(8,128)S(1)}, u32[]{:S(2)}, u32[]{:S(2)}) collective-permute-start(f32[66,8,128]{2,1,0:T(8,128)S(1)} %get-tuple-element.24), channel_id=1, source_target_pairs={{0,8},{8,16},{16,24},{24,0},{1,9},{9,17},{17,25},{25,1},{2,10},{10... | collective-permute-start | bytes 811016 | tf_op jit(solution)/shard_map/ppermute | solution.py:617
  15.4 6.8 %collective-permute-start.3 = (f32[66,8,128]{2,1,0:T(8,128)S(1)}, f32[66,8,128]{2,1,0:T(8,128)S(1)}, u32[]{:S(2)}, u32[]{:S(2)}) collective-permute-start(f32[66,8,128]{2,1,0:T(8,128)S(1)} %get-tuple-element.25), channel_id=1, source_target_pairs={{8,0},{16,8},{24,16},{0,24},{9,1},{17,9},{25,17},{1,25},{10,2},{18... | collective-permute-start | bytes 811016 | tf_op jit(solution)/shard_map/ppermute | solution.py:616
  22.6 5.3 %collective-permute-start.4 = (f32[36,8,128]{2,1,0:T(8,128)S(1)}, f32[36,8,128]{2,1,0:T(8,128)S(1)}, u32[]{:S(2)}, u32[]{:S(2)}) collective-permute-start(f32[36,8,128]{2,1,0:T(8,128)S(1)} %get-tuple-element.26), channel_id=1, source_target_pairs={{0,1},{1,2},{2,3},{3,4},{4,5},{5,6},{6,7},{7,0},{8,9},{9,10},{10,1... | collective-permute-start | bytes 442376 | tf_op jit(solution)/shard_map/ppermute | solution.py:617
  25.8 4.6 %collective-permute-start.5 = (f32[36,8,128]{2,1,0:T(8,128)S(1)}, f32[36,8,128]{2,1,0:T(8,128)S(1)}, u32[]{:S(2)}, u32[]{:S(2)}) collective-permute-start(f32[36,8,128]{2,1,0:T(8,128)S(1)} %get-tuple-element.27), channel_id=1, source_target_pairs={{1,0},{2,1},{3,2},{4,3},{5,4},{6,5},{7,6},{0,7},{9,8},{10,9},{11,1... | collective-permute-start | bytes 442376 | tf_op jit(solution)/shard_map/ppermute | solution.py:616
  40.7 2.1 %copy-start = (f32[8,24,48,128]{3,2,1,0:T(8,128)}, f32[8,24,48,128]{3,2,1,0:T(8,128)S(1)}, u32[]{:S(2)}) copy-start(f32[8,24,48,128]{3,2,1,0:T(8,128)S(1)} %get-tuple-element.36.c0b_in) | copy-start | bytes 14155780
  65.7 5.5 %collective-permute-start.6 = (f32[2,4,64,128]{3,2,1,0:T(8,128)S(1)}, f32[2,4,64,128]{3,2,1,0:T(8,128)S(1)}, u32[]{:S(2)}, u32[]{:S(2)}) collective-permute-start(f32[2,4,64,128]{3,2,1,0:T(8,128)S(1)} %get-tuple-element.29), channel_id=1, source_target_pairs={{0,1},{1,2},{2,3},{3,4},{4,5},{5,6},{6,7},{7,0},{8,9},{9,10},{10,1... | collective-permute-start | bytes 786440 | tf_op jit(solution)/shard_map/ppermute | solution.py:617
  67.9 6.0 %collective-permute-start.7 = (f32[2,4,64,128]{3,2,1,0:T(8,128)S(1)}, f32[2,4,64,128]{3,2,1,0:T(8,128)S(1)}, u32[]{:S(2)}, u32[]{:S(2)}) collective-permute-start(f32[2,4,64,128]{3,2,1,0:T(8,128)S(1)} %get-tuple-element.30), channel_id=1, source_target_pairs={{1,0},{2,1},{3,2},{4,3},{5,4},{6,5},{7,6},{0,7},{9,8},{10,9},{11,1... | collective-permute-start | bytes 786440 | tf_op jit(solution)/shard_map/ppermute | solution.py:616
  96.3 1.9 %collective-permute-start.8 = (f32[4,8,32,128]{3,2,1,0:T(8,128)S(1)}, f32[4,8,32,128]{3,2,1,0:T(8,128)S(1)}, u32[]{:S(2)}, u32[]{:S(2)}) collective-permute-start(f32[4,8,32,128]{3,2,1,0:T(8,128)S(1)} %all_to_all.11.mine), channel_id=1, source_target_pairs={{0,1},{1,0},{2,3},{3,2},{4,5},{5,4},{6,7},{7,6},{8,9},{9,8},{10,11... | collective-permute-start | bytes 1572872 | tf_op jit(solution)/shard_map/ppermute | solution.py:661

commit v2 on v1

--- a/solution.py
+++ b/solution.py
@@ -10,6 +10,8 @@
 F32 = jnp.float32
 COARSE_ITERS = 20
 MIB = 1 << 20
+GROUP = 64
+LIMIT = 50
 
 
 def lanes(rows):
@@ -53,25 +55,46 @@
     return jax.ShapeDtypeStruct(shape, F32)
 
 
-def split_fine(f_ref, b_ref, wf_ref, wb_ref, lo_ref, hi_ref):
+def split_fine(f_in, b_in, wf_ref, wb_ref, lo_ref, hi_ref, b1_ref, f_ref, b_ref, tmp, sems):
+    loads = [pltpu.make_async_copy(b_in, b_ref, sems.at[0]), pltpu.make_async_copy(f_in, f_ref, sems.at[1])]
+    for c in loads:
+        c.start()
     lane, row = lanes(32), sublanes(32)
     index = []
     for parity in range(2):
         odd = (row + parity) % 2
         index.append(2 * (lane % 64) + jnp.where(lane < 64, odd, 1 - odd))
+    loads[0].wait()
+    for n in range(8):
+        w = [pick(b_ref[2 * n + parity], index[parity]) for parity in range(2)]
+        for parity in range(2):
+            i = 2 * n + parity
+            wb_ref[i] = w[parity]
+            if i < 9:
+                lo_ref[8 + i] = w[parity]
+            if i > 6:
+                hi_ref[1 + i] = w[parity]
+        both = w[0] + w[1]
+        b1 = halve_rows(tmp, both + turn(both, 64), 32)
+        b1_ref[16 * n : 16 * n + 16] = pick(b1, by_colour(n, False))
+    loads[1].wait()
     for i in range(16):
         wf = pick(f_ref[i], index[i % 2])
-        wb = pick(b_ref[i], index[i % 2])
         wf_ref[i] = wf
-        wb_ref[i] = wb
         if i < 8:
             lo_ref[i] = wf
         else:
             hi_ref[i - 8] = wf
-        if i < 9:
-            lo_ref[8 + i] = wb
-        if i > 6:
-            hi_ref[1 + i] = wb
+
+
+def by_colour(n, swap):
+    lane, row = lanes(16), sublanes(16)
+    odd = (row + n) % 2
+    return (2 * (lane % 64) + jnp.where((lane < 64) != swap, odd, 1 - odd)) % 128
+
+
+def spared(index):
+    return (index + jnp.where(lanes(16) % 64 < 48, -12, 12)) % 128
 
 
 def plane_f(wf, xl, xu, p):
@@ -100,7 +123,7 @@
 
 def pack_lanes(wf, wb, xl, xu, yl, yu, lo_ref, hi_ref):
     slot_of = lanes(48) % 64
-    for which, width, base in ((0, 4, 0), (1, 8, 12)):
+    for which, width, base in ((0, 16, 0), (1, 16, 48)):
         count = 64 // width
         slot = slot_of // width
         for group in range(32 // count):
@@ -154,20 +177,26 @@
     return out + coef[5, q, c] * pick(mid, index)
 
 
-def pairs(start, stop, body):
+def pairs(start, stop, body, rows):
+    count = stop - start
+    width = max(w for w in (2, 4, 8, 16) if w == 2 or (count % w == 0 and w * rows <= 8 * GROUP))
+
     def step(t, carry):
-        for parity in range(2):
-            body(2 * t + parity, parity)
+        for n in range(width):
+            body(start + t * width + n, n % 2)
         return carry
 
-    lax.fori_loop(start // 2, stop // 2, step, 0)
+    if count == width:
+        step(0, 0)
+    else:
+        lax.fori_loop(0, count // width, step, 0)
 
 
 def update(mine, other, coef, index, start, stop, rows, flip, shift=0):
     def body(p, parity):
         mine[p + 1, 8 : 8 + rows] = relaxed(other, coef, p, index[(parity + flip) % 2], rows, 0, shift)
 
-    pairs(start, stop, body)
+    pairs(start, stop, body, rows)
 
 
 def defect(red, black, cr, cb, p, parity, index, rows, first=0, shift=0):
@@ -210,7 +239,7 @@
             b[q, 56:64] = edge
         for q in (0, 33):
             b[q, 8:56] = jnp.zeros((48, 128), F32)
-    for which, width, base in ((0, 4, 0), (1, 8, 12)):
+    for which, width, base in ((0, 16, 0), (1, 16, 48)):
         count = 64 // width
         slot = (lane % 64) // width
         for p in range(32):
@@ -248,7 +277,7 @@
         make_coefs(bb, br, fb[p], cb, p, index[1 - parity], 1.0, 48)
         vr[p + 1, 8:56] = cr[6, p]
 
-    pairs(0, 32, coefs)
+    pairs(0, 32, coefs, 48)
     copies = [
         pltpu.make_async_copy(cr.at[:, pl.ds(4, 24)], cr_out, sems.at[0]),
         pltpu.make_async_copy(cb.at[:, pl.ds(4, 24)], cb_out, sems.at[1]),
@@ -260,50 +289,35 @@
     update(vr, vb, cr, index, 2, 30, 48, 0)
     update(vb, vr, cb, index, 2, 30, 48, 1)
     copies[2].start()
-
-    lane, row = lanes(16), sublanes(16)
     inner = [side_index(32, parity, 128) for parity in range(2)]
-    swap = jnp.where(gx >= 2, 64, 0)
+    swap = gx >= 2
+    spare = (lanes(16) % 64 >= 38) & (lanes(16) % 64 < 58)
     for n in range(8):
         total = coarse = None
         for parity in range(2):
             p = 8 + 2 * n + parity
             er, eb = defect(vr, vb, cr, cb, p, parity, inner, 32, 8)
-            e = er + eb
             b = br[p + 1, 16:48] + bb[p + 1, 16:48]
-            total = e if total is None else total + e
+            total = er + eb if total is None else total + (er + eb)
             coarse = b if coarse is None else coarse + b
-        f1 = halve_rows(tmp, total, 32)
-        b1 = halve_rows(tmp, coarse, 32)
-        odd = (row + n) % 2
-        idx = 64 * (lane // 64) + 2 * (lane % 32) + jnp.where(lane % 64 < 32, odd, 1 - odd)
-        w1 = pick(jnp.where(lane < 64, f1, turn(b1, 64)), idx ^ swap)
+        f1 = pick(halve_rows(tmp, total, 32), by_colour(n, swap))
+        b1 = pick(halve_rows(tmp, coarse, 32), spared(by_colour(n, swap)))
+        w1 = jnp.where(spare, b1, f1)
         for copy in range(16):
-            g_ref[copy, n] = w1
+            g_ref[copy, 16 * n : 16 * n + 16] = w1
     for c in copies:
         c.wait()
 
 
-def joined(g, p):
+def joined(g, p, swapped):
     a, i = p // 8, p % 8
-    wa = jnp.concatenate([g[4 * a + y, i] for y in range(4)], axis=0)
-    wb = jnp.concatenate([g[4 * (a + 2) + y, i] for y in range(4)], axis=0)
+    r = slice(16 * i, 16 * i + 16)
+    wa = jnp.concatenate([g[4 * a + y, r] for y in range(4)], axis=0)
+    wb = jnp.concatenate([g[4 * (a + 2) + y, r] for y in range(4)], axis=0)
     half = lanes(64) < 64
-    return jnp.where(half, wa, wb), jnp.where(half, wb, wa)
-
-
-def pack_mid(g, lo_ref, hi_ref):
-    slot = (lanes(64) % 32) // 8
-    for group in range(4):
-        low, high = [None] * 2, [None] * 2
-        for s in range(4):
-            for which, v in enumerate(joined(g, 4 * group + s)):
-                v = turn(v, 8 * s)
-                low[which] = v if s == 0 else jnp.where(slot == s, v, low[which])
-                high[which] = v if s == 0 else jnp.where(slot == s - 1, v, high[which])
-        for which in range(2):
-            lo_ref[which, group] = low[which]
-            hi_ref[which, group] = high[which]
+    if swapped:
+        return jnp.where(half, wa, wb), turn(jnp.where(half, wb, wa), 64)
+    return jnp.where(half, wa, turn(wb, 64)), jnp.where(half, turn(wa, 64), wb)
 
 
 def seam(v, rows):
@@ -313,27 +327,23 @@
     v[17, r] = jnp.where(half, turn(v[1, r], 64), 0.0)
 
 
-def mid_down(at, g, zl, zu, w2_ref, cr_out, cb_out, vb_out, br, bb, fr, fb, cr, cb, vr, vb, tmp, sems):
+def mid_down(at, g, gb, w2_ref, cr_out, cb_out, vb_out, br, bb, fr, fb, cr, cb, vr, vb, tmp, sems):
     gy, gz = at[1], at[2]
     lane = lanes(64)
     own = lane % 64 < 32
     keep = own | ((lane % 64 < 48) & (gz < 7)) | ((lane % 64 >= 48) & (gz > 0))
     kept = jnp.where(keep, 1.0, 0.0).astype(F32)
-    slot = (lane % 32) // 8
+    halo = (lane + jnp.where(lane % 64 < 48, 6, -6)) % 128
     for v in (vr, vb):
         v[...] = jnp.zeros_like(v)
     for b in (br, bb):
         b[:, 0:8] = jnp.zeros((18, 8, 128), F32)
         b[:, 72:80] = jnp.zeros((18, 8, 128), F32)
     for p in range(16):
-        mf, mb = joined(g, p)
-        s, group = p % 4, p // 4
-        both = jnp.where(slot == s, zu[0, group], zl[0, group])
-        fr[p] = jnp.where(own, mf, turn(both, 32 - 8 * s))
-        fb[p] = jnp.where(own, turn(mf, 96), turn(both, -8 * s))
-        both = jnp.where(slot == s, zu[1, group], zl[1, group])
-        br[p + 1, 8:72] = kept * jnp.where(own, turn(mb, 64), turn(both, 96 - 8 * s))
-        bb[p + 1, 8:72] = kept * jnp.where(own, turn(mb, 32), turn(both, 64 - 8 * s))
+        fr[p], fb[p] = joined(g, p, True)
+        red, black = joined(gb, p, False)
+        br[p + 1, 8:72] = kept * jnp.where(own, red, pick(fr[p], halo))
+        bb[p + 1, 8:72] = kept * jnp.where(own, black, pick(fb[p], halo))
     seam(br, 64)
     seam(bb, 64)
     index = [side_index(64, parity, 64) for parity in range(2)]
@@ -343,7 +353,7 @@
         make_coefs(bb, br, fb[p], cb, p, index[1 - parity], 0.25, 64)
         vr[p + 1, 8:72] = cr[6, p]
 
-    pairs(0, 16, coefs)
+    pairs(0, 16, coefs, 64)
     seam(vr, 64)
     window = pl.multiple_of(jnp.clip(gy * 16 - 8, 0, 32), 8)
     copies = [
@@ -375,8 +385,7 @@
         odd = (row + n) % 2
         idx = 64 * ((lane % 64) // 32) + 2 * (lane % 16) + jnp.where(lane % 32 < 16, odd, 1 - odd)
         w2 = jnp.where(lane < 64, pick(f2, idx), pick(b2, idx))
-        for copy in range(4):
-            w2_ref[copy, n] = w2
+        w2_ref[n] = w2
     for c in copies:
         c.wait()
 
@@ -410,7 +419,7 @@
         make_coefs(bb, br, fb, cb, p, index[1 - parity], scale, rows, inside and inside[1 - parity])
         vr[p + 1, 8 : 8 + rows] = cr[6, p]
 
-    pairs(0, planes, coefs)
+    pairs(0, planes, coefs, rows)
     update(vb, vr, cb, index, 0, planes, rows, 1)
     update(vr, vb, cr, index, 0, planes, rows, 0)
     update(vb, vr, cb, index, 0, planes, rows, 1)
@@ -454,7 +463,7 @@
 
 
 def coarse_up(
-    at, mine, pair, c1r_in, c1b_in, v1b_in, c0r_in, c0b_in, v0b_in, u_ref, res_ref,
+    at, m0, m1, m2, m3, q0, q1, q2, q3, c1r_in, c1b_in, v1b_in, c0r_in, c0b_in, v0b_in, u_ref, res_ref,
     b2r, b2b, v2r, v2b, c2r, c2b, f2,
     b3r, b3b, v3r, v3b, c3r, c3b, f3,
     b4r, b4b, v4r, v4b, c4r, c4b, f4,
@@ -475,12 +484,17 @@
     v1b[:, 0:8] = jnp.zeros((18, 8, 128), F32)
     v1b[:, 40:48] = jnp.zeros((18, 8, 128), F32)
 
+    chip = gz // 2
     first = gz % 2 == 0
     for n in range(8):
+        near = [(jnp.where(first, a[n], b[n]), jnp.where(first, b[n], a[n])) for a, b in ((m0, q0), (m1, q1), (m2, q2), (m3, q3))]
         blocks = []
-        for chip in range(4):
-            a, b = mine[chip, n], pair[chip, n]
-            blocks += [jnp.where(first, a, b), jnp.where(first, b, a)]
+        for c in range(4):
+            for core in range(2):
+                v = near[0][core]
+                for back in range(1, 4):
+                    v = jnp.where(chip == (c + back) % 4, near[back][core], v)
+                blocks.append(v)
         out = transposed(blocks)
         for h in range(2):
             p = n + 8 * h
@@ -608,7 +622,7 @@
         u_ref[p - 8] = jnp.where(even, pick(red, lane // 2), pick(black, lane // 2))
 
     index1_0 = [side_index(32, parity, 128) for parity in range(2)]
-    pairs(8, 24, finish)
+    pairs(8, 24, finish, 32)
 
 
 def around(lo, hi, axis):
@@ -619,32 +633,40 @@
 
 
 def body(source, conductance):
-    vmem, smem, anywhere = (pl.BlockSpec(memory_space=m) for m in (pltpu.VMEM, pltpu.SMEM, pl.ANY))
+    vmem, smem, hbm = (pl.BlockSpec(memory_space=m) for m in (pltpu.VMEM, pltpu.SMEM, pltpu.HBM))
     at = jnp.stack([lax.axis_index(a) for a in ("gx", "gy", "gz")]).astype(jnp.int32)
     dma = pltpu.SemaphoreType.DMA
 
     block, x_slab = arr(16, 32, 128), arr(17, 32, 128)
-    wf, wb, lo, hi = call(split_fine, [(block, block, x_slab, x_slab)], (source, conductance))
+    buffer = pltpu.VMEM((16, 32, 128), F32)
+    wf, wb, lo, hi, b1 = call(
+        split_fine,
+        [(block, block, x_slab, x_slab, arr(128, 128))],
+        (source, conductance),
+        [hbm] * 2,
+        [buffer, buffer, pltpu.VMEM((32, 128), F32), dma((2,))],
+        8,
+    )
+    gb = lax.all_gather(b1, ("gx", "gy"))
     xl, xu = around(lo, hi, "gx")
-    lo, hi = call(pack_rows, [(arr(66, 8, 128),) * 2], (wf, wb, xl, xu))
+    lo, hi = call(pack_rows, [(arr(66, 8, 128),) * 2], (wf, wb, xl, xu), limit=8)
     yl, yu = around(lo, hi, "gy")
-    lo, hi = call(pack_lanes, [(arr(36, 8, 128),) * 2], (wf, wb, xl, xu, yl, yu))
+    lo, hi = call(pack_lanes, [(arr(96, 8, 128),) * 2], (wf, wb, xl, xu, yl, yu), limit=8)
     zl, zu = around(lo, hi, "gz")
 
-    state0 = (arr(8, 24, 48, 128), arr(8, 24, 48, 128), arr(34, 64, 128))
     colour0 = pltpu.VMEM((34, 64, 128), F32)
     right0 = pltpu.VMEM((32, 48, 128), F32)
     coef0 = pltpu.VMEM((8, 32, 48, 128), F32)
+    state0 = (arr(8, 24, 48, 128), arr(8, 24, 48, 128), arr(34, 64, 128))
     g, c0r, c0b, v0b = call(
         fine_down,
-        [(arr(16, 8, 16, 128),) + state0, (vmem, anywhere, anywhere, anywhere)],
+        [(arr(16, 128, 128),) + state0, (vmem, hbm, hbm, hbm)],
         (at, wf, wb, xl, xu, yl, yu, zl, zu),
         [smem] + [vmem] * 8,
         [colour0, colour0, right0, right0, coef0, coef0, colour0, colour0, pltpu.VMEM((32, 128), F32), dma((3,))],
+        LIMIT,
     )
     g = lax.all_to_all(g, ("gx", "gy"), 0, 0, tiled=True)
-    lo, hi = call(pack_mid, [(arr(2, 4, 64, 128),) * 2], (g,))
-    zl, zu = around(lo, hi, "gz")
 
     state1 = (arr(8, 16, 32, 128), arr(8, 16, 32, 128), arr(18, 32, 128))
     colour1 = pltpu.VMEM((18, 80, 128), F32)
@@ -652,13 +674,14 @@
     coef1 = pltpu.VMEM((8, 16, 64, 128), F32)
     w2, c1r, c1b, v1b = call(
         mid_down,
-        [(arr(4, 8, 32, 128),) + state1, (vmem, anywhere, anywhere, anywhere)],
-        (at, g, zl, zu),
-        [smem] + [vmem] * 3,
+        [(arr(8, 32, 128),) + state1, (vmem, hbm, hbm, hbm)],
+        (at, g, gb),
+        [smem] + [vmem] * 2,
         [colour1, colour1, right1, right1, coef1, coef1, colour1, colour1, pltpu.VMEM((64, 128), F32), dma((3,))],
+        LIMIT,
     )
-    mine = lax.all_to_all(w2, "gz", 0, 0, axis_index_groups=[[0, 2, 4, 6], [1, 3, 5, 7]], tiled=True)
-    pair = lax.ppermute(mine, "gz", [(i, i ^ 1) for i in range(8)])
+    mine = [w2] + [lax.ppermute(w2, "gz", [(i, (i + d) % 8) for i in range(8)]) for d in (2, 4, 6)]
+    pair = [lax.ppermute(w, "gz", [(i, i ^ 1) for i in range(8)]) for w in mine]
 
     scratch = []
     for planes, rows in ((16, 32), (8, 16), (4, 8)):
@@ -669,9 +692,10 @@
     return call(
         coarse_up,
         [(block, block)],
-        (at, mine, pair, c1r, c1b, v1b, c0r, c0b, v0b),
-        [smem, vmem, vmem] + [anywhere] * 6,
+        (at, *mine, *pair, c1r, c1b, v1b, c0r, c0b, v0b),
+        [smem] + [vmem] * 8 + [hbm] * 6,
         scratch,
+        LIMIT,
     )
 
 

time: 125 us -> 117 us (0.936)
  Pallas kernels: 46.5 us -> 31.9 us
  blocking collectives: 36.7 us -> 22.9 us
  between operations: 0.86 us -> 14.1 us
  starting transfers between devices: 13.4 us -> 22.9 us
  waiting for transfers between devices: 23.6 us -> 21.6 us
    pallas_call x7 -> x6, Pallas kernels: 46.5 us -> 31.9 us  [call(): pl.pallas_call(kernel, out_shape=out[0], in_specs=specs or [vmem] * len(a...]
    all_to_all x1 -> x0, blocking collectives: 14 us -> none  [body(): lax.all_to_all(w2, 'gz', 0, 0, axis_index_groups=[[0, 2, 4, 6], [1, 3, 5,...]
    ppermute x1 -> x7, starting transfers between devices: 0.4 us -> 11.9 us  [the longest x4 6.81 us: body(): pair = [lax.ppermute(w, 'gz', [(i, i ^ 1) for i in range(8)]) for w in mine]]
    ppermute x4 -> x3, waiting for transfers between devices: 5.14 us -> 2.65 us  [around(): lax.ppermute(lo, axis, [((i + 1) % count, i) for i in range(count)])]
    ppermute x4 -> x3, starting transfers between devices: 9.3 us -> 7.17 us  [around(): lax.ppermute(hi, axis, [(i, (i + 1) % count) for i in range(count)])]
    unnamed x6 -> x8, local copies, waits for them, and re-layouts: 4.01 us -> 3.12 us
    ppermute x4 -> x3, waiting for transfers between devices: 16.9 us -> 16.6 us  [around(): lax.ppermute(hi, axis, [(i, (i + 1) % count) for i in range(count)])]
    ppermute x4 -> x3, starting transfers between devices: 3.73 us -> 3.72 us  [around(): lax.ppermute(lo, axis, [((i + 1) % count, i) for i in range(count)])]
  transfers between devices with their start and end apart: 9 -> 14, of which waited for: 7 -> 7; matrix products, arithmetic and copies ran while one was open for 0% -> 0% of each run, Pallas kernels for 0% -> 7%
where the time goes in v2:
time: 117 us
  Pallas kernels  31.9 us (27%)
  starting transfers between devices  22.9 us (20%)
  blocking collectives  22.9 us (20%)
  waiting for transfers between devices  21.6 us (18%)
  between operations  14.1 us (12%)
  local copies, waits for them, and re-layouts  3.12 us (3%)
    pallas_call x6, Pallas kernels, call(): pl.pallas_call(kernel, out_shape=out[0], in_specs=specs or [vmem] * len(a...  31.9 us
    all_to_all x1, blocking collectives, body(): g = lax.all_to_all(g, ('gx', 'gy'), 0, 0, tiled=True)  22.9 us
    ppermute x3, waiting for transfers between devices, around(): lax.ppermute(hi, axis, [(i, (i + 1) % count) for i in range(count)])  16.6 us
    ppermute x3, starting transfers between devices, around(): lax.ppermute(hi, axis, [(i, (i + 1) % count) for i in range(count)])  7.17 us
    ppermute x4, starting transfers between devices, body(): pair = [lax.ppermute(w, 'gz', [(i, i ^ 1) for i in range(8)]) for w in mine]  6.81 us
    ppermute x3, starting transfers between devices, body(): lax.ppermute(w2, 'gz', [(i, (i + d) % 8) for i in range(8)])  5.11 us
    ppermute x3, starting transfers between devices, around(): lax.ppermute(lo, axis, [((i + 1) % count, i) for i in range(count)])  3.72 us
    unnamed x8, local copies, waits for them, and re-layouts  3.12 us
  transfers between devices with their start and end apart: 14, of which 7 were waited for; matrix products, arithmetic and copies ran while one was open for 0% of the time, Pallas kernels for 7%

profile of v2, /device:TPU:1, one launch (start us, length us, event | category | flops | bytes accessed | tf_op | source)
XLA Modules:
  0.0 116.5 jit_solution(5167267937188226215)
XLA Ops:
  7.2 0.9 copy-done.2
  8.2 0.9 copy-done.3
  9.1 1.1 split_fine.1
  10.2 2.5 %collective-permute-start = (f32[17,32,128]{2,1,0:T(8,128)S(1)}, f32[17,32,128]{2,1,0:T(8,128)S(1)}, u32[]{:S(2)}, u32[]{:S(2)}) collective-permute-start(f32[17,32,128]{2,1,0:T(8,128)S(1)} %get-tuple-element.21), channel_id=1, source_target_pairs={{0,32},{32,64},{64,96},{96,0},{1,33},{33,65},{65,97},{97,1},{2,34}... | collective-permute-start | bytes 835592 | tf_op jit(solution)/shard_map/ppermute | solution.py:631
  12.8 2.2 %collective-permute-start.1 = (f32[17,32,128]{2,1,0:T(8,128)S(1)}, f32[17,32,128]{2,1,0:T(8,128)S(1)}, u32[]{:S(2)}, u32[]{:S(2)}) collective-permute-start(f32[17,32,128]{2,1,0:T(8,128)S(1)} %get-tuple-element.22), channel_id=1, source_target_pairs={{32,0},{64,32},{96,64},{0,96},{33,1},{65,33},{97,65},{1,97},{34,2}... | collective-permute-start | bytes 835592 | tf_op jit(solution)/shard_map/ppermute | solution.py:630
  15.0 6.3 %collective-permute-done.xl = f32[17,32,128]{2,1,0:T(8,128)S(1)} collective-permute-done((f32[17,32,128]{2,1,0:T(8,128)S(1)}, f32[17,32,128]{2,1,0:T(8,128)S(1)}, u32[]{:S(2)}, u32[]{:S(2)}) %collective-permute-start) | collective-permute-done | bytes 278560 | tf_op jit(solution)/shard_map/ppermute | solution.py:631
  21.3 1.4 %collective-permute-start.2 = (f32[66,8,128]{2,1,0:T(8,128)S(1)}, f32[66,8,128]{2,1,0:T(8,128)S(1)}, u32[]{:S(2)}, u32[]{:S(2)}) collective-permute-start(f32[66,8,128]{2,1,0:T(8,128)S(1)} %get-tuple-element.23), channel_id=1, source_target_pairs={{0,8},{8,16},{16,24},{24,0},{1,9},{9,17},{17,25},{25,1},{2,10},{10... | collective-permute-start | bytes 811016 | tf_op jit(solution)/shard_map/ppermute | solution.py:631
  22.7 1.5 %collective-permute-start.3 = (f32[66,8,128]{2,1,0:T(8,128)S(1)}, f32[66,8,128]{2,1,0:T(8,128)S(1)}, u32[]{:S(2)}, u32[]{:S(2)}) collective-permute-start(f32[66,8,128]{2,1,0:T(8,128)S(1)} %get-tuple-element.24), channel_id=1, source_target_pairs={{8,0},{16,8},{24,16},{0,24},{9,1},{17,9},{25,17},{1,25},{10,2},{18... | collective-permute-start | bytes 811016 | tf_op jit(solution)/shard_map/ppermute | solution.py:630
  24.2 5.6 %collective-permute-done.2.yl = f32[66,8,128]{2,1,0:T(8,128)S(1)} collective-permute-done((f32[66,8,128]{2,1,0:T(8,128)S(1)}, f32[66,8,128]{2,1,0:T(8,128)S(1)}, u32[]{:S(2)}, u32[]{:S(2)}) %collective-permute-start.2) | collective-permute-done | bytes 270368 | tf_op jit(solution)/shard_map/ppermute | solution.py:631
  30.4 3.3 %collective-permute-start.4 = (f32[96,8,128]{2,1,0:T(8,128)S(1)}, f32[96,8,128]{2,1,0:T(8,128)S(1)}, u32[]{:S(2)}, u32[]{:S(2)}) collective-permute-start(f32[96,8,128]{2,1,0:T(8,128)S(1)} %get-tuple-element.25), channel_id=1, source_target_pairs={{0,1},{1,2},{2,3},{3,4},{4,5},{5,6},{6,7},{7,0},{8,9},{9,10},{10,1... | collective-permute-start | bytes 1179656 | tf_op jit(solution)/shard_map/ppermute | solution.py:631
  33.7 4.6 %collective-permute-done.4.zl = f32[96,8,128]{2,1,0:T(8,128)S(1)} collective-permute-done((f32[96,8,128]{2,1,0:T(8,128)S(1)}, f32[96,8,128]{2,1,0:T(8,128)S(1)}, u32[]{:S(2)}, u32[]{:S(2)}) %collective-permute-start.4) | collective-permute-done | bytes 393248 | tf_op jit(solution)/shard_map/ppermute | solution.py:631
  38.4 2.5 %collective-permute-done.5.zu = f32[96,8,128]{2,1,0:T(8,128)S(1)} collective-permute-done((f32[96,8,128]{2,1,0:T(8,128)S(1)}, f32[96,8,128]{2,1,0:T(8,128)S(1)}, u32[]{:S(2)}, u32[]{:S(2)}) %collective-permute-start.5) | collective-permute-done | bytes 393248 | tf_op jit(solution)/shard_map/ppermute | solution.py:630
  40.9 7.8 %fine_down.1 = (f32[16,128,128]{2,1,0:T(8,128)S(1)}, f32[8,24,48,128]{3,2,1,0:T(8,128)}, f32[8,24,48,128]{3,2,1,0:T(8,128)}, f32[34,64,128]{2,1,0:T(8,128)}) custom-call(s32[3]{0:T(128)S(1)} %pad_add_fusion.at, f32[16,32,128]{2,1,0:T(8,128)S(1)} %get-tuple-element.19.wf, f32[16,32,128]{2,1,0:T(8,128)S(1)} %get-tuple-element.20.wb, ...), custom_call_target="tpu_custom_call" | custom-call | tf_op jit(solution)/shard_map/fine_down/pallas_call | solution.py:43
  48.6 22.9 %all_to_all.5.g = f32[16,128,128]{2,1,0:T(8,128)S(1)} all-to-all(f32[16,128,128]{2,1,0:T(8,128)S(1)} %get-tuple-element.27), channel_id=1, replica_groups=mesh['gx'=4,'gy'=4,'gz'=8] {'gx','gy'}, dimensions={0} | all-to-all | bytes 2097152 | tf_op jit(solution)/shard_map/all_to_all | solution.py:669
  71.6 1.2 %copy-done.1 = f32[2048,128]{1,0:T(8,128)S(1)} copy-done((f32[2048,128]{1,0:T(8,128)S(1)}, f32[2048,128]{1,0:T(8,128)}, u32[]{:S(2)}) %copy-start.1) | copy-done | bytes 1048600
  72.8 6.6 %mid_down.1 = (f32[8,32,128]{2,1,0:T(8,128)S(1)}, f32[8,16,32,128]{3,2,1,0:T(8,128)}, f32[8,16,32,128]{3,2,1,0:T(8,128)}, f32[18,32,128]{2,1,0:T(8,128)S(1)}) custom-call(s32[3]{0:T(128)S(1)} %pad_add_fusion.at, f32[16,128,128]{2,1,0:T(8,128)S(1)} %all_to_all.5.g, f32[16,128,128]{2,1,0:T(8,128)S(1)} %bitcast.4), custom_call_target="tpu_custom_call" | custom-call | tf_op jit(solution)/shard_map/mid_down/pallas_call | solution.py:43
  79.4 3.1 %collective-permute-start.8 = (f32[8,32,128]{2,1,0:T(8,128)S(1)}, f32[8,32,128]{2,1,0:T(8,128)S(1)}, u32[]{:S(2)}, u32[]{:S(2)}) collective-permute-start(f32[8,32,128]{2,1,0:T(8,128)S(1)} %get-tuple-element.29.m0), channel_id=1, source_target_pairs={{0,6},{1,7},{2,0},{3,1},{4,2},{5,3},{6,4},{7,5},{8,14},{9,15},{10,... | collective-permute-start | bytes 393224 | tf_op jit(solution)/shard_map/ppermute | solution.py:683
  82.4 1.3 %collective-permute-start.7 = (f32[8,32,128]{2,1,0:T(8,128)S(1)}, f32[8,32,128]{2,1,0:T(8,128)S(1)}, u32[]{:S(2)}, u32[]{:S(2)}) collective-permute-start(f32[8,32,128]{2,1,0:T(8,128)S(1)} %get-tuple-element.29.m0), channel_id=1, source_target_pairs={{0,4},{1,5},{2,6},{3,7},{4,0},{5,1},{6,2},{7,3},{8,12},{9,13},{10,... | collective-permute-start | bytes 393224 | tf_op jit(solution)/shard_map/ppermute | solution.py:683
  84.5 1.2 %collective-permute-start.9 = (f32[8,32,128]{2,1,0:T(8,128)S(1)}, f32[8,32,128]{2,1,0:T(8,128)S(1)}, u32[]{:S(2)}, u32[]{:S(2)}) collective-permute-start(f32[8,32,128]{2,1,0:T(8,128)S(1)} %get-tuple-element.29.m0), channel_id=1, source_target_pairs={{0,1},{1,0},{2,3},{3,2},{4,5},{5,4},{6,7},{7,6},{8,9},{9,8},{10,11... | collective-permute-start | bytes 393224 | tf_op jit(solution)/shard_map/ppermute | solution.py:684
  85.7 3.3 %collective-permute-start.12 = (f32[8,32,128]{2,1,0:T(8,128)S(1)}, f32[8,32,128]{2,1,0:T(8,128)S(1)}, u32[]{:S(2)}, u32[]{:S(2)}) collective-permute-start(f32[8,32,128]{2,1,0:T(8,128)S(1)} %collective-permute-done.8.m3), channel_id=1, source_target_pairs={{0,1},{1,0},{2,3},{3,2},{4,5},{5,4},{6,7},{7,6},{8,9},{9,8},{10,11... | collective-permute-start | bytes 393224 | tf_op jit(solution)/shard_map/ppermute | solution.py:684
  89.0 1.8 %collective-permute-start.11 = (f32[8,32,128]{2,1,0:T(8,128)S(1)}, f32[8,32,128]{2,1,0:T(8,128)S(1)}, u32[]{:S(2)}, u32[]{:S(2)}) collective-permute-start(f32[8,32,128]{2,1,0:T(8,128)S(1)} %collective-permute-done.7.m2), channel_id=1, source_target_pairs={{0,1},{1,0},{2,3},{3,2},{4,5},{5,4},{6,7},{7,6},{8,9},{9,8},{10,11... | collective-permute-start | bytes 393224 | tf_op jit(solution)/shard_map/ppermute | solution.py:684
  90.8 1.4 %collective-permute-done.6.m1 = f32[8,32,128]{2,1,0:T(8,128)S(1)} collective-permute-done((f32[8,32,128]{2,1,0:T(8,128)S(1)}, f32[8,32,128]{2,1,0:T(8,128)S(1)}, u32[]{:S(2)}, u32[]{:S(2)}) %collective-permute-start.6) | collective-permute-done | bytes 131104 | tf_op jit(solution)/shard_map/ppermute | solution.py:683
  92.7 1.0 collective-permute-done.10.q1
  93.7 16.0 %coarse_up.1 = (f32[16,32,128]{2,1,0:T(8,128)}, f32[16,32,128]{2,1,0:T(8,128)}) custom-call(s32[3]{0:T(128)S(1)} %pad_add_fusion.at, f32[8,32,128]{2,1,0:T(8,128)S(1)} %get-tuple-element.29.m0, f32[8,32,128]{2,1,0:T(8,128)S(1)} %collective-permute-done.6.m1, f32[8,32,128]{2,1,0:T(8,128)S(1)} %collective-permute-done.7.m2, ...), custom_call_target="tpu_custom_call" | custom-call | tf_op jit(solution)/shard_map/coarse_up/pallas_call | solution.py:43
  (21 shorter events, 2.0 us)
Async XLA Ops:
  7.2 64.4 %all-gather.3.cloned.1.call-start = ((), (), s32[]{:S(2)}) async-start(), calls=%async_computation.1 | async-start | bytes 1114112 | tf_op jit(solution)/shard_map/all_gather | solution.py:650
  7.2 1.0 copy-start.2
  8.2 0.9 copy-start.3
  10.2 11.0 %collective-permute-start = (f32[17,32,128]{2,1,0:T(8,128)S(1)}, f32[17,32,128]{2,1,0:T(8,128)S(1)}, u32[]{:S(2)}, u32[]{:S(2)}) collective-permute-start(f32[17,32,128]{2,1,0:T(8,128)S(1)} %get-tuple-element.21), channel_id=1, source_target_pairs={{0,32},{32,64},{64,96},{96,0},{1,33},{33,65},{65,97},{97,1},{2,34}... | collective-permute-start | bytes 835592 | tf_op jit(solution)/shard_map/ppermute | solution.py:631
  12.8 8.5 %collective-permute-start.1 = (f32[17,32,128]{2,1,0:T(8,128)S(1)}, f32[17,32,128]{2,1,0:T(8,128)S(1)}, u32[]{:S(2)}, u32[]{:S(2)}) collective-permute-start(f32[17,32,128]{2,1,0:T(8,128)S(1)} %get-tuple-element.22), channel_id=1, source_target_pairs={{32,0},{64,32},{96,64},{0,96},{33,1},{65,33},{97,65},{1,97},{34,2}... | collective-permute-start | bytes 835592 | tf_op jit(solution)/shard_map/ppermute | solution.py:630
  21.3 8.5 %collective-permute-start.2 = (f32[66,8,128]{2,1,0:T(8,128)S(1)}, f32[66,8,128]{2,1,0:T(8,128)S(1)}, u32[]{:S(2)}, u32[]{:S(2)}) collective-permute-start(f32[66,8,128]{2,1,0:T(8,128)S(1)} %get-tuple-element.23), channel_id=1, source_target_pairs={{0,8},{8,16},{16,24},{24,0},{1,9},{9,17},{17,25},{25,1},{2,10},{10... | collective-permute-start | bytes 811016 | tf_op jit(solution)/shard_map/ppermute | solution.py:631
  22.7 7.3 %collective-permute-start.3 = (f32[66,8,128]{2,1,0:T(8,128)S(1)}, f32[66,8,128]{2,1,0:T(8,128)S(1)}, u32[]{:S(2)}, u32[]{:S(2)}) collective-permute-start(f32[66,8,128]{2,1,0:T(8,128)S(1)} %get-tuple-element.24), channel_id=1, source_target_pairs={{8,0},{16,8},{24,16},{0,24},{9,1},{17,9},{25,17},{1,25},{10,2},{18... | collective-permute-start | bytes 811016 | tf_op jit(solution)/shard_map/ppermute | solution.py:630
  30.4 8.0 %collective-permute-start.4 = (f32[96,8,128]{2,1,0:T(8,128)S(1)}, f32[96,8,128]{2,1,0:T(8,128)S(1)}, u32[]{:S(2)}, u32[]{:S(2)}) collective-permute-start(f32[96,8,128]{2,1,0:T(8,128)S(1)} %get-tuple-element.25), channel_id=1, source_target_pairs={{0,1},{1,2},{2,3},{3,4},{4,5},{5,6},{6,7},{7,0},{8,9},{9,10},{10,1... | collective-permute-start | bytes 1179656 | tf_op jit(solution)/shard_map/ppermute | solution.py:631
  33.7 7.2 %collective-permute-start.5 = (f32[96,8,128]{2,1,0:T(8,128)S(1)}, f32[96,8,128]{2,1,0:T(8,128)S(1)}, u32[]{:S(2)}, u32[]{:S(2)}) collective-permute-start(f32[96,8,128]{2,1,0:T(8,128)S(1)} %get-tuple-element.26), channel_id=1, source_target_pairs={{1,0},{2,1},{3,2},{4,3},{5,4},{6,5},{7,6},{0,7},{9,8},{10,9},{11,1... | collective-permute-start | bytes 1179656 | tf_op jit(solution)/shard_map/ppermute | solution.py:630
  48.6 45.0 %copy-start = (f32[34,64,128]{2,1,0:T(8,128)S(1)}, f32[34,64,128]{2,1,0:T(8,128)}, u32[]{:S(2)}) copy-start(f32[34,64,128]{2,1,0:T(8,128)} %get-tuple-element.35.v0b_in) | copy-start | bytes 3342340
  71.6 1.2 %copy-start.1 = (f32[2048,128]{1,0:T(8,128)S(1)}, f32[2048,128]{1,0:T(8,128)}, u32[]{:S(2)}) copy-start(f32[2048,128]{1,0:T(8,128)} %all-gather.3.cloned.1.call-done) | copy-start | bytes 3145732
  79.4 6.4 %collective-permute-start.8 = (f32[8,32,128]{2,1,0:T(8,128)S(1)}, f32[8,32,128]{2,1,0:T(8,128)S(1)}, u32[]{:S(2)}, u32[]{:S(2)}) collective-permute-start(f32[8,32,128]{2,1,0:T(8,128)S(1)} %get-tuple-element.29.m0), channel_id=1, source_target_pairs={{0,6},{1,7},{2,0},{3,1},{4,2},{5,3},{6,4},{7,5},{8,14},{9,15},{10,... | collective-permute-start | bytes 393224 | tf_op jit(solution)/shard_map/ppermute | solution.py:683
  82.4 6.6 %collective-permute-start.7 = (f32[8,32,128]{2,1,0:T(8,128)S(1)}, f32[8,32,128]{2,1,0:T(8,128)S(1)}, u32[]{:S(2)}, u32[]{:S(2)}) collective-permute-start(f32[8,32,128]{2,1,0:T(8,128)S(1)} %get-tuple-element.29.m0), channel_id=1, source_target_pairs={{0,4},{1,5},{2,6},{3,7},{4,0},{5,1},{6,2},{7,3},{8,12},{9,13},{10,... | collective-permute-start | bytes 393224 | tf_op jit(solution)/shard_map/ppermute | solution.py:683
  83.7 8.4 %collective-permute-start.6 = (f32[8,32,128]{2,1,0:T(8,128)S(1)}, f32[8,32,128]{2,1,0:T(8,128)S(1)}, u32[]{:S(2)}, u32[]{:S(2)}) collective-permute-start(f32[8,32,128]{2,1,0:T(8,128)S(1)} %get-tuple-element.29.m0), channel_id=1, source_target_pairs={{0,2},{1,3},{2,4},{3,5},{4,6},{5,7},{6,0},{7,1},{8,10},{9,11},{10,... | collective-permute-start | bytes 393224 | tf_op jit(solution)/shard_map/ppermute | solution.py:683
  84.5 8.2 %collective-permute-start.9 = (f32[8,32,128]{2,1,0:T(8,128)S(1)}, f32[8,32,128]{2,1,0:T(8,128)S(1)}, u32[]{:S(2)}, u32[]{:S(2)}) collective-permute-start(f32[8,32,128]{2,1,0:T(8,128)S(1)} %get-tuple-element.29.m0), channel_id=1, source_target_pairs={{0,1},{1,0},{2,3},{3,2},{4,5},{5,4},{6,7},{7,6},{8,9},{9,8},{10,11... | collective-permute-start | bytes 393224 | tf_op jit(solution)/shard_map/ppermute | solution.py:684
  85.7 6.9 %collective-permute-start.12 = (f32[8,32,128]{2,1,0:T(8,128)S(1)}, f32[8,32,128]{2,1,0:T(8,128)S(1)}, u32[]{:S(2)}, u32[]{:S(2)}) collective-permute-start(f32[8,32,128]{2,1,0:T(8,128)S(1)} %collective-permute-done.8.m3), channel_id=1, source_target_pairs={{0,1},{1,0},{2,3},{3,2},{4,5},{5,4},{6,7},{7,6},{8,9},{9,8},{10,11... | collective-permute-start | bytes 393224 | tf_op jit(solution)/shard_map/ppermute | solution.py:684
  89.0 3.7 %collective-permute-start.11 = (f32[8,32,128]{2,1,0:T(8,128)S(1)}, f32[8,32,128]{2,1,0:T(8,128)S(1)}, u32[]{:S(2)}, u32[]{:S(2)}) collective-permute-start(f32[8,32,128]{2,1,0:T(8,128)S(1)} %collective-permute-done.7.m2), channel_id=1, source_target_pairs={{0,1},{1,0},{2,3},{3,2},{4,5},{5,4},{6,7},{7,6},{8,9},{9,8},{10,11... | collective-permute-start | bytes 393224 | tf_op jit(solution)/shard_map/ppermute | solution.py:684
  92.2 1.5 %collective-permute-start.10 = (f32[8,32,128]{2,1,0:T(8,128)S(1)}, f32[8,32,128]{2,1,0:T(8,128)S(1)}, u32[]{:S(2)}, u32[]{:S(2)}) collective-permute-start(f32[8,32,128]{2,1,0:T(8,128)S(1)} %collective-permute-done.6.m1), channel_id=1, source_target_pairs={{0,1},{1,0},{2,3},{3,2},{4,5},{5,4},{6,7},{7,6},{8,9},{9,8},{10,11... | collective-permute-start | bytes 393224 | tf_op jit(solution)/shard_map/ppermute | solution.py:684
Sparse Core Ops, SparseCore 0:
  10.7 44.7 all-gather.2

commit v3 on v2

--- a/solution.py
+++ b/solution.py
@@ -55,7 +55,7 @@
     return jax.ShapeDtypeStruct(shape, F32)
 
 
-def split_fine(f_in, b_in, wf_ref, wb_ref, lo_ref, hi_ref, b1_ref, f_ref, b_ref, tmp, sems):
+def split_fine(f_in, b_in, wf_ref, wb_ref, lo_ref, hi_ref, f_ref, b_ref, sems):
     loads = [pltpu.make_async_copy(b_in, b_ref, sems.at[0]), pltpu.make_async_copy(f_in, f_ref, sems.at[1])]
     for c in loads:
         c.start()
@@ -65,18 +65,13 @@
         odd = (row + parity) % 2
         index.append(2 * (lane % 64) + jnp.where(lane < 64, odd, 1 - odd))
     loads[0].wait()
-    for n in range(8):
-        w = [pick(b_ref[2 * n + parity], index[parity]) for parity in range(2)]
-        for parity in range(2):
-            i = 2 * n + parity
-            wb_ref[i] = w[parity]
-            if i < 9:
-                lo_ref[8 + i] = w[parity]
-            if i > 6:
-                hi_ref[1 + i] = w[parity]
-        both = w[0] + w[1]
-        b1 = halve_rows(tmp, both + turn(both, 64), 32)
-        b1_ref[16 * n : 16 * n + 16] = pick(b1, by_colour(n, False))
+    for i in range(16):
+        wb = pick(b_ref[i], index[i % 2])
+        wb_ref[i] = wb
+        if i < 9:
+            lo_ref[8 + i] = wb
+        if i > 6:
+            hi_ref[1 + i] = wb
     loads[1].wait()
     for i in range(16):
         wf = pick(f_ref[i], index[i % 2])
@@ -291,7 +286,10 @@
     copies[2].start()
     inner = [side_index(32, parity, 128) for parity in range(2)]
     swap = gx >= 2
-    spare = (lanes(16) % 64 >= 38) & (lanes(16) % 64 < 58)
+    lane16, row16 = lanes(16), sublanes(16)
+    spare = (lane16 % 64 >= 38) & (lane16 % 64 < 58)
+    odd16 = [(row16 + parity) % 2 for parity in range(2)]
+    own1 = {}
     for n in range(8):
         total = coarse = None
         for parity in range(2):
@@ -301,23 +299,36 @@
             total = er + eb if total is None else total + (er + eb)
             coarse = b if coarse is None else coarse + b
         f1 = pick(halve_rows(tmp, total, 32), by_colour(n, swap))
-        b1 = pick(halve_rows(tmp, coarse, 32), spared(by_colour(n, swap)))
-        w1 = jnp.where(spare, b1, f1)
+        b1 = halve_rows(tmp, coarse, 32)
+        w1 = jnp.where(spare, pick(b1, spared(by_colour(n, swap))), f1)
+        own1[n] = pick(b1, 2 * (lane16 % 32) + jnp.where(lane16 % 64 < 32, odd16[n % 2], 1 - odd16[n % 2]))
         for copy in range(16):
             g_ref[copy, 16 * n : 16 * n + 16] = w1
+    for n in range(4):
+        w1 = jnp.where(lane16 < 64, own1[n], own1[n + 4])
+        for copy in range(16):
+            g_ref[copy, 128 + 16 * n : 144 + 16 * n] = w1
     for c in copies:
         c.wait()
 
 
-def joined(g, p, swapped):
-    a, i = p // 8, p % 8
-    r = slice(16 * i, 16 * i + 16)
-    wa = jnp.concatenate([g[4 * a + y, r] for y in range(4)], axis=0)
-    wb = jnp.concatenate([g[4 * (a + 2) + y, r] for y in range(4)], axis=0)
+def across(g, a, start):
+    r = slice(start, start + 16)
+    return jnp.concatenate([g[4 * a + y, r] for y in range(4)], axis=0)
+
+
+def joined_f(g, p):
+    wa, wb = (across(g, p // 8 + up, 16 * (p % 8)) for up in (0, 2))
     half = lanes(64) < 64
-    if swapped:
-        return jnp.where(half, wa, wb), turn(jnp.where(half, wb, wa), 64)
-    return jnp.where(half, wa, turn(wb, 64)), jnp.where(half, turn(wa, 64), wb)
+    return jnp.where(half, wa, wb), turn(jnp.where(half, wb, wa), 64)
+
+
+def joined_b(g, p):
+    i = p % 8
+    wa, wb = (across(g, p // 8 + up, 128 + 16 * (i % 4)) for up in (0, 2))
+    half = lanes(64) < 64
+    red = jnp.where(half, wa, turn(wb, 64)) if i < 4 else jnp.where(half, turn(wa, 64), wb)
+    return red, turn(red, -32)
 
 
 def seam(v, rows):
@@ -327,7 +338,7 @@
     v[17, r] = jnp.where(half, turn(v[1, r], 64), 0.0)
 
 
-def mid_down(at, g, gb, w2_ref, cr_out, cb_out, vb_out, br, bb, fr, fb, cr, cb, vr, vb, tmp, sems):
+def mid_down(at, g, w2_ref, cr_out, cb_out, vb_out, br, bb, fr, fb, cr, cb, vr, vb, tmp, sems):
     gy, gz = at[1], at[2]
     lane = lanes(64)
     own = lane % 64 < 32
@@ -340,8 +351,8 @@
         b[:, 0:8] = jnp.zeros((18, 8, 128), F32)
         b[:, 72:80] = jnp.zeros((18, 8, 128), F32)
     for p in range(16):
-        fr[p], fb[p] = joined(g, p, True)
-        red, black = joined(gb, p, False)
+        fr[p], fb[p] = joined_f(g, p)
+        red, black = joined_b(g, p)
         br[p + 1, 8:72] = kept * jnp.where(own, red, pick(fr[p], halo))
         bb[p + 1, 8:72] = kept * jnp.where(own, black, pick(fb[p], halo))
     seam(br, 64)
@@ -639,15 +650,14 @@
 
     block, x_slab = arr(16, 32, 128), arr(17, 32, 128)
     buffer = pltpu.VMEM((16, 32, 128), F32)
-    wf, wb, lo, hi, b1 = call(
+    wf, wb, lo, hi = call(
         split_fine,
-        [(block, block, x_slab, x_slab, arr(128, 128))],
+        [(block, block, x_slab, x_slab)],
         (source, conductance),
         [hbm] * 2,
-        [buffer, buffer, pltpu.VMEM((32, 128), F32), dma((2,))],
+        [buffer, buffer, dma((2,))],
         8,
     )
-    gb = lax.all_gather(b1, ("gx", "gy"))
     xl, xu = around(lo, hi, "gx")
     lo, hi = call(pack_rows, [(arr(66, 8, 128),) * 2], (wf, wb, xl, xu), limit=8)
     yl, yu = around(lo, hi, "gy")
@@ -660,7 +670,7 @@
     state0 = (arr(8, 24, 48, 128), arr(8, 24, 48, 128), arr(34, 64, 128))
     g, c0r, c0b, v0b = call(
         fine_down,
-        [(arr(16, 128, 128),) + state0, (vmem, hbm, hbm, hbm)],
+        [(arr(16, 192, 128),) + state0, (vmem, hbm, hbm, hbm)],
         (at, wf, wb, xl, xu, yl, yu, zl, zu),
         [smem] + [vmem] * 8,
         [colour0, colour0, right0, right0, coef0, coef0, colour0, colour0, pltpu.VMEM((32, 128), F32), dma((3,))],
@@ -675,8 +685,8 @@
     w2, c1r, c1b, v1b = call(
         mid_down,
         [(arr(8, 32, 128),) + state1, (vmem, hbm, hbm, hbm)],
-        (at, g, gb),
-        [smem] + [vmem] * 2,
+        (at, g),
+        [smem, vmem],
         [colour1, colour1, right1, right1, coef1, coef1, colour1, colour1, pltpu.VMEM((64, 128), F32), dma((3,))],
         LIMIT,
     )

time: 117 us -> 110 us (0.940)
  between operations: 14.1 us -> 0.86 us
  blocking collectives: 22.9 us -> 28.5 us
    all_to_all x1, blocking collectives: 22.9 us -> 28.5 us  [body(): g = lax.all_to_all(g, ('gx', 'gy'), 0, 0, tiled=True)]
    unnamed x8 -> x6, local copies, waits for them, and re-layouts: 3.12 us -> 3.33 us
  transfers between devices with their start and end apart: 14 -> 13, of which waited for: 7 -> 6; matrix products, arithmetic and copies ran while one was open for 0% -> 0% of each run, Pallas kernels for 7% -> 0%
where the time goes in v3:
time: 110 us
  Pallas kernels  33 us (30%)
  blocking collectives  28.5 us (26%)
  starting transfers between devices  22.8 us (21%)
  waiting for transfers between devices  21 us (19%)
  local copies, waits for them, and re-layouts  3.33 us (3%)
    pallas_call x6, Pallas kernels, call(): pl.pallas_call(kernel, out_shape=out[0], in_specs=specs or [vmem] * len(a...  33 us
    all_to_all x1, blocking collectives, body(): g = lax.all_to_all(g, ('gx', 'gy'), 0, 0, tiled=True)  28.5 us
    ppermute x3, waiting for transfers between devices, around(): lax.ppermute(hi, axis, [(i, (i + 1) % count) for i in range(count)])  16.2 us
    ppermute x3, starting transfers between devices, around(): lax.ppermute(hi, axis, [(i, (i + 1) % count) for i in range(count)])  7.12 us
    ppermute x4, starting transfers between devices, body(): pair = [lax.ppermute(w, 'gz', [(i, i ^ 1) for i in range(8)]) for w in mine]  6.64 us
    ppermute x3, starting transfers between devices, body(): lax.ppermute(w2, 'gz', [(i, (i + d) % 8) for i in range(8)])  5.28 us
    ppermute x3, starting transfers between devices, around(): lax.ppermute(lo, axis, [((i + 1) % count, i) for i in range(count)])  3.72 us
    unnamed x6, local copies, waits for them, and re-layouts  3.33 us
  transfers between devices with their start and end apart: 13, of which 6 were waited for; matrix products, arithmetic and copies ran while one was open for 0% of the time, Pallas kernels for 0%

profile of v3, /device:TPU:1, one launch (start us, length us, event | category | flops | bytes accessed | tf_op | source)
XLA Modules:
  0.0 109.5 jit_solution(8048577048149674052)
XLA Ops:
  0.6 0.9 copy-done.1
  1.6 0.9 copy-done.2
  3.1 2.5 %collective-permute-start = (f32[17,32,128]{2,1,0:T(8,128)S(1)}, f32[17,32,128]{2,1,0:T(8,128)S(1)}, u32[]{:S(2)}, u32[]{:S(2)}) collective-permute-start(f32[17,32,128]{2,1,0:T(8,128)S(1)} %get-tuple-element.20), channel_id=1, source_target_pairs={{0,32},{32,64},{64,96},{96,0},{1,33},{33,65},{65,97},{97,1},{2,34}... | collective-permute-start | bytes 835592 | tf_op jit(solution)/shard_map/ppermute | solution.py:642
  5.6 2.2 %collective-permute-start.1 = (f32[17,32,128]{2,1,0:T(8,128)S(1)}, f32[17,32,128]{2,1,0:T(8,128)S(1)}, u32[]{:S(2)}, u32[]{:S(2)}) collective-permute-start(f32[17,32,128]{2,1,0:T(8,128)S(1)} %get-tuple-element.21), channel_id=1, source_target_pairs={{32,0},{64,32},{96,64},{0,96},{33,1},{65,33},{97,65},{1,97},{34,2}... | collective-permute-start | bytes 835592 | tf_op jit(solution)/shard_map/ppermute | solution.py:641
  7.8 6.3 %collective-permute-done.xl = f32[17,32,128]{2,1,0:T(8,128)S(1)} collective-permute-done((f32[17,32,128]{2,1,0:T(8,128)S(1)}, f32[17,32,128]{2,1,0:T(8,128)S(1)}, u32[]{:S(2)}, u32[]{:S(2)}) %collective-permute-start) | collective-permute-done | bytes 278560 | tf_op jit(solution)/shard_map/ppermute | solution.py:642
  14.2 1.4 %collective-permute-start.2 = (f32[66,8,128]{2,1,0:T(8,128)S(1)}, f32[66,8,128]{2,1,0:T(8,128)S(1)}, u32[]{:S(2)}, u32[]{:S(2)}) collective-permute-start(f32[66,8,128]{2,1,0:T(8,128)S(1)} %get-tuple-element.22), channel_id=1, source_target_pairs={{0,8},{8,16},{16,24},{24,0},{1,9},{9,17},{17,25},{25,1},{2,10},{10... | collective-permute-start | bytes 811016 | tf_op jit(solution)/shard_map/ppermute | solution.py:642
  15.5 1.5 %collective-permute-start.3 = (f32[66,8,128]{2,1,0:T(8,128)S(1)}, f32[66,8,128]{2,1,0:T(8,128)S(1)}, u32[]{:S(2)}, u32[]{:S(2)}) collective-permute-start(f32[66,8,128]{2,1,0:T(8,128)S(1)} %get-tuple-element.23), channel_id=1, source_target_pairs={{8,0},{16,8},{24,16},{0,24},{9,1},{17,9},{25,17},{1,25},{10,2},{18... | collective-permute-start | bytes 811016 | tf_op jit(solution)/shard_map/ppermute | solution.py:641
  17.1 5.3 %collective-permute-done.2.yl = f32[66,8,128]{2,1,0:T(8,128)S(1)} collective-permute-done((f32[66,8,128]{2,1,0:T(8,128)S(1)}, f32[66,8,128]{2,1,0:T(8,128)S(1)}, u32[]{:S(2)}, u32[]{:S(2)}) %collective-permute-start.2) | collective-permute-done | bytes 270368 | tf_op jit(solution)/shard_map/ppermute | solution.py:642
  22.7 3.2 %collective-permute-start.4 = (f32[96,8,128]{2,1,0:T(8,128)S(1)}, f32[96,8,128]{2,1,0:T(8,128)S(1)}, u32[]{:S(2)}, u32[]{:S(2)}) collective-permute-start(f32[96,8,128]{2,1,0:T(8,128)S(1)} %get-tuple-element.24), channel_id=1, source_target_pairs={{0,1},{1,2},{2,3},{3,4},{4,5},{5,6},{6,7},{7,0},{8,9},{9,10},{10,1... | collective-permute-start | bytes 1179656 | tf_op jit(solution)/shard_map/ppermute | solution.py:642
  26.0 4.6 %collective-permute-done.4.zl = f32[96,8,128]{2,1,0:T(8,128)S(1)} collective-permute-done((f32[96,8,128]{2,1,0:T(8,128)S(1)}, f32[96,8,128]{2,1,0:T(8,128)S(1)}, u32[]{:S(2)}, u32[]{:S(2)}) %collective-permute-start.4) | collective-permute-done | bytes 393248 | tf_op jit(solution)/shard_map/ppermute | solution.py:642
  30.7 2.5 %collective-permute-done.5.zu = f32[96,8,128]{2,1,0:T(8,128)S(1)} collective-permute-done((f32[96,8,128]{2,1,0:T(8,128)S(1)}, f32[96,8,128]{2,1,0:T(8,128)S(1)}, u32[]{:S(2)}, u32[]{:S(2)}) %collective-permute-start.5) | collective-permute-done | bytes 393248 | tf_op jit(solution)/shard_map/ppermute | solution.py:641
  33.1 8.8 %fine_down.1 = (f32[16,192,128]{2,1,0:T(8,128)}, f32[8,24,48,128]{3,2,1,0:T(8,128)}, f32[8,24,48,128]{3,2,1,0:T(8,128)}, f32[34,64,128]{2,1,0:T(8,128)S(1)}) custom-call(s32[3]{0:T(128)S(1)} %pad_add_fusion.at, f32[16,32,128]{2,1,0:T(8,128)S(1)} %get-tuple-element.18.wf, f32[16,32,128]{2,1,0:T(8,128)S(1)} %get-tuple-element.19.wb, ...), custom_call_target="tpu_custom_call" | custom-call | tf_op jit(solution)/shard_map/fine_down/pallas_call | solution.py:43
  41.9 28.5 %all_to_all.5.g = f32[16,192,128]{2,1,0:T(8,128)S(1)} all-to-all(f32[16,192,128]{2,1,0:T(8,128)} %get-tuple-element.26), channel_id=1, replica_groups=mesh['gx'=4,'gy'=4,'gz'=8] {'gx','gy'}, dimensions={0} | all-to-all | bytes 3145728 | tf_op jit(solution)/shard_map/all_to_all | solution.py:679
  70.4 7.3 %mid_down.1 = (f32[8,32,128]{2,1,0:T(8,128)S(1)}, f32[8,16,32,128]{3,2,1,0:T(8,128)S(1)}, f32[8,16,32,128]{3,2,1,0:T(8,128)}, f32[18,32,128]{2,1,0:T(8,128)S(1)}) custom-call(s32[3]{0:T(128)S(1)} %pad_add_fusion.at, f32[16,192,128]{2,1,0:T(8,128)S(1)} %all_to_all.5.g), custom_call_target="tpu_custom_call" | custom-call | tf_op jit(solution)/shard_map/mid_down/pallas_call | solution.py:43
  77.7 1.4 %copy-done = f32[8,16,32,128]{3,2,1,0:T(8,128)} copy-done((f32[8,16,32,128]{3,2,1,0:T(8,128)}, f32[8,16,32,128]{3,2,1,0:T(8,128)S(1)}, u32[]{:S(2)}) %copy-start) | copy-done | bytes 2097176
  79.2 3.0 %collective-permute-start.8 = (f32[8,32,128]{2,1,0:T(8,128)S(1)}, f32[8,32,128]{2,1,0:T(8,128)S(1)}, u32[]{:S(2)}, u32[]{:S(2)}) collective-permute-start(f32[8,32,128]{2,1,0:T(8,128)S(1)} %get-tuple-element.27.m0), channel_id=1, source_target_pairs={{0,6},{1,7},{2,0},{3,1},{4,2},{5,3},{6,4},{7,5},{8,14},{9,15},{10,... | collective-permute-start | bytes 393224 | tf_op jit(solution)/shard_map/ppermute | solution.py:693
  82.2 1.4 %collective-permute-start.7 = (f32[8,32,128]{2,1,0:T(8,128)S(1)}, f32[8,32,128]{2,1,0:T(8,128)S(1)}, u32[]{:S(2)}, u32[]{:S(2)}) collective-permute-start(f32[8,32,128]{2,1,0:T(8,128)S(1)} %get-tuple-element.27.m0), channel_id=1, source_target_pairs={{0,4},{1,5},{2,6},{3,7},{4,0},{5,1},{6,2},{7,3},{8,12},{9,13},{10,... | collective-permute-start | bytes 393224 | tf_op jit(solution)/shard_map/ppermute | solution.py:693
  83.6 0.9 collective-permute-start.6
  84.5 1.2 %collective-permute-start.9 = (f32[8,32,128]{2,1,0:T(8,128)S(1)}, f32[8,32,128]{2,1,0:T(8,128)S(1)}, u32[]{:S(2)}, u32[]{:S(2)}) collective-permute-start(f32[8,32,128]{2,1,0:T(8,128)S(1)} %get-tuple-element.27.m0), channel_id=1, source_target_pairs={{0,1},{1,0},{2,3},{3,2},{4,5},{5,4},{6,7},{7,6},{8,9},{9,8},{10,11... | collective-permute-start | bytes 393224 | tf_op jit(solution)/shard_map/ppermute | solution.py:694
  85.7 3.0 %collective-permute-start.12 = (f32[8,32,128]{2,1,0:T(8,128)S(1)}, f32[8,32,128]{2,1,0:T(8,128)S(1)}, u32[]{:S(2)}, u32[]{:S(2)}) collective-permute-start(f32[8,32,128]{2,1,0:T(8,128)S(1)} %collective-permute-done.8.m3), channel_id=1, source_target_pairs={{0,1},{1,0},{2,3},{3,2},{4,5},{5,4},{6,7},{7,6},{8,9},{9,8},{10,11... | collective-permute-start | bytes 393224 | tf_op jit(solution)/shard_map/ppermute | solution.py:694
  88.7 1.8 %collective-permute-start.11 = (f32[8,32,128]{2,1,0:T(8,128)S(1)}, f32[8,32,128]{2,1,0:T(8,128)S(1)}, u32[]{:S(2)}, u32[]{:S(2)}) collective-permute-start(f32[8,32,128]{2,1,0:T(8,128)S(1)} %collective-permute-done.7.m2), channel_id=1, source_target_pairs={{0,1},{1,0},{2,3},{3,2},{4,5},{5,4},{6,7},{7,6},{8,9},{9,8},{10,11... | collective-permute-start | bytes 393224 | tf_op jit(solution)/shard_map/ppermute | solution.py:694
  90.5 1.3 %collective-permute-done.6.m1 = f32[8,32,128]{2,1,0:T(8,128)S(1)} collective-permute-done((f32[8,32,128]{2,1,0:T(8,128)S(1)}, f32[8,32,128]{2,1,0:T(8,128)S(1)}, u32[]{:S(2)}, u32[]{:S(2)}) %collective-permute-start.6) | collective-permute-done | bytes 131104 | tf_op jit(solution)/shard_map/ppermute | solution.py:693
  92.4 1.0 collective-permute-done.10.q1
  93.4 16.0 %coarse_up.1 = (f32[16,32,128]{2,1,0:T(8,128)}, f32[16,32,128]{2,1,0:T(8,128)}) custom-call(s32[3]{0:T(128)S(1)} %pad_add_fusion.at, f32[8,32,128]{2,1,0:T(8,128)S(1)} %get-tuple-element.27.m0, f32[8,32,128]{2,1,0:T(8,128)S(1)} %collective-permute-done.6.m1, f32[8,32,128]{2,1,0:T(8,128)S(1)} %collective-permute-done.7.m2, ...), custom_call_target="tpu_custom_call" | custom-call | tf_op jit(solution)/shard_map/coarse_up/pallas_call | solution.py:43
  (16 shorter events, 1.7 us)
Async XLA Ops:
  0.6 1.0 copy-start.1
  1.6 0.9 copy-start.2
  3.1 11.0 %collective-permute-start = (f32[17,32,128]{2,1,0:T(8,128)S(1)}, f32[17,32,128]{2,1,0:T(8,128)S(1)}, u32[]{:S(2)}, u32[]{:S(2)}) collective-permute-start(f32[17,32,128]{2,1,0:T(8,128)S(1)} %get-tuple-element.20), channel_id=1, source_target_pairs={{0,32},{32,64},{64,96},{96,0},{1,33},{33,65},{65,97},{97,1},{2,34}... | collective-permute-start | bytes 835592 | tf_op jit(solution)/shard_map/ppermute | solution.py:642
  5.6 8.5 %collective-permute-start.1 = (f32[17,32,128]{2,1,0:T(8,128)S(1)}, f32[17,32,128]{2,1,0:T(8,128)S(1)}, u32[]{:S(2)}, u32[]{:S(2)}) collective-permute-start(f32[17,32,128]{2,1,0:T(8,128)S(1)} %get-tuple-element.21), channel_id=1, source_target_pairs={{32,0},{64,32},{96,64},{0,96},{33,1},{65,33},{97,65},{1,97},{34,2}... | collective-permute-start | bytes 835592 | tf_op jit(solution)/shard_map/ppermute | solution.py:641
  14.2 8.2 %collective-permute-start.2 = (f32[66,8,128]{2,1,0:T(8,128)S(1)}, f32[66,8,128]{2,1,0:T(8,128)S(1)}, u32[]{:S(2)}, u32[]{:S(2)}) collective-permute-start(f32[66,8,128]{2,1,0:T(8,128)S(1)} %get-tuple-element.22), channel_id=1, source_target_pairs={{0,8},{8,16},{16,24},{24,0},{1,9},{9,17},{17,25},{25,1},{2,10},{10... | collective-permute-start | bytes 811016 | tf_op jit(solution)/shard_map/ppermute | solution.py:642
  15.5 6.8 %collective-permute-start.3 = (f32[66,8,128]{2,1,0:T(8,128)S(1)}, f32[66,8,128]{2,1,0:T(8,128)S(1)}, u32[]{:S(2)}, u32[]{:S(2)}) collective-permute-start(f32[66,8,128]{2,1,0:T(8,128)S(1)} %get-tuple-element.23), channel_id=1, source_target_pairs={{8,0},{16,8},{24,16},{0,24},{9,1},{17,9},{25,17},{1,25},{10,2},{18... | collective-permute-start | bytes 811016 | tf_op jit(solution)/shard_map/ppermute | solution.py:641
  22.7 7.9 %collective-permute-start.4 = (f32[96,8,128]{2,1,0:T(8,128)S(1)}, f32[96,8,128]{2,1,0:T(8,128)S(1)}, u32[]{:S(2)}, u32[]{:S(2)}) collective-permute-start(f32[96,8,128]{2,1,0:T(8,128)S(1)} %get-tuple-element.24), channel_id=1, source_target_pairs={{0,1},{1,2},{2,3},{3,4},{4,5},{5,6},{6,7},{7,0},{8,9},{9,10},{10,1... | collective-permute-start | bytes 1179656 | tf_op jit(solution)/shard_map/ppermute | solution.py:642
  25.9 7.2 %collective-permute-start.5 = (f32[96,8,128]{2,1,0:T(8,128)S(1)}, f32[96,8,128]{2,1,0:T(8,128)S(1)}, u32[]{:S(2)}, u32[]{:S(2)}) collective-permute-start(f32[96,8,128]{2,1,0:T(8,128)S(1)} %get-tuple-element.25), channel_id=1, source_target_pairs={{1,0},{2,1},{3,2},{4,3},{5,4},{6,5},{7,6},{0,7},{9,8},{10,9},{11,1... | collective-permute-start | bytes 1179656 | tf_op jit(solution)/shard_map/ppermute | solution.py:641
  77.7 1.4 %copy-start = (f32[8,16,32,128]{3,2,1,0:T(8,128)}, f32[8,16,32,128]{3,2,1,0:T(8,128)S(1)}, u32[]{:S(2)}) copy-start(f32[8,16,32,128]{3,2,1,0:T(8,128)S(1)} %get-tuple-element.28.c1r_in) | copy-start | bytes 6291460
  79.2 6.5 %collective-permute-start.8 = (f32[8,32,128]{2,1,0:T(8,128)S(1)}, f32[8,32,128]{2,1,0:T(8,128)S(1)}, u32[]{:S(2)}, u32[]{:S(2)}) collective-permute-start(f32[8,32,128]{2,1,0:T(8,128)S(1)} %get-tuple-element.27.m0), channel_id=1, source_target_pairs={{0,6},{1,7},{2,0},{3,1},{4,2},{5,3},{6,4},{7,5},{8,14},{9,15},{10,... | collective-permute-start | bytes 393224 | tf_op jit(solution)/shard_map/ppermute | solution.py:693
  82.2 6.6 %collective-permute-start.7 = (f32[8,32,128]{2,1,0:T(8,128)S(1)}, f32[8,32,128]{2,1,0:T(8,128)S(1)}, u32[]{:S(2)}, u32[]{:S(2)}) collective-permute-start(f32[8,32,128]{2,1,0:T(8,128)S(1)} %get-tuple-element.27.m0), channel_id=1, source_target_pairs={{0,4},{1,5},{2,6},{3,7},{4,0},{5,1},{6,2},{7,3},{8,12},{9,13},{10,... | collective-permute-start | bytes 393224 | tf_op jit(solution)/shard_map/ppermute | solution.py:693
  83.6 8.2 %collective-permute-start.6 = (f32[8,32,128]{2,1,0:T(8,128)S(1)}, f32[8,32,128]{2,1,0:T(8,128)S(1)}, u32[]{:S(2)}, u32[]{:S(2)}) collective-permute-start(f32[8,32,128]{2,1,0:T(8,128)S(1)} %get-tuple-element.27.m0), channel_id=1, source_target_pairs={{0,2},{1,3},{2,4},{3,5},{4,6},{5,7},{6,0},{7,1},{8,10},{9,11},{10,... | collective-permute-start | bytes 393224 | tf_op jit(solution)/shard_map/ppermute | solution.py:693
  84.5 7.9 %collective-permute-start.9 = (f32[8,32,128]{2,1,0:T(8,128)S(1)}, f32[8,32,128]{2,1,0:T(8,128)S(1)}, u32[]{:S(2)}, u32[]{:S(2)}) collective-permute-start(f32[8,32,128]{2,1,0:T(8,128)S(1)} %get-tuple-element.27.m0), channel_id=1, source_target_pairs={{0,1},{1,0},{2,3},{3,2},{4,5},{5,4},{6,7},{7,6},{8,9},{9,8},{10,11... | collective-permute-start | bytes 393224 | tf_op jit(solution)/shard_map/ppermute | solution.py:694
  85.7 6.7 %collective-permute-start.12 = (f32[8,32,128]{2,1,0:T(8,128)S(1)}, f32[8,32,128]{2,1,0:T(8,128)S(1)}, u32[]{:S(2)}, u32[]{:S(2)}) collective-permute-start(f32[8,32,128]{2,1,0:T(8,128)S(1)} %collective-permute-done.8.m3), channel_id=1, source_target_pairs={{0,1},{1,0},{2,3},{3,2},{4,5},{5,4},{6,7},{7,6},{8,9},{9,8},{10,11... | collective-permute-start | bytes 393224 | tf_op jit(solution)/shard_map/ppermute | solution.py:694
  88.7 3.7 %collective-permute-start.11 = (f32[8,32,128]{2,1,0:T(8,128)S(1)}, f32[8,32,128]{2,1,0:T(8,128)S(1)}, u32[]{:S(2)}, u32[]{:S(2)}) collective-permute-start(f32[8,32,128]{2,1,0:T(8,128)S(1)} %collective-permute-done.7.m2), channel_id=1, source_target_pairs={{0,1},{1,0},{2,3},{3,2},{4,5},{5,4},{6,7},{7,6},{8,9},{9,8},{10,11... | collective-permute-start | bytes 393224 | tf_op jit(solution)/shard_map/ppermute | solution.py:694
  91.8 1.6 %collective-permute-start.10 = (f32[8,32,128]{2,1,0:T(8,128)S(1)}, f32[8,32,128]{2,1,0:T(8,128)S(1)}, u32[]{:S(2)}, u32[]{:S(2)}) collective-permute-start(f32[8,32,128]{2,1,0:T(8,128)S(1)} %collective-permute-done.6.m1), channel_id=1, source_target_pairs={{0,1},{1,0},{2,3},{3,2},{4,5},{5,4},{6,7},{7,6},{8,9},{9,8},{10,11... | collective-permute-start | bytes 393224 | tf_op jit(solution)/shard_map/ppermute | solution.py:694

commit v4 on v3

--- a/solution.py
+++ b/solution.py
@@ -12,6 +12,8 @@
 MIB = 1 << 20
 GROUP = 64
 LIMIT = 50
+LIMIT_MID = 50
+LIMIT_UP = 44
 
 
 def lanes(rows):
@@ -36,6 +38,16 @@
     step = 2 * ((row + parity) % 2) - 1
     within = (lane % period + step + period) % period
     return lane - lane % period + within
+
+
+def side_rule(rows, parity):
+    return (sublanes(rows) + parity) % 2 == 0
+
+
+def beside(x, rule):
+    if rule.dtype == jnp.bool_:
+        return jnp.where(rule, pltpu.roll(x, 1, 1), pltpu.roll(x, 127, 1))
+    return pick(x, rule)
 
 
 def call(kernel, out, args, specs=None, scratch=(), limit=40):
@@ -140,11 +152,11 @@
     r = slice(8, 8 + rows)
     centre = mine[p + 1, r]
     mid = other[p + 1, r]
-    side = pick(mid, index)
+    side = beside(mid, index)
     if inside is not None:
         side = jnp.where(inside, side, 0.0)
-    beside = (other[p, r], other[p + 2, r], other[p + 1, 7 : 7 + rows], other[p + 1, 9 : 9 + rows], mid, side)
-    weights = [centre + b for b in beside]
+    others = (other[p, r], other[p + 2, r], other[p + 1, 7 : 7 + rows], other[p + 1, 9 : 9 + rows], mid, side)
+    weights = [centre + b for b in others]
     total = weights[0]
     for w in weights[1:]:
         total = total + w
@@ -169,12 +181,13 @@
     out = out + coef[2, q, c] * other[p + 1, a - 1 : a - 1 + rows]
     out = out + coef[3, q, c] * other[p + 1, a + 1 : a + 1 + rows]
     out = out + coef[4, q, c] * mid
-    return out + coef[5, q, c] * pick(mid, index)
+    return out + coef[5, q, c] * beside(mid, index)
 
 
 def pairs(start, stop, body, rows):
     count = stop - start
-    width = max(w for w in (2, 4, 8, 16) if w == 2 or (count % w == 0 and w * rows <= 8 * GROUP))
+    most = 8 * GROUP if rows < 64 else 16 * GROUP
+    width = max(w for w in (2, 4, 8, 16) if w == 2 or (count % w == 0 and w * rows <= most))
 
     def step(t, carry):
         for n in range(width):
@@ -265,7 +278,7 @@
         br[q, 16:48] = v
         bb[q, 16:48] = turn(v, 64)
 
-    index = [side_index(48, parity, 128) for parity in range(2)]
+    index = [side_rule(48, parity) for parity in range(2)]
 
     def coefs(p, parity):
         make_coefs(br, bb, fr[p], cr, p, index[parity], 1.0, 48)
@@ -284,7 +297,7 @@
     update(vr, vb, cr, index, 2, 30, 48, 0)
     update(vb, vr, cb, index, 2, 30, 48, 1)
     copies[2].start()
-    inner = [side_index(32, parity, 128) for parity in range(2)]
+    inner = [side_rule(32, parity) for parity in range(2)]
     swap = gx >= 2
     lane16, row16 = lanes(16), sublanes(16)
     spare = (lane16 % 64 >= 38) & (lane16 % 64 < 58)
@@ -514,8 +527,8 @@
             b2r[p + 1, 8:40] = out[4 + 2 * h]
             b2b[p + 1, 8:40] = out[5 + 2 * h]
     lane = lanes(32)
-    index2 = [side_index(32, parity, 128) for parity in range(2)]
-    inside2 = [jnp.abs(index2[parity] - lane) < 64 for parity in range(2)]
+    index2 = [side_rule(32, parity) for parity in range(2)]
+    inside2 = [lane != jnp.where(index2[parity], 0, 127) for parity in range(2)]
     smooth_down(b2r, b2b, v2r, v2b, c2r, c2b, lambda p: (f2[0, p], f2[1, p]), index2, 0.25**2, 16, 32, inside2)
 
     def put3(n, fr, fb, br, bb):
@@ -524,7 +537,7 @@
 
     restrict((b2r, b2b, v2r, v2b, c2r, c2b), tmp, index2, 16, 32, 64, put3)
 
-    index3 = [side_index(16, parity, 128) for parity in range(2)]
+    index3 = [side_rule(16, parity) for parity in range(2)]
     smooth_down(b3r, b3b, v3r, v3b, c3r, c3b, lambda p: (f3[0, p], f3[1, p]), index3, 0.25**3, 8, 16, None)
 
     def put4(n, fr, fb, br, bb):
@@ -533,7 +546,7 @@
 
     restrict((b3r, b3b, v3r, v3b, c3r, c3b), tmp, index3, 8, 16, 32, put4)
 
-    index4 = [side_index(8, parity, 128) for parity in range(2)]
+    index4 = [side_rule(8, parity) for parity in range(2)]
 
     for p in range(4):
         make_coefs(b4r, b4b, f4[0, p], c4r, p, index4[p % 2], 0.25**4, 8)
@@ -556,7 +569,7 @@
             if p < 3:
                 w = w + c[1] * other[p + 1]
             w = w + c[2] * pltpu.roll(v, 1, 0) + c[3] * pltpu.roll(v, 7, 0)
-            out.append(w + c[5] * pick(v, index4[(p + flip) % 2]))
+            out.append(w + c[5] * beside(v, index4[(p + flip) % 2]))
         return out
 
     def coarse_step(count, state):
@@ -619,7 +632,7 @@
         double_rows(tmp, tmp[68:92], 24)
         for p in (2 * n + 8, 2 * n + 9):
             v0b[p + 1, 8:56] += tmp[0:48]
-    index0 = [side_index(48, parity, 128) for parity in range(2)]
+    index0 = [side_rule(48, parity) for parity in range(2)]
     update(v0r, v0b, c0r, index0, 4, 28, 48, 0, 4)
     update(v0b, v0r, c0b, index0, 4, 28, 48, 1, 4)
     update(v0r, v0b, c0r, index0, 6, 26, 48, 0, 4)
@@ -632,7 +645,7 @@
         red, black = v0r[p + 1, 16:48], v0b[p + 1, 16:48]
         u_ref[p - 8] = jnp.where(even, pick(red, lane // 2), pick(black, lane // 2))
 
-    index1_0 = [side_index(32, parity, 128) for parity in range(2)]
+    index1_0 = [side_rule(32, parity) for parity in range(2)]
     pairs(8, 24, finish, 32)
 
 
@@ -688,7 +701,7 @@
         (at, g),
         [smem, vmem],
         [colour1, colour1, right1, right1, coef1, coef1, colour1, colour1, pltpu.VMEM((64, 128), F32), dma((3,))],
-        LIMIT,
+        LIMIT_MID,
     )
     mine = [w2] + [lax.ppermute(w2, "gz", [(i, (i + d) % 8) for i in range(8)]) for d in (2, 4, 6)]
     pair = [lax.ppermute(w, "gz", [(i, i ^ 1) for i in range(8)]) for w in mine]
@@ -705,7 +718,7 @@
         (at, *mine, *pair, c1r, c1b, v1b, c0r, c0b, v0b),
         [smem] + [vmem] * 8 + [hbm] * 6,
         scratch,
-        LIMIT,
+        LIMIT_UP,
     )
 
 

time: 110 us -> 108 us (0.982)
  Pallas kernels: 33 us -> 31.5 us
    pallas_call x6, Pallas kernels: 33 us -> 31.5 us  [call(): pl.pallas_call(kernel, out_shape=out[0], in_specs=specs or [vmem] * len(a...]
where the time goes in v4:
time: 108 us
  Pallas kernels  31.5 us (29%)
  blocking collectives  28.5 us (26%)
  starting transfers between devices  22.9 us (21%)
  waiting for transfers between devices  20.9 us (19%)
  local copies, waits for them, and re-layouts  3.48 us (3%)
    pallas_call x6, Pallas kernels, call(): pl.pallas_call(kernel, out_shape=out[0], in_specs=specs or [vmem] * len(a...  31.5 us
    all_to_all x1, blocking collectives, body(): g = lax.all_to_all(g, ('gx', 'gy'), 0, 0, tiled=True)  28.5 us
    ppermute x3, waiting for transfers between devices, around(): lax.ppermute(hi, axis, [(i, (i + 1) % count) for i in range(count)])  16.2 us
    ppermute x3, starting transfers between devices, around(): lax.ppermute(hi, axis, [(i, (i + 1) % count) for i in range(count)])  7.12 us
    ppermute x4, starting transfers between devices, body(): pair = [lax.ppermute(w, 'gz', [(i, i ^ 1) for i in range(8)]) for w in mine]  6.69 us
    ppermute x3, starting transfers between devices, body(): lax.ppermute(w2, 'gz', [(i, (i + d) % 8) for i in range(8)])  5.35 us
    ppermute x3, starting transfers between devices, around(): lax.ppermute(lo, axis, [((i + 1) % count, i) for i in range(count)])  3.72 us
    unnamed x6, local copies, waits for them, and re-layouts  3.48 us
  transfers between devices with their start and end apart: 13, of which 6 were waited for; matrix products, arithmetic and copies ran while one was open for 0% of the time, Pallas kernels for 0%

profile of v4, /device:TPU:1, one launch (start us, length us, event | category | flops | bytes accessed | tf_op | source)
XLA Modules:
  0.0 108.2 jit_solution(11916749606504100628)
XLA Ops:
  0.6 0.9 copy-done.1
  1.6 0.9 copy-done.2
  3.1 2.5 %collective-permute-start = (f32[17,32,128]{2,1,0:T(8,128)S(1)}, f32[17,32,128]{2,1,0:T(8,128)S(1)}, u32[]{:S(2)}, u32[]{:S(2)}) collective-permute-start(f32[17,32,128]{2,1,0:T(8,128)S(1)} %get-tuple-element.20), channel_id=1, source_target_pairs={{0,32},{32,64},{64,96},{96,0},{1,33},{33,65},{65,97},{97,1},{2,34}... | collective-permute-start | bytes 835592 | tf_op jit(solution)/shard_map/ppermute | solution.py:655
  5.6 2.2 %collective-permute-start.1 = (f32[17,32,128]{2,1,0:T(8,128)S(1)}, f32[17,32,128]{2,1,0:T(8,128)S(1)}, u32[]{:S(2)}, u32[]{:S(2)}) collective-permute-start(f32[17,32,128]{2,1,0:T(8,128)S(1)} %get-tuple-element.21), channel_id=1, source_target_pairs={{32,0},{64,32},{96,64},{0,96},{33,1},{65,33},{97,65},{1,97},{34,2}... | collective-permute-start | bytes 835592 | tf_op jit(solution)/shard_map/ppermute | solution.py:654
  7.8 6.3 %collective-permute-done.xl = f32[17,32,128]{2,1,0:T(8,128)S(1)} collective-permute-done((f32[17,32,128]{2,1,0:T(8,128)S(1)}, f32[17,32,128]{2,1,0:T(8,128)S(1)}, u32[]{:S(2)}, u32[]{:S(2)}) %collective-permute-start) | collective-permute-done | bytes 278560 | tf_op jit(solution)/shard_map/ppermute | solution.py:655
  14.2 1.4 %collective-permute-start.2 = (f32[66,8,128]{2,1,0:T(8,128)S(1)}, f32[66,8,128]{2,1,0:T(8,128)S(1)}, u32[]{:S(2)}, u32[]{:S(2)}) collective-permute-start(f32[66,8,128]{2,1,0:T(8,128)S(1)} %get-tuple-element.22), channel_id=1, source_target_pairs={{0,8},{8,16},{16,24},{24,0},{1,9},{9,17},{17,25},{25,1},{2,10},{10... | collective-permute-start | bytes 811016 | tf_op jit(solution)/shard_map/ppermute | solution.py:655
  15.5 1.5 %collective-permute-start.3 = (f32[66,8,128]{2,1,0:T(8,128)S(1)}, f32[66,8,128]{2,1,0:T(8,128)S(1)}, u32[]{:S(2)}, u32[]{:S(2)}) collective-permute-start(f32[66,8,128]{2,1,0:T(8,128)S(1)} %get-tuple-element.23), channel_id=1, source_target_pairs={{8,0},{16,8},{24,16},{0,24},{9,1},{17,9},{25,17},{1,25},{10,2},{18... | collective-permute-start | bytes 811016 | tf_op jit(solution)/shard_map/ppermute | solution.py:654
  17.1 5.3 %collective-permute-done.2.yl = f32[66,8,128]{2,1,0:T(8,128)S(1)} collective-permute-done((f32[66,8,128]{2,1,0:T(8,128)S(1)}, f32[66,8,128]{2,1,0:T(8,128)S(1)}, u32[]{:S(2)}, u32[]{:S(2)}) %collective-permute-start.2) | collective-permute-done | bytes 270368 | tf_op jit(solution)/shard_map/ppermute | solution.py:655
  22.7 3.2 %collective-permute-start.4 = (f32[96,8,128]{2,1,0:T(8,128)S(1)}, f32[96,8,128]{2,1,0:T(8,128)S(1)}, u32[]{:S(2)}, u32[]{:S(2)}) collective-permute-start(f32[96,8,128]{2,1,0:T(8,128)S(1)} %get-tuple-element.24), channel_id=1, source_target_pairs={{0,1},{1,2},{2,3},{3,4},{4,5},{5,6},{6,7},{7,0},{8,9},{9,10},{10,1... | collective-permute-start | bytes 1179656 | tf_op jit(solution)/shard_map/ppermute | solution.py:655
  26.0 4.6 %collective-permute-done.4.zl = f32[96,8,128]{2,1,0:T(8,128)S(1)} collective-permute-done((f32[96,8,128]{2,1,0:T(8,128)S(1)}, f32[96,8,128]{2,1,0:T(8,128)S(1)}, u32[]{:S(2)}, u32[]{:S(2)}) %collective-permute-start.4) | collective-permute-done | bytes 393248 | tf_op jit(solution)/shard_map/ppermute | solution.py:655
  30.7 2.5 %collective-permute-done.5.zu = f32[96,8,128]{2,1,0:T(8,128)S(1)} collective-permute-done((f32[96,8,128]{2,1,0:T(8,128)S(1)}, f32[96,8,128]{2,1,0:T(8,128)S(1)}, u32[]{:S(2)}, u32[]{:S(2)}) %collective-permute-start.5) | collective-permute-done | bytes 393248 | tf_op jit(solution)/shard_map/ppermute | solution.py:654
  33.1 8.3 %fine_down.1 = (f32[16,192,128]{2,1,0:T(8,128)}, f32[8,24,48,128]{3,2,1,0:T(8,128)}, f32[8,24,48,128]{3,2,1,0:T(8,128)}, f32[34,64,128]{2,1,0:T(8,128)S(1)}) custom-call(s32[3]{0:T(128)S(1)} %pad_add_fusion.at, f32[16,32,128]{2,1,0:T(8,128)S(1)} %get-tuple-element.18.wf, f32[16,32,128]{2,1,0:T(8,128)S(1)} %get-tuple-element.19.wb, ...), custom_call_target="tpu_custom_call" | custom-call | tf_op jit(solution)/shard_map/fine_down/pallas_call | solution.py:55
  41.4 28.5 %all_to_all.5.g = f32[16,192,128]{2,1,0:T(8,128)S(1)} all-to-all(f32[16,192,128]{2,1,0:T(8,128)} %get-tuple-element.26), channel_id=1, replica_groups=mesh['gx'=4,'gy'=4,'gz'=8] {'gx','gy'}, dimensions={0} | all-to-all | bytes 3145728 | tf_op jit(solution)/shard_map/all_to_all | solution.py:692
  69.9 6.7 %mid_down.1 = (f32[8,32,128]{2,1,0:T(8,128)S(1)}, f32[8,16,32,128]{3,2,1,0:T(8,128)S(1)}, f32[8,16,32,128]{3,2,1,0:T(8,128)}, f32[18,32,128]{2,1,0:T(8,128)S(1)}) custom-call(s32[3]{0:T(128)S(1)} %pad_add_fusion.at, f32[16,192,128]{2,1,0:T(8,128)S(1)} %all_to_all.5.g), custom_call_target="tpu_custom_call" | custom-call | tf_op jit(solution)/shard_map/mid_down/pallas_call | solution.py:55
  76.7 3.1 %collective-permute-start.8 = (f32[8,32,128]{2,1,0:T(8,128)S(1)}, f32[8,32,128]{2,1,0:T(8,128)S(1)}, u32[]{:S(2)}, u32[]{:S(2)}) collective-permute-start(f32[8,32,128]{2,1,0:T(8,128)S(1)} %get-tuple-element.27.m0), channel_id=1, source_target_pairs={{0,6},{1,7},{2,0},{3,1},{4,2},{5,3},{6,4},{7,5},{8,14},{9,15},{10,... | collective-permute-start | bytes 393224 | tf_op jit(solution)/shard_map/ppermute | solution.py:706
  79.7 1.5 %collective-permute-start.7 = (f32[8,32,128]{2,1,0:T(8,128)S(1)}, f32[8,32,128]{2,1,0:T(8,128)S(1)}, u32[]{:S(2)}, u32[]{:S(2)}) collective-permute-start(f32[8,32,128]{2,1,0:T(8,128)S(1)} %get-tuple-element.27.m0), channel_id=1, source_target_pairs={{0,4},{1,5},{2,6},{3,7},{4,0},{5,1},{6,2},{7,3},{8,12},{9,13},{10,... | collective-permute-start | bytes 393224 | tf_op jit(solution)/shard_map/ppermute | solution.py:706
  81.3 0.8 collective-permute-start.6
  82.0 1.2 %collective-permute-start.9 = (f32[8,32,128]{2,1,0:T(8,128)S(1)}, f32[8,32,128]{2,1,0:T(8,128)S(1)}, u32[]{:S(2)}, u32[]{:S(2)}) collective-permute-start(f32[8,32,128]{2,1,0:T(8,128)S(1)} %get-tuple-element.27.m0), channel_id=1, source_target_pairs={{0,1},{1,0},{2,3},{3,2},{4,5},{5,4},{6,7},{7,6},{8,9},{9,8},{10,11... | collective-permute-start | bytes 393224 | tf_op jit(solution)/shard_map/ppermute | solution.py:707
  83.3 3.0 %collective-permute-start.12 = (f32[8,32,128]{2,1,0:T(8,128)S(1)}, f32[8,32,128]{2,1,0:T(8,128)S(1)}, u32[]{:S(2)}, u32[]{:S(2)}) collective-permute-start(f32[8,32,128]{2,1,0:T(8,128)S(1)} %collective-permute-done.8.m3), channel_id=1, source_target_pairs={{0,1},{1,0},{2,3},{3,2},{4,5},{5,4},{6,7},{7,6},{8,9},{9,8},{10,11... | collective-permute-start | bytes 393224 | tf_op jit(solution)/shard_map/ppermute | solution.py:707
  86.3 1.8 %collective-permute-start.11 = (f32[8,32,128]{2,1,0:T(8,128)S(1)}, f32[8,32,128]{2,1,0:T(8,128)S(1)}, u32[]{:S(2)}, u32[]{:S(2)}) collective-permute-start(f32[8,32,128]{2,1,0:T(8,128)S(1)} %collective-permute-done.7.m2), channel_id=1, source_target_pairs={{0,1},{1,0},{2,3},{3,2},{4,5},{5,4},{6,7},{7,6},{8,9},{9,8},{10,11... | collective-permute-start | bytes 393224 | tf_op jit(solution)/shard_map/ppermute | solution.py:707
  88.1 1.2 %collective-permute-done.6.m1 = f32[8,32,128]{2,1,0:T(8,128)S(1)} collective-permute-done((f32[8,32,128]{2,1,0:T(8,128)S(1)}, f32[8,32,128]{2,1,0:T(8,128)S(1)}, u32[]{:S(2)}, u32[]{:S(2)}) %collective-permute-start.6) | collective-permute-done | bytes 131104 | tf_op jit(solution)/shard_map/ppermute | solution.py:706
  90.0 1.0 collective-permute-done.10.q1
  91.0 1.6 %copy-done = f32[8,16,32,128]{3,2,1,0:T(8,128)S(1)} copy-done((f32[8,16,32,128]{3,2,1,0:T(8,128)S(1)}, f32[8,16,32,128]{3,2,1,0:T(8,128)}, u32[]{:S(2)}) %copy-start) | copy-done | bytes 2097176
  92.5 15.5 %coarse_up.1 = (f32[16,32,128]{2,1,0:T(8,128)}, f32[16,32,128]{2,1,0:T(8,128)}) custom-call(s32[3]{0:T(128)S(1)} %pad_add_fusion.at, f32[8,32,128]{2,1,0:T(8,128)S(1)} %get-tuple-element.27.m0, f32[8,32,128]{2,1,0:T(8,128)S(1)} %collective-permute-done.6.m1, f32[8,32,128]{2,1,0:T(8,128)S(1)} %collective-permute-done.7.m2, ...), custom_call_target="tpu_custom_call" | custom-call | tf_op jit(solution)/shard_map/coarse_up/pallas_call | solution.py:55
  (16 shorter events, 1.7 us)
Async XLA Ops:
  0.6 1.0 copy-start.1
  1.6 0.9 copy-start.2
  3.1 11.0 %collective-permute-start = (f32[17,32,128]{2,1,0:T(8,128)S(1)}, f32[17,32,128]{2,1,0:T(8,128)S(1)}, u32[]{:S(2)}, u32[]{:S(2)}) collective-permute-start(f32[17,32,128]{2,1,0:T(8,128)S(1)} %get-tuple-element.20), channel_id=1, source_target_pairs={{0,32},{32,64},{64,96},{96,0},{1,33},{33,65},{65,97},{97,1},{2,34}... | collective-permute-start | bytes 835592 | tf_op jit(solution)/shard_map/ppermute | solution.py:655
  5.6 8.5 %collective-permute-start.1 = (f32[17,32,128]{2,1,0:T(8,128)S(1)}, f32[17,32,128]{2,1,0:T(8,128)S(1)}, u32[]{:S(2)}, u32[]{:S(2)}) collective-permute-start(f32[17,32,128]{2,1,0:T(8,128)S(1)} %get-tuple-element.21), channel_id=1, source_target_pairs={{32,0},{64,32},{96,64},{0,96},{33,1},{65,33},{97,65},{1,97},{34,2}... | collective-permute-start | bytes 835592 | tf_op jit(solution)/shard_map/ppermute | solution.py:654
  14.2 8.2 %collective-permute-start.2 = (f32[66,8,128]{2,1,0:T(8,128)S(1)}, f32[66,8,128]{2,1,0:T(8,128)S(1)}, u32[]{:S(2)}, u32[]{:S(2)}) collective-permute-start(f32[66,8,128]{2,1,0:T(8,128)S(1)} %get-tuple-element.22), channel_id=1, source_target_pairs={{0,8},{8,16},{16,24},{24,0},{1,9},{9,17},{17,25},{25,1},{2,10},{10... | collective-permute-start | bytes 811016 | tf_op jit(solution)/shard_map/ppermute | solution.py:655
  15.5 6.8 %collective-permute-start.3 = (f32[66,8,128]{2,1,0:T(8,128)S(1)}, f32[66,8,128]{2,1,0:T(8,128)S(1)}, u32[]{:S(2)}, u32[]{:S(2)}) collective-permute-start(f32[66,8,128]{2,1,0:T(8,128)S(1)} %get-tuple-element.23), channel_id=1, source_target_pairs={{8,0},{16,8},{24,16},{0,24},{9,1},{17,9},{25,17},{1,25},{10,2},{18... | collective-permute-start | bytes 811016 | tf_op jit(solution)/shard_map/ppermute | solution.py:654
  22.7 7.9 %collective-permute-start.4 = (f32[96,8,128]{2,1,0:T(8,128)S(1)}, f32[96,8,128]{2,1,0:T(8,128)S(1)}, u32[]{:S(2)}, u32[]{:S(2)}) collective-permute-start(f32[96,8,128]{2,1,0:T(8,128)S(1)} %get-tuple-element.24), channel_id=1, source_target_pairs={{0,1},{1,2},{2,3},{3,4},{4,5},{5,6},{6,7},{7,0},{8,9},{9,10},{10,1... | collective-permute-start | bytes 1179656 | tf_op jit(solution)/shard_map/ppermute | solution.py:655
  25.9 7.2 %collective-permute-start.5 = (f32[96,8,128]{2,1,0:T(8,128)S(1)}, f32[96,8,128]{2,1,0:T(8,128)S(1)}, u32[]{:S(2)}, u32[]{:S(2)}) collective-permute-start(f32[96,8,128]{2,1,0:T(8,128)S(1)} %get-tuple-element.25), channel_id=1, source_target_pairs={{1,0},{2,1},{3,2},{4,3},{5,4},{6,5},{7,6},{0,7},{9,8},{10,9},{11,1... | collective-permute-start | bytes 1179656 | tf_op jit(solution)/shard_map/ppermute | solution.py:654
  76.7 6.6 %collective-permute-start.8 = (f32[8,32,128]{2,1,0:T(8,128)S(1)}, f32[8,32,128]{2,1,0:T(8,128)S(1)}, u32[]{:S(2)}, u32[]{:S(2)}) collective-permute-start(f32[8,32,128]{2,1,0:T(8,128)S(1)} %get-tuple-element.27.m0), channel_id=1, source_target_pairs={{0,6},{1,7},{2,0},{3,1},{4,2},{5,3},{6,4},{7,5},{8,14},{9,15},{10,... | collective-permute-start | bytes 393224 | tf_op jit(solution)/shard_map/ppermute | solution.py:706
  79.7 6.6 %collective-permute-start.7 = (f32[8,32,128]{2,1,0:T(8,128)S(1)}, f32[8,32,128]{2,1,0:T(8,128)S(1)}, u32[]{:S(2)}, u32[]{:S(2)}) collective-permute-start(f32[8,32,128]{2,1,0:T(8,128)S(1)} %get-tuple-element.27.m0), channel_id=1, source_target_pairs={{0,4},{1,5},{2,6},{3,7},{4,0},{5,1},{6,2},{7,3},{8,12},{9,13},{10,... | collective-permute-start | bytes 393224 | tf_op jit(solution)/shard_map/ppermute | solution.py:706
  81.3 8.1 %collective-permute-start.6 = (f32[8,32,128]{2,1,0:T(8,128)S(1)}, f32[8,32,128]{2,1,0:T(8,128)S(1)}, u32[]{:S(2)}, u32[]{:S(2)}) collective-permute-start(f32[8,32,128]{2,1,0:T(8,128)S(1)} %get-tuple-element.27.m0), channel_id=1, source_target_pairs={{0,2},{1,3},{2,4},{3,5},{4,6},{5,7},{6,0},{7,1},{8,10},{9,11},{10,... | collective-permute-start | bytes 393224 | tf_op jit(solution)/shard_map/ppermute | solution.py:706
  82.0 7.9 %collective-permute-start.9 = (f32[8,32,128]{2,1,0:T(8,128)S(1)}, f32[8,32,128]{2,1,0:T(8,128)S(1)}, u32[]{:S(2)}, u32[]{:S(2)}) collective-permute-start(f32[8,32,128]{2,1,0:T(8,128)S(1)} %get-tuple-element.27.m0), channel_id=1, source_target_pairs={{0,1},{1,0},{2,3},{3,2},{4,5},{5,4},{6,7},{7,6},{8,9},{9,8},{10,11... | collective-permute-start | bytes 393224 | tf_op jit(solution)/shard_map/ppermute | solution.py:707
  83.3 6.7 %collective-permute-start.12 = (f32[8,32,128]{2,1,0:T(8,128)S(1)}, f32[8,32,128]{2,1,0:T(8,128)S(1)}, u32[]{:S(2)}, u32[]{:S(2)}) collective-permute-start(f32[8,32,128]{2,1,0:T(8,128)S(1)} %collective-permute-done.8.m3), channel_id=1, source_target_pairs={{0,1},{1,0},{2,3},{3,2},{4,5},{5,4},{6,7},{7,6},{8,9},{9,8},{10,11... | collective-permute-start | bytes 393224 | tf_op jit(solution)/shard_map/ppermute | solution.py:707
  86.3 3.7 %collective-permute-start.11 = (f32[8,32,128]{2,1,0:T(8,128)S(1)}, f32[8,32,128]{2,1,0:T(8,128)S(1)}, u32[]{:S(2)}, u32[]{:S(2)}) collective-permute-start(f32[8,32,128]{2,1,0:T(8,128)S(1)} %collective-permute-done.7.m2), channel_id=1, source_target_pairs={{0,1},{1,0},{2,3},{3,2},{4,5},{5,4},{6,7},{7,6},{8,9},{9,8},{10,11... | collective-permute-start | bytes 393224 | tf_op jit(solution)/shard_map/ppermute | solution.py:707
  89.3 1.6 %collective-permute-start.10 = (f32[8,32,128]{2,1,0:T(8,128)S(1)}, f32[8,32,128]{2,1,0:T(8,128)S(1)}, u32[]{:S(2)}, u32[]{:S(2)}) collective-permute-start(f32[8,32,128]{2,1,0:T(8,128)S(1)} %collective-permute-done.6.m1), channel_id=1, source_target_pairs={{0,1},{1,0},{2,3},{3,2},{4,5},{5,4},{6,7},{7,6},{8,9},{9,8},{10,11... | collective-permute-start | bytes 393224 | tf_op jit(solution)/shard_map/ppermute | solution.py:707
  91.0 1.6 %copy-start = (f32[8,16,32,128]{3,2,1,0:T(8,128)S(1)}, f32[8,16,32,128]{3,2,1,0:T(8,128)}, u32[]{:S(2)}) copy-start(f32[8,16,32,128]{3,2,1,0:T(8,128)} %get-tuple-element.29.c1b_in) | copy-start | bytes 6291460

commit v5 on v4

--- a/solution.py
+++ b/solution.py
@@ -13,7 +13,7 @@
 GROUP = 64
 LIMIT = 50
 LIMIT_MID = 50
-LIMIT_UP = 44
+LIMIT_UP = 50
 
 
 def lanes(rows):
@@ -67,7 +67,7 @@
     return jax.ShapeDtypeStruct(shape, F32)
 
 
-def split_fine(f_in, b_in, wf_ref, wb_ref, lo_ref, hi_ref, f_ref, b_ref, sems):
+def split_fine(f_in, b_in, wf_ref, wb_ref, lo_ref, hi_ref, b1_ref, f_ref, b_ref, tmp, sems):
     loads = [pltpu.make_async_copy(b_in, b_ref, sems.at[0]), pltpu.make_async_copy(f_in, f_ref, sems.at[1])]
     for c in loads:
         c.start()
@@ -77,13 +77,23 @@
         odd = (row + parity) % 2
         index.append(2 * (lane % 64) + jnp.where(lane < 64, odd, 1 - odd))
     loads[0].wait()
-    for i in range(16):
-        wb = pick(b_ref[i], index[i % 2])
-        wb_ref[i] = wb
-        if i < 9:
-            lo_ref[8 + i] = wb
-        if i > 6:
-            hi_ref[1 + i] = wb
+    lane16, row16 = lanes(16), sublanes(16)
+    own = []
+    for n in range(8):
+        w = [pick(b_ref[2 * n + parity], index[parity]) for parity in range(2)]
+        for parity in range(2):
+            i = 2 * n + parity
+            wb_ref[i] = w[parity]
+            if i < 9:
+                lo_ref[8 + i] = w[parity]
+            if i > 6:
+                hi_ref[1 + i] = w[parity]
+        both = w[0] + w[1]
+        odd = (row16 + n) % 2
+        cell = 2 * (lane16 % 32) + jnp.where(lane16 % 64 < 32, odd, 1 - odd)
+        own.append(pick(halve_rows(tmp, both + turn(both, 64), 32), cell))
+    for n in range(4):
+        b1_ref[16 * n : 16 * n + 16] = jnp.where(lane16 < 64, own[n], own[n + 4])
     loads[1].wait()
     for i in range(16):
         wf = pick(f_ref[i], index[i % 2])
@@ -112,7 +122,9 @@
     return xl.at[9 + p] if p < 8 else wb.at[p - 8] if p < 24 else xu.at[8 + p - 24]
 
 
-def pack_rows(wf, wb, xl, xu, lo_ref, hi_ref):
+def pack_rows(wf, wb, xl, xu, b0, b1, b2, b3, lo_ref, hi_ref, b1_ref):
+    for back, b in enumerate((b0, b1, b2, b3)):
+        b1_ref[back] = b[...]
     for p in range(32):
         f, b = plane_f(wf, xl, xu, p), plane_b(wb, xl, xu, p)
         lo_ref[p] = f[0:8]
@@ -299,10 +311,8 @@
     copies[2].start()
     inner = [side_rule(32, parity) for parity in range(2)]
     swap = gx >= 2
-    lane16, row16 = lanes(16), sublanes(16)
+    lane16 = lanes(16)
     spare = (lane16 % 64 >= 38) & (lane16 % 64 < 58)
-    odd16 = [(row16 + parity) % 2 for parity in range(2)]
-    own1 = {}
     for n in range(8):
         total = coarse = None
         for parity in range(2):
@@ -314,13 +324,8 @@
         f1 = pick(halve_rows(tmp, total, 32), by_colour(n, swap))
         b1 = halve_rows(tmp, coarse, 32)
         w1 = jnp.where(spare, pick(b1, spared(by_colour(n, swap))), f1)
-        own1[n] = pick(b1, 2 * (lane16 % 32) + jnp.where(lane16 % 64 < 32, odd16[n % 2], 1 - odd16[n % 2]))
         for copy in range(16):
             g_ref[copy, 16 * n : 16 * n + 16] = w1
-    for n in range(4):
-        w1 = jnp.where(lane16 < 64, own1[n], own1[n + 4])
-        for copy in range(16):
-            g_ref[copy, 128 + 16 * n : 144 + 16 * n] = w1
     for c in copies:
         c.wait()
 
@@ -336,12 +341,24 @@
     return jnp.where(half, wa, wb), turn(jnp.where(half, wb, wa), 64)
 
 
-def joined_b(g, p):
-    i = p % 8
-    wa, wb = (across(g, p // 8 + up, 128 + 16 * (i % 4)) for up in (0, 2))
+def across_b(gx, gy, held, a, n):
+    back = (gx - a + 4) % 4
+    r = slice(16 * n, 16 * n + 16)
+    out = []
+    for y in range(4):
+        e = (gy - y + 4) % 4
+        v = held[0][e, r]
+        for d in range(1, 4):
+            v = jnp.where(back == d, held[d][e, r], v)
+        out.append(v)
+    return jnp.concatenate(out, axis=0)
+
+
+def joined_b(gx, gy, held, a, n):
+    wa, wb = (across_b(gx, gy, held, a + up, n) for up in (0, 2))
     half = lanes(64) < 64
-    red = jnp.where(half, wa, turn(wb, 64)) if i < 4 else jnp.where(half, turn(wa, 64), wb)
-    return red, turn(red, -32)
+    reds = jnp.where(half, wa, turn(wb, 64)), jnp.where(half, turn(wa, 64), wb)
+    return [(red, turn(red, -32)) for red in reds]
 
 
 def seam(v, rows):
@@ -351,8 +368,8 @@
     v[17, r] = jnp.where(half, turn(v[1, r], 64), 0.0)
 
 
-def mid_down(at, g, w2_ref, cr_out, cb_out, vb_out, br, bb, fr, fb, cr, cb, vr, vb, tmp, sems):
-    gy, gz = at[1], at[2]
+def mid_down(at, g, h0, h1, h2, h3, w2_ref, c_out, vb_out, br, bb, fr, fb, cr, cb, vr, vb, tmp, sems):
+    gx, gy, gz = at[0], at[1], at[2]
     lane = lanes(64)
     own = lane % 64 < 32
     keep = own | ((lane % 64 < 48) & (gz < 7)) | ((lane % 64 >= 48) & (gz > 0))
@@ -365,9 +382,12 @@
         b[:, 72:80] = jnp.zeros((18, 8, 128), F32)
     for p in range(16):
         fr[p], fb[p] = joined_f(g, p)
-        red, black = joined_b(g, p)
-        br[p + 1, 8:72] = kept * jnp.where(own, red, pick(fr[p], halo))
-        bb[p + 1, 8:72] = kept * jnp.where(own, black, pick(fb[p], halo))
+    for a in range(2):
+        for n in range(4):
+            for up, (red, black) in enumerate(joined_b(gx, gy, (h0, h1, h2, h3), a, n)):
+                p = 8 * a + n + 4 * up
+                br[p + 1, 8:72] = kept * jnp.where(own, red, pick(fr[p], halo))
+                bb[p + 1, 8:72] = kept * jnp.where(own, black, pick(fb[p], halo))
     seam(br, 64)
     seam(bb, 64)
     index = [side_index(64, parity, 64) for parity in range(2)]
@@ -381,8 +401,8 @@
     seam(vr, 64)
     window = pl.multiple_of(jnp.clip(gy * 16 - 8, 0, 32), 8)
     copies = [
-        pltpu.make_async_copy(cr.at[:, :, pl.ds(window, 32)], cr_out, sems.at[0]),
-        pltpu.make_async_copy(cb.at[:, :, pl.ds(window, 32)], cb_out, sems.at[1]),
+        pltpu.make_async_copy(cr.at[:, :, pl.ds(window, 32)], c_out.at[0], sems.at[0]),
+        pltpu.make_async_copy(cb.at[:, :, pl.ds(window, 32)], c_out.at[1], sems.at[1]),
         pltpu.make_async_copy(vb.at[:, pl.ds(window + 8, 32)], vb_out, sems.at[2]),
     ]
     copies[0].start()
@@ -487,7 +507,7 @@
 
 
 def coarse_up(
-    at, m0, m1, m2, m3, q0, q1, q2, q3, c1r_in, c1b_in, v1b_in, c0r_in, c0b_in, v0b_in, u_ref, res_ref,
+    at, m0, m1, m2, m3, q0, q1, q2, q3, c1_in, v1b_in, c0r_in, c0b_in, v0b_in, u_ref, res_ref,
     b2r, b2b, v2r, v2b, c2r, c2b, f2,
     b3r, b3b, v3r, v3b, c3r, c3b, f3,
     b4r, b4b, v4r, v4b, c4r, c4b, f4,
@@ -495,8 +515,8 @@
 ):
     gx, gy, gz = at[0], at[1], at[2]
     copies = [
-        pltpu.make_async_copy(c1r_in, c1r, sems.at[0]),
-        pltpu.make_async_copy(c1b_in, c1b, sems.at[1]),
+        pltpu.make_async_copy(c1_in.at[0], c1r, sems.at[0]),
+        pltpu.make_async_copy(c1_in.at[1], c1b, sems.at[1]),
         pltpu.make_async_copy(v1b_in, v1b.at[:, pl.ds(8, 32)], sems.at[2]),
         pltpu.make_async_copy(c0r_in, c0r, sems.at[3]),
         pltpu.make_async_copy(c0b_in, c0b, sems.at[4]),
@@ -656,6 +676,11 @@
     return from_below, from_above
 
 
+def beyond(x, axis):
+    count = lax.axis_size(axis)
+    return [lax.ppermute(x, axis, [(i, (i + d) % count) for i in range(count)]) for d in range(1, count)]
+
+
 def body(source, conductance):
     vmem, smem, hbm = (pl.BlockSpec(memory_space=m) for m in (pltpu.VMEM, pltpu.SMEM, pltpu.HBM))
     at = jnp.stack([lax.axis_index(a) for a in ("gx", "gy", "gz")]).astype(jnp.int32)
@@ -663,17 +688,20 @@
 
     block, x_slab = arr(16, 32, 128), arr(17, 32, 128)
     buffer = pltpu.VMEM((16, 32, 128), F32)
-    wf, wb, lo, hi = call(
+    wf, wb, lo, hi, b1 = call(
         split_fine,
-        [(block, block, x_slab, x_slab)],
+        [(block, block, x_slab, x_slab, arr(64, 128))],
         (source, conductance),
         [hbm] * 2,
-        [buffer, buffer, dma((2,))],
+        [buffer, buffer, pltpu.VMEM((32, 128), F32), dma((2,))],
         8,
     )
     xl, xu = around(lo, hi, "gx")
-    lo, hi = call(pack_rows, [(arr(66, 8, 128),) * 2], (wf, wb, xl, xu), limit=8)
+    b1 = [b1] + beyond(b1, "gy")
+    y_slab = arr(66, 8, 128)
+    lo, hi, b1 = call(pack_rows, [(y_slab, y_slab, arr(4, 64, 128))], (wf, wb, xl, xu, *b1), limit=8)
     yl, yu = around(lo, hi, "gy")
+    b1 = [b1] + beyond(b1, "gx")
     lo, hi = call(pack_lanes, [(arr(96, 8, 128),) * 2], (wf, wb, xl, xu, yl, yu), limit=8)
     zl, zu = around(lo, hi, "gz")
 
@@ -683,7 +711,7 @@
     state0 = (arr(8, 24, 48, 128), arr(8, 24, 48, 128), arr(34, 64, 128))
     g, c0r, c0b, v0b = call(
         fine_down,
-        [(arr(16, 192, 128),) + state0, (vmem, hbm, hbm, hbm)],
+        [(arr(16, 128, 128),) + state0, (vmem, hbm, hbm, hbm)],
         (at, wf, wb, xl, xu, yl, yu, zl, zu),
         [smem] + [vmem] * 8,
         [colour0, colour0, right0, right0, coef0, coef0, colour0, colour0, pltpu.VMEM((32, 128), F32), dma((3,))],
@@ -691,15 +719,15 @@
     )
     g = lax.all_to_all(g, ("gx", "gy"), 0, 0, tiled=True)
 
-    state1 = (arr(8, 16, 32, 128), arr(8, 16, 32, 128), arr(18, 32, 128))
+    state1 = (arr(2, 8, 16, 32, 128), arr(18, 32, 128))
     colour1 = pltpu.VMEM((18, 80, 128), F32)
     right1 = pltpu.VMEM((16, 64, 128), F32)
     coef1 = pltpu.VMEM((8, 16, 64, 128), F32)
-    w2, c1r, c1b, v1b = call(
+    w2, c1, v1b = call(
         mid_down,
-        [(arr(8, 32, 128),) + state1, (vmem, hbm, hbm, hbm)],
-        (at, g),
-        [smem, vmem],
+        [(arr(8, 32, 128),) + state1, (vmem, hbm, hbm)],
+        (at, g, *b1),
+        [smem] + [vmem] * 5,
         [colour1, colour1, right1, right1, coef1, coef1, colour1, colour1, pltpu.VMEM((64, 128), F32), dma((3,))],
         LIMIT_MID,
     )
@@ -715,8 +743,8 @@
     return call(
         coarse_up,
         [(block, block)],
-        (at, *mine, *pair, c1r, c1b, v1b, c0r, c0b, v0b),
-        [smem] + [vmem] * 8 + [hbm] * 6,
+        (at, *mine, *pair, c1, v1b, c0r, c0b, v0b),
+        [smem] + [vmem] * 8 + [hbm] * 5,
         scratch,
         LIMIT_UP,
     )

time: 108 us -> 106 us (0.981)
  blocking collectives: 28.5 us -> 0 us
  waiting for transfers between devices: 20.9 us -> 34.6 us
  starting transfers between devices: 22.9 us -> 36.3 us
    all_to_all x1 -> x0, blocking collectives: 28.5 us -> none  [body(): g = lax.all_to_all(g, ('gx', 'gy'), 0, 0, tiled=True)]
    ppermute x0 -> x6, waiting for transfers between devices: none -> 21 us  [beyond(): lax.ppermute(x, axis, [(i, (i + d) % count) for i in range(count)])]
    ppermute x3, waiting for transfers between devices: 16.2 us -> 8.49 us  [around(): lax.ppermute(hi, axis, [(i, (i + 1) % count) for i in range(count)])]
    ppermute x0 -> x6, starting transfers between devices: none -> 7.51 us  [beyond(): lax.ppermute(x, axis, [(i, (i + d) % count) for i in range(count)])]
    all_to_all x0 -> x1, starting transfers between devices: none -> 5.67 us  [body(): g = lax.all_to_all(g, ('gx', 'gy'), 0, 0, tiled=True)]
    ppermute x3, starting transfers between devices: 5.35 us -> 3.48 us  [body(): lax.ppermute(w2, 'gz', [(i, (i + d) % 8) for i in range(8)])]
  transfers between devices with their start and end apart: 13 -> 20, of which waited for: 6 -> 11; matrix products, arithmetic and copies ran while one was open for 0% -> 0% of each run, Pallas kernels for 0% -> 0%
where the time goes in v5:
time: 106 us
  starting transfers between devices  36.3 us (34%)
  waiting for transfers between devices  34.6 us (33%)
  Pallas kernels  31.2 us (29%)
  local copies, waits for them, and re-layouts  3.14 us (3%)
    pallas_call x6, Pallas kernels, call(): pl.pallas_call(kernel, out_shape=out[0], in_specs=specs or [vmem] * len(a...  31.2 us
    ppermute x6, waiting for transfers between devices, beyond(): lax.ppermute(x, axis, [(i, (i + d) % count) for i in range(count)])  21 us
    ppermute x3, waiting for transfers between devices, around(): lax.ppermute(hi, axis, [(i, (i + 1) % count) for i in range(count)])  8.49 us
    ppermute x3, starting transfers between devices, around(): lax.ppermute(hi, axis, [(i, (i + 1) % count) for i in range(count)])  7.54 us
    ppermute x6, starting transfers between devices, beyond(): lax.ppermute(x, axis, [(i, (i + d) % count) for i in range(count)])  7.51 us
    ppermute x4, starting transfers between devices, body(): pair = [lax.ppermute(w, 'gz', [(i, i ^ 1) for i in range(8)]) for w in mine]  7.45 us
    all_to_all x1, starting transfers between devices, body(): g = lax.all_to_all(g, ('gx', 'gy'), 0, 0, tiled=True)  5.67 us
    ppermute x3, starting transfers between devices, around(): lax.ppermute(lo, axis, [((i + 1) % count, i) for i in range(count)])  4.64 us
  transfers between devices with their start and end apart: 20, of which 11 were waited for; matrix products, arithmetic and copies ran while one was open for 0% of the time, Pallas kernels for 0%

profile of v5, /device:TPU:1, one launch (start us, length us, event | category | flops | bytes accessed | tf_op | source)
XLA Modules:
  0.0 106.2 jit_solution(5469645784367916303)
XLA Ops:
  1.6 0.9 copy-done.2
  3.3 2.5 %collective-permute-start = (f32[17,32,128]{2,1,0:T(8,128)S(1)}, f32[17,32,128]{2,1,0:T(8,128)S(1)}, u32[]{:S(2)}, u32[]{:S(2)}) collective-permute-start(f32[17,32,128]{2,1,0:T(8,128)S(1)} %get-tuple-element.21), channel_id=1, source_target_pairs={{0,32},{32,64},{64,96},{96,0},{1,33},{33,65},{65,97},{97,1},{2,34}... | collective-permute-start | bytes 835592 | tf_op jit(solution)/shard_map/ppermute | solution.py:675
  5.8 2.2 %collective-permute-start.1 = (f32[17,32,128]{2,1,0:T(8,128)S(1)}, f32[17,32,128]{2,1,0:T(8,128)S(1)}, u32[]{:S(2)}, u32[]{:S(2)}) collective-permute-start(f32[17,32,128]{2,1,0:T(8,128)S(1)} %get-tuple-element.22), channel_id=1, source_target_pairs={{32,0},{64,32},{96,64},{0,96},{33,1},{65,33},{97,65},{1,97},{34,2}... | collective-permute-start | bytes 835592 | tf_op jit(solution)/shard_map/ppermute | solution.py:674
  8.0 2.7 %collective-permute-start.4 = (f32[64,128]{1,0:T(8,128)S(1)}, f32[64,128]{1,0:T(8,128)S(1)}, u32[]{:S(2)}, u32[]{:S(2)}) collective-permute-start(f32[64,128]{1,0:T(8,128)S(1)} %get-tuple-element.23.b0), channel_id=1, source_target_pairs={{0,24},{8,0},{16,8},{24,16},{1,25},{9,1},{17,9},{25,17},{2,26},{10... | collective-permute-start | bytes 98312 | tf_op jit(solution)/shard_map/ppermute | solution.py:681
  11.8 3.3 %collective-permute-done.3.b2 = f32[64,128]{1,0:T(8,128)S(1)} collective-permute-done((f32[64,128]{1,0:T(8,128)S(1)}, f32[64,128]{1,0:T(8,128)S(1)}, u32[]{:S(2)}, u32[]{:S(2)}) %collective-permute-start.3) | collective-permute-done | bytes 32800 | tf_op jit(solution)/shard_map/ppermute | solution.py:681
  15.7 2.4 %collective-permute-start.6 = (f32[66,8,128]{2,1,0:T(8,128)S(1)}, f32[66,8,128]{2,1,0:T(8,128)S(1)}, u32[]{:S(2)}, u32[]{:S(2)}) collective-permute-start(f32[66,8,128]{2,1,0:T(8,128)S(1)} %get-tuple-element.25), channel_id=1, source_target_pairs={{8,0},{16,8},{24,16},{0,24},{9,1},{17,9},{25,17},{1,25},{10,2},{18... | collective-permute-start | bytes 811016 | tf_op jit(solution)/shard_map/ppermute | solution.py:674
  18.2 3.8 %collective-permute-done.5.yl = f32[66,8,128]{2,1,0:T(8,128)S(1)} collective-permute-done((f32[66,8,128]{2,1,0:T(8,128)S(1)}, f32[66,8,128]{2,1,0:T(8,128)S(1)}, u32[]{:S(2)}, u32[]{:S(2)}) %collective-permute-start.5) | collective-permute-done | bytes 270368 | tf_op jit(solution)/shard_map/ppermute | solution.py:675
  22.4 4.7 %collective-permute-start.7 = (f32[96,8,128]{2,1,0:T(8,128)S(1)}, f32[96,8,128]{2,1,0:T(8,128)S(1)}, u32[]{:S(2)}, u32[]{:S(2)}) collective-permute-start(f32[96,8,128]{2,1,0:T(8,128)S(1)} %get-tuple-element.26), channel_id=1, source_target_pairs={{0,1},{1,2},{2,3},{3,4},{4,5},{5,6},{6,7},{7,0},{8,9},{9,10},{10,1... | collective-permute-start | bytes 1179656 | tf_op jit(solution)/shard_map/ppermute | solution.py:675
  27.2 4.6 %collective-permute-done.7.zl = f32[96,8,128]{2,1,0:T(8,128)S(1)} collective-permute-done((f32[96,8,128]{2,1,0:T(8,128)S(1)}, f32[96,8,128]{2,1,0:T(8,128)S(1)}, u32[]{:S(2)}, u32[]{:S(2)}) %collective-permute-start.7) | collective-permute-done | bytes 393248 | tf_op jit(solution)/shard_map/ppermute | solution.py:675
  31.8 2.5 %collective-permute-done.8.zu = f32[96,8,128]{2,1,0:T(8,128)S(1)} collective-permute-done((f32[96,8,128]{2,1,0:T(8,128)S(1)}, f32[96,8,128]{2,1,0:T(8,128)S(1)}, u32[]{:S(2)}, u32[]{:S(2)}) %collective-permute-start.8) | collective-permute-done | bytes 393248 | tf_op jit(solution)/shard_map/ppermute | solution.py:674
  34.3 8.5 %fine_down.1 = (f32[16,128,128]{2,1,0:T(8,128)}, f32[8,24,48,128]{3,2,1,0:T(8,128)}, f32[8,24,48,128]{3,2,1,0:T(8,128)}, f32[34,64,128]{2,1,0:T(8,128)}) custom-call(s32[3]{0:T(128)S(1)} %pad_add_fusion.at, f32[16,32,128]{2,1,0:T(8,128)S(1)} %get-tuple-element.19.wf, f32[16,32,128]{2,1,0:T(8,128)S(1)} %get-tuple-element.20.wb, ...), custom_call_target="tpu_custom_call" | custom-call | tf_op jit(solution)/shard_map/fine_down/pallas_call | solution.py:55
  42.8 5.7 %all-to-all-start = ((f32[16,128,128]{2,1,0:T(8,128)}), f32[16,128,128]{2,1,0:T(8,128)S(1)}, u32[]{:S(2)}, u32[]{:S(2)}) async-start(f32[16,128,128]{2,1,0:T(8,128)} %get-tuple-element.28), calls=%async_computation | async-start | bytes 2097152 | tf_op jit(solution)/shard_map/all_to_all | solution.py:720
  48.5 2.6 %collective-permute-start.11 = (f32[4,64,128]{2,1,0:T(8,128)S(1)}, f32[4,64,128]{2,1,0:T(8,128)S(1)}, u32[]{:S(2)}, u32[]{:S(2)}) collective-permute-start(f32[4,64,128]{2,1,0:T(8,128)S(1)} %get-tuple-element.29.h0), channel_id=1, source_target_pairs={{0,96},{32,0},{64,32},{96,64},{1,97},{33,1},{65,33},{97,65},{2,98}... | collective-permute-start | bytes 393224 | tf_op jit(solution)/shard_map/ppermute | solution.py:681
  52.2 12.2 %collective-permute-done.11.h3 = f32[4,64,128]{2,1,0:T(8,128)S(1)} collective-permute-done((f32[4,64,128]{2,1,0:T(8,128)S(1)}, f32[4,64,128]{2,1,0:T(8,128)S(1)}, u32[]{:S(2)}, u32[]{:S(2)}) %collective-permute-start.11) | collective-permute-done | bytes 131104 | tf_op jit(solution)/shard_map/ppermute | solution.py:681
  65.4 4.2 %collective-permute-done.9.h1 = f32[4,64,128]{2,1,0:T(8,128)S(1)} collective-permute-done((f32[4,64,128]{2,1,0:T(8,128)S(1)}, f32[4,64,128]{2,1,0:T(8,128)S(1)}, u32[]{:S(2)}, u32[]{:S(2)}) %collective-permute-start.9) | collective-permute-done | bytes 131104 | tf_op jit(solution)/shard_map/ppermute | solution.py:681
  69.6 6.3 %mid_down.1 = (f32[8,32,128]{2,1,0:T(8,128)S(1)}, f32[2,8,16,32,128]{4,3,2,1,0:T(8,128)}, f32[18,32,128]{2,1,0:T(8,128)S(1)}) custom-call(s32[3]{0:T(128)S(1)} %pad_add_fusion.at, f32[16,128,128]{2,1,0:T(8,128)S(1)} %all-to-all-done.g, f32[4,64,128]{2,1,0:T(8,128)S(1)} %get-tuple-element.29.h0, f32[4,64,128]{2,1,0:T(8,128)S(1)} %collective-permute-done.9.h1, ...), custom_call_target="tpu_custom_call" | custom-call | tf_op jit(solution)/shard_map/mid_down/pallas_call | solution.py:55
  76.0 2.4 %collective-permute-start.14 = (f32[8,32,128]{2,1,0:T(8,128)S(1)}, f32[8,32,128]{2,1,0:T(8,128)S(1)}, u32[]{:S(2)}, u32[]{:S(2)}) collective-permute-start(f32[8,32,128]{2,1,0:T(8,128)S(1)} %get-tuple-element.30.m0), channel_id=1, source_target_pairs={{0,6},{1,7},{2,0},{3,1},{4,2},{5,3},{6,4},{7,5},{8,14},{9,15},{10,... | collective-permute-start | bytes 393224 | tf_op jit(solution)/shard_map/ppermute | solution.py:734
  79.4 1.3 %collective-permute-start.15 = (f32[8,32,128]{2,1,0:T(8,128)S(1)}, f32[8,32,128]{2,1,0:T(8,128)S(1)}, u32[]{:S(2)}, u32[]{:S(2)}) collective-permute-start(f32[8,32,128]{2,1,0:T(8,128)S(1)} %get-tuple-element.30.m0), channel_id=1, source_target_pairs={{0,1},{1,0},{2,3},{3,2},{4,5},{5,4},{6,7},{7,6},{8,9},{9,8},{10,11... | collective-permute-start | bytes 393224 | tf_op jit(solution)/shard_map/ppermute | solution.py:735
  81.3 3.6 %collective-permute-start.18 = (f32[8,32,128]{2,1,0:T(8,128)S(1)}, f32[8,32,128]{2,1,0:T(8,128)S(1)}, u32[]{:S(2)}, u32[]{:S(2)}) collective-permute-start(f32[8,32,128]{2,1,0:T(8,128)S(1)} %collective-permute-done.14.m3), channel_id=1, source_target_pairs={{0,1},{1,0},{2,3},{3,2},{4,5},{5,4},{6,7},{7,6},{8,9},{9,8},{10,11... | collective-permute-start | bytes 393224 | tf_op jit(solution)/shard_map/ppermute | solution.py:735
  84.9 2.0 %collective-permute-start.17 = (f32[8,32,128]{2,1,0:T(8,128)S(1)}, f32[8,32,128]{2,1,0:T(8,128)S(1)}, u32[]{:S(2)}, u32[]{:S(2)}) collective-permute-start(f32[8,32,128]{2,1,0:T(8,128)S(1)} %collective-permute-done.13.m2), channel_id=1, source_target_pairs={{0,1},{1,0},{2,3},{3,2},{4,5},{5,4},{6,7},{7,6},{8,9},{9,8},{10,11... | collective-permute-start | bytes 393224 | tf_op jit(solution)/shard_map/ppermute | solution.py:735
  87.0 1.1 %collective-permute-done.12.m1 = f32[8,32,128]{2,1,0:T(8,128)S(1)} collective-permute-done((f32[8,32,128]{2,1,0:T(8,128)S(1)}, f32[8,32,128]{2,1,0:T(8,128)S(1)}, u32[]{:S(2)}, u32[]{:S(2)}) %collective-permute-start.12) | collective-permute-done | bytes 131104 | tf_op jit(solution)/shard_map/ppermute | solution.py:734
  88.6 1.0 collective-permute-done.16.q1
  89.6 1.2 %copy-done = f32[34,64,128]{2,1,0:T(8,128)S(1)} copy-done((f32[34,64,128]{2,1,0:T(8,128)S(1)}, f32[34,64,128]{2,1,0:T(8,128)}, u32[]{:S(2)}) %copy-start) | copy-done | bytes 1114136
  90.8 15.2 %coarse_up.1 = (f32[16,32,128]{2,1,0:T(8,128)}, f32[16,32,128]{2,1,0:T(8,128)}) custom-call(s32[3]{0:T(128)S(1)} %pad_add_fusion.at, f32[8,32,128]{2,1,0:T(8,128)S(1)} %get-tuple-element.30.m0, f32[8,32,128]{2,1,0:T(8,128)S(1)} %collective-permute-done.12.m1, f32[8,32,128]{2,1,0:T(8,128)S(1)} %collective-permute-done.13.m2, ...), custom_call_target="tpu_custom_call" | custom-call | tf_op jit(solution)/shard_map/coarse_up/pallas_call | solution.py:55
  (29 shorter events, 8.1 us)
Async XLA Ops:
  0.6 1.0 copy-start.1
  1.6 0.9 copy-start.2
  3.3 12.1 %collective-permute-start = (f32[17,32,128]{2,1,0:T(8,128)S(1)}, f32[17,32,128]{2,1,0:T(8,128)S(1)}, u32[]{:S(2)}, u32[]{:S(2)}) collective-permute-start(f32[17,32,128]{2,1,0:T(8,128)S(1)} %get-tuple-element.21), channel_id=1, source_target_pairs={{0,32},{32,64},{64,96},{96,0},{1,33},{33,65},{65,97},{97,1},{2,34}... | collective-permute-start | bytes 835592 | tf_op jit(solution)/shard_map/ppermute | solution.py:675
  5.8 9.6 %collective-permute-start.1 = (f32[17,32,128]{2,1,0:T(8,128)S(1)}, f32[17,32,128]{2,1,0:T(8,128)S(1)}, u32[]{:S(2)}, u32[]{:S(2)}) collective-permute-start(f32[17,32,128]{2,1,0:T(8,128)S(1)} %get-tuple-element.22), channel_id=1, source_target_pairs={{32,0},{64,32},{96,64},{0,96},{33,1},{65,33},{97,65},{1,97},{34,2}... | collective-permute-start | bytes 835592 | tf_op jit(solution)/shard_map/ppermute | solution.py:674
  8.0 3.8 %collective-permute-start.4 = (f32[64,128]{1,0:T(8,128)S(1)}, f32[64,128]{1,0:T(8,128)S(1)}, u32[]{:S(2)}, u32[]{:S(2)}) collective-permute-start(f32[64,128]{1,0:T(8,128)S(1)} %get-tuple-element.23.b0), channel_id=1, source_target_pairs={{0,24},{8,0},{16,8},{24,16},{1,25},{9,1},{17,9},{25,17},{2,26},{10... | collective-permute-start | bytes 98312 | tf_op jit(solution)/shard_map/ppermute | solution.py:681
  10.7 4.3 %collective-permute-start.3 = (f32[64,128]{1,0:T(8,128)S(1)}, f32[64,128]{1,0:T(8,128)S(1)}, u32[]{:S(2)}, u32[]{:S(2)}) collective-permute-start(f32[64,128]{1,0:T(8,128)S(1)} %get-tuple-element.23.b0), channel_id=1, source_target_pairs={{0,16},{8,24},{16,0},{24,8},{1,17},{9,25},{17,1},{25,9},{2,18},{10... | collective-permute-start | bytes 98312 | tf_op jit(solution)/shard_map/ppermute | solution.py:681
  11.1 4.3 %collective-permute-start.2 = (f32[64,128]{1,0:T(8,128)S(1)}, f32[64,128]{1,0:T(8,128)S(1)}, u32[]{:S(2)}, u32[]{:S(2)}) collective-permute-start(f32[64,128]{1,0:T(8,128)S(1)} %get-tuple-element.23.b0), channel_id=1, source_target_pairs={{0,8},{8,16},{16,24},{24,0},{1,9},{9,17},{17,25},{25,1},{2,10},{10... | collective-permute-start | bytes 98312 | tf_op jit(solution)/shard_map/ppermute | solution.py:681
  15.4 6.6 %collective-permute-start.5 = (f32[66,8,128]{2,1,0:T(8,128)S(1)}, f32[66,8,128]{2,1,0:T(8,128)S(1)}, u32[]{:S(2)}, u32[]{:S(2)}) collective-permute-start(f32[66,8,128]{2,1,0:T(8,128)S(1)} %get-tuple-element.24), channel_id=1, source_target_pairs={{0,8},{8,16},{16,24},{24,0},{1,9},{9,17},{17,25},{25,1},{2,10},{10... | collective-permute-start | bytes 811016 | tf_op jit(solution)/shard_map/ppermute | solution.py:675
  15.7 6.3 %collective-permute-start.6 = (f32[66,8,128]{2,1,0:T(8,128)S(1)}, f32[66,8,128]{2,1,0:T(8,128)S(1)}, u32[]{:S(2)}, u32[]{:S(2)}) collective-permute-start(f32[66,8,128]{2,1,0:T(8,128)S(1)} %get-tuple-element.25), channel_id=1, source_target_pairs={{8,0},{16,8},{24,16},{0,24},{9,1},{17,9},{25,17},{1,25},{10,2},{18... | collective-permute-start | bytes 811016 | tf_op jit(solution)/shard_map/ppermute | solution.py:674
  22.4 9.4 %collective-permute-start.7 = (f32[96,8,128]{2,1,0:T(8,128)S(1)}, f32[96,8,128]{2,1,0:T(8,128)S(1)}, u32[]{:S(2)}, u32[]{:S(2)}) collective-permute-start(f32[96,8,128]{2,1,0:T(8,128)S(1)} %get-tuple-element.26), channel_id=1, source_target_pairs={{0,1},{1,2},{2,3},{3,4},{4,5},{5,6},{6,7},{7,0},{8,9},{9,10},{10,1... | collective-permute-start | bytes 1179656 | tf_op jit(solution)/shard_map/ppermute | solution.py:675
  27.1 7.2 %collective-permute-start.8 = (f32[96,8,128]{2,1,0:T(8,128)S(1)}, f32[96,8,128]{2,1,0:T(8,128)S(1)}, u32[]{:S(2)}, u32[]{:S(2)}) collective-permute-start(f32[96,8,128]{2,1,0:T(8,128)S(1)} %get-tuple-element.27), channel_id=1, source_target_pairs={{1,0},{2,1},{3,2},{4,3},{5,4},{6,5},{7,6},{0,7},{9,8},{10,9},{11,1... | collective-permute-start | bytes 1179656 | tf_op jit(solution)/shard_map/ppermute | solution.py:674
  42.8 26.8 %all-to-all-start = ((f32[16,128,128]{2,1,0:T(8,128)}), f32[16,128,128]{2,1,0:T(8,128)S(1)}, u32[]{:S(2)}, u32[]{:S(2)}) async-start(f32[16,128,128]{2,1,0:T(8,128)} %get-tuple-element.28), calls=%async_computation | async-start | bytes 2097152 | tf_op jit(solution)/shard_map/all_to_all | solution.py:720
  48.5 16.0 %collective-permute-start.11 = (f32[4,64,128]{2,1,0:T(8,128)S(1)}, f32[4,64,128]{2,1,0:T(8,128)S(1)}, u32[]{:S(2)}, u32[]{:S(2)}) collective-permute-start(f32[4,64,128]{2,1,0:T(8,128)S(1)} %get-tuple-element.29.h0), channel_id=1, source_target_pairs={{0,96},{32,0},{64,32},{96,64},{1,97},{33,1},{65,33},{97,65},{2,98}... | collective-permute-start | bytes 393224 | tf_op jit(solution)/shard_map/ppermute | solution.py:681
  51.1 14.3 %collective-permute-start.10 = (f32[4,64,128]{2,1,0:T(8,128)S(1)}, f32[4,64,128]{2,1,0:T(8,128)S(1)}, u32[]{:S(2)}, u32[]{:S(2)}) collective-permute-start(f32[4,64,128]{2,1,0:T(8,128)S(1)} %get-tuple-element.29.h0), channel_id=1, source_target_pairs={{0,64},{32,96},{64,0},{96,32},{1,65},{33,97},{65,1},{97,33},{2,66}... | collective-permute-start | bytes 393224 | tf_op jit(solution)/shard_map/ppermute | solution.py:681
  51.6 18.0 %collective-permute-start.9 = (f32[4,64,128]{2,1,0:T(8,128)S(1)}, f32[4,64,128]{2,1,0:T(8,128)S(1)}, u32[]{:S(2)}, u32[]{:S(2)}) collective-permute-start(f32[4,64,128]{2,1,0:T(8,128)S(1)} %get-tuple-element.29.h0), channel_id=1, source_target_pairs={{0,32},{32,64},{64,96},{96,0},{1,33},{33,65},{65,97},{97,1},{2,34}... | collective-permute-start | bytes 393224 | tf_op jit(solution)/shard_map/ppermute | solution.py:681
  76.0 5.4 %collective-permute-start.14 = (f32[8,32,128]{2,1,0:T(8,128)S(1)}, f32[8,32,128]{2,1,0:T(8,128)S(1)}, u32[]{:S(2)}, u32[]{:S(2)}) collective-permute-start(f32[8,32,128]{2,1,0:T(8,128)S(1)} %get-tuple-element.30.m0), channel_id=1, source_target_pairs={{0,6},{1,7},{2,0},{3,1},{4,2},{5,3},{6,4},{7,5},{8,14},{9,15},{10,... | collective-permute-start | bytes 393224 | tf_op jit(solution)/shard_map/ppermute | solution.py:734
  78.4 6.6 %collective-permute-start.13 = (f32[8,32,128]{2,1,0:T(8,128)S(1)}, f32[8,32,128]{2,1,0:T(8,128)S(1)}, u32[]{:S(2)}, u32[]{:S(2)}) collective-permute-start(f32[8,32,128]{2,1,0:T(8,128)S(1)} %get-tuple-element.30.m0), channel_id=1, source_target_pairs={{0,4},{1,5},{2,6},{3,7},{4,0},{5,1},{6,2},{7,3},{8,12},{9,13},{10,... | collective-permute-start | bytes 393224 | tf_op jit(solution)/shard_map/ppermute | solution.py:734
  78.9 9.2 %collective-permute-start.12 = (f32[8,32,128]{2,1,0:T(8,128)S(1)}, f32[8,32,128]{2,1,0:T(8,128)S(1)}, u32[]{:S(2)}, u32[]{:S(2)}) collective-permute-start(f32[8,32,128]{2,1,0:T(8,128)S(1)} %get-tuple-element.30.m0), channel_id=1, source_target_pairs={{0,2},{1,3},{2,4},{3,5},{4,6},{5,7},{6,0},{7,1},{8,10},{9,11},{10,... | collective-permute-start | bytes 393224 | tf_op jit(solution)/shard_map/ppermute | solution.py:734
  79.4 9.2 %collective-permute-start.15 = (f32[8,32,128]{2,1,0:T(8,128)S(1)}, f32[8,32,128]{2,1,0:T(8,128)S(1)}, u32[]{:S(2)}, u32[]{:S(2)}) collective-permute-start(f32[8,32,128]{2,1,0:T(8,128)S(1)} %get-tuple-element.30.m0), channel_id=1, source_target_pairs={{0,1},{1,0},{2,3},{3,2},{4,5},{5,4},{6,7},{7,6},{8,9},{9,8},{10,11... | collective-permute-start | bytes 393224 | tf_op jit(solution)/shard_map/ppermute | solution.py:735
  81.3 7.3 %collective-permute-start.18 = (f32[8,32,128]{2,1,0:T(8,128)S(1)}, f32[8,32,128]{2,1,0:T(8,128)S(1)}, u32[]{:S(2)}, u32[]{:S(2)}) collective-permute-start(f32[8,32,128]{2,1,0:T(8,128)S(1)} %collective-permute-done.14.m3), channel_id=1, source_target_pairs={{0,1},{1,0},{2,3},{3,2},{4,5},{5,4},{6,7},{7,6},{8,9},{9,8},{10,11... | collective-permute-start | bytes 393224 | tf_op jit(solution)/shard_map/ppermute | solution.py:735
  84.9 3.7 %collective-permute-start.17 = (f32[8,32,128]{2,1,0:T(8,128)S(1)}, f32[8,32,128]{2,1,0:T(8,128)S(1)}, u32[]{:S(2)}, u32[]{:S(2)}) collective-permute-start(f32[8,32,128]{2,1,0:T(8,128)S(1)} %collective-permute-done.13.m2), channel_id=1, source_target_pairs={{0,1},{1,0},{2,3},{3,2},{4,5},{5,4},{6,7},{7,6},{8,9},{9,8},{10,11... | collective-permute-start | bytes 393224 | tf_op jit(solution)/shard_map/ppermute | solution.py:735
  88.1 1.5 %collective-permute-start.16 = (f32[8,32,128]{2,1,0:T(8,128)S(1)}, f32[8,32,128]{2,1,0:T(8,128)S(1)}, u32[]{:S(2)}, u32[]{:S(2)}) collective-permute-start(f32[8,32,128]{2,1,0:T(8,128)S(1)} %collective-permute-done.12.m1), channel_id=1, source_target_pairs={{0,1},{1,0},{2,3},{3,2},{4,5},{5,4},{6,7},{7,6},{8,9},{9,8},{10,11... | collective-permute-start | bytes 393224 | tf_op jit(solution)/shard_map/ppermute | solution.py:735
  89.6 1.2 %copy-start = (f32[34,64,128]{2,1,0:T(8,128)S(1)}, f32[34,64,128]{2,1,0:T(8,128)}, u32[]{:S(2)}) copy-start(f32[34,64,128]{2,1,0:T(8,128)} %get-tuple-element.35.v0b_in) | copy-start | bytes 3342340

commit v6 on v5

--- a/solution.py
+++ b/solution.py
@@ -238,7 +238,7 @@
 
 
 def fine_down(
-    at, wf, wb, xl, xu, yl, yu, zl, zu, g_ref, cr_out, cb_out, vb_out, br, bb, fr, fb, cr, cb, vr, vb, tmp, sems
+    at, wf, wb, xl, xu, yl, yu, zl, zu, g_ref, cr_out, cb_out, br, bb, fr, fb, cr, cb, vr, vb, tmp, sems
 ):
     gx, gy, gz = at[0], at[1], at[2]
     lane, row = lanes(48), sublanes(48)
@@ -300,8 +300,8 @@
     pairs(0, 32, coefs, 48)
     copies = [
         pltpu.make_async_copy(cr.at[:, pl.ds(4, 24)], cr_out, sems.at[0]),
-        pltpu.make_async_copy(cb.at[:, pl.ds(4, 24)], cb_out, sems.at[1]),
-        pltpu.make_async_copy(vb, vb_out, sems.at[2]),
+        pltpu.make_async_copy(cb.at[:, pl.ds(3, 26)], cb_out.at[pl.ds(0, 8)], sems.at[1]),
+        pltpu.make_async_copy(vb.at[pl.ds(4, 26), pl.ds(8, 48)], cb_out.at[8], sems.at[2]),
     ]
     copies[0].start()
     copies[1].start()
@@ -507,7 +507,7 @@
 
 
 def coarse_up(
-    at, m0, m1, m2, m3, q0, q1, q2, q3, c1_in, v1b_in, c0r_in, c0b_in, v0b_in, u_ref, res_ref,
+    at, m0, m1, m2, m3, q0, q1, q2, q3, c1_in, v1b_in, c0r_in, c0b_in, u_ref, res_ref,
     b2r, b2b, v2r, v2b, c2r, c2b, f2,
     b3r, b3b, v3r, v3b, c3r, c3b, f3,
     b4r, b4b, v4r, v4b, c4r, c4b, f4,
@@ -519,12 +519,14 @@
         pltpu.make_async_copy(c1_in.at[1], c1b, sems.at[1]),
         pltpu.make_async_copy(v1b_in, v1b.at[:, pl.ds(8, 32)], sems.at[2]),
         pltpu.make_async_copy(c0r_in, c0r, sems.at[3]),
-        pltpu.make_async_copy(c0b_in, c0b, sems.at[4]),
-        pltpu.make_async_copy(v0b_in, v0b, sems.at[5]),
+        pltpu.make_async_copy(c0b_in.at[pl.ds(0, 8), pl.ds(1, 24)], c0b, sems.at[4]),
+        pltpu.make_async_copy(c0b_in.at[8], v0b.at[pl.ds(4, 26), pl.ds(8, 48)], sems.at[5]),
     ]
     for c in copies:
         c.start()
     clear((b2r, b2b, v2r, v2b, b3r, b3b, v3r, v3b, b4r, b4b, v4r, v4b, v1r, v0r))
+    v0b[:, 0:8] = jnp.zeros((34, 8, 128), F32)
+    v0b[:, 56:64] = jnp.zeros((34, 8, 128), F32)
     v1b[:, 0:8] = jnp.zeros((18, 8, 128), F32)
     v1b[:, 40:48] = jnp.zeros((18, 8, 128), F32)
 
@@ -705,13 +707,15 @@
     lo, hi = call(pack_lanes, [(arr(96, 8, 128),) * 2], (wf, wb, xl, xu, yl, yu), limit=8)
     zl, zu = around(lo, hi, "gz")
 
+    zl, zu, *b1 = lax.optimization_barrier((zl, zu, *b1))
+
     colour0 = pltpu.VMEM((34, 64, 128), F32)
     right0 = pltpu.VMEM((32, 48, 128), F32)
     coef0 = pltpu.VMEM((8, 32, 48, 128), F32)
-    state0 = (arr(8, 24, 48, 128), arr(8, 24, 48, 128), arr(34, 64, 128))
-    g, c0r, c0b, v0b = call(
+    state0 = (arr(8, 24, 48, 128), arr(9, 26, 48, 128))
+    g, c0r, c0b = call(
         fine_down,
-        [(arr(16, 128, 128),) + state0, (vmem, hbm, hbm, hbm)],
+        [(arr(16, 128, 128),) + state0, (vmem, hbm, hbm)],
         (at, wf, wb, xl, xu, yl, yu, zl, zu),
         [smem] + [vmem] * 8,
         [colour0, colour0, right0, right0, coef0, coef0, colour0, colour0, pltpu.VMEM((32, 128), F32), dma((3,))],
@@ -743,8 +747,8 @@
     return call(
         coarse_up,
         [(block, block)],
-        (at, *mine, *pair, c1, v1b, c0r, c0b, v0b),
-        [smem] + [vmem] * 8 + [hbm] * 5,
+        (at, *mine, *pair, c1, v1b, c0r, c0b),
+        [smem] + [vmem] * 8 + [hbm] * 4,
         scratch,
         LIMIT_UP,
     )

time: 106 us -> 101 us (0.953)
  waiting for transfers between devices: 34.6 us -> 14.6 us
  blocking collectives: 0 us -> 19.1 us
  starting transfers between devices: 36.3 us -> 33.5 us
  local copies, waits for them, and re-layouts: 3.14 us -> 1.89 us
    all_to_all x0 -> x1, blocking collectives: none -> 19.1 us  [body(): g = lax.all_to_all(g, ('gx', 'gy'), 0, 0, tiled=True)]
    ppermute x6, waiting for transfers between devices: 21 us -> 9.74 us  [beyond(): lax.ppermute(x, axis, [(i, (i + d) % count) for i in range(count)])]
    all_to_all x1 -> x0, starting transfers between devices: 5.67 us -> none  [body(): g = lax.all_to_all(g, ('gx', 'gy'), 0, 0, tiled=True)]
    ppermute x3, waiting for transfers between devices: 8.49 us -> 3.85 us  [around(): lax.ppermute(hi, axis, [(i, (i + 1) % count) for i in range(count)])]
    ppermute x3, starting transfers between devices: 3.48 us -> 6.48 us  [body(): lax.ppermute(w2, 'gz', [(i, (i + d) % 8) for i in range(8)])]
    ppermute x3, waiting for transfers between devices: 2.49 us -> 0.01 us  [around(): lax.ppermute(lo, axis, [((i + 1) % count, i) for i in range(count)])]
    ppermute x3, waiting for transfers between devices: 1.7 us -> 0.01 us  [body(): lax.ppermute(w2, 'gz', [(i, (i + d) % 8) for i in range(8)])]
    ppermute x6, starting transfers between devices: 7.51 us -> 6.09 us  [beyond(): lax.ppermute(x, axis, [(i, (i + d) % count) for i in range(count)])]
  transfers between devices with their start and end apart: 20 -> 19, of which waited for: 11 -> 7; matrix products, arithmetic and copies ran while one was open for 0% -> 0% of each run, Pallas kernels for 0% -> 0%
where the time goes in v6:
time: 101 us
  starting transfers between devices  33.5 us (33%)
  Pallas kernels  30.7 us (30%)
  blocking collectives  19.1 us (19%)
  waiting for transfers between devices  14.6 us (14%)
  local copies, waits for them, and re-layouts  1.89 us (2%)
    pallas_call x6, Pallas kernels, call(): pl.pallas_call(kernel, out_shape=out[0], in_specs=specs or [vmem] * len(a...  30.7 us
    all_to_all x1, blocking collectives, body(): g = lax.all_to_all(g, ('gx', 'gy'), 0, 0, tiled=True)  19.1 us
    ppermute x6, waiting for transfers between devices, beyond(): lax.ppermute(x, axis, [(i, (i + d) % count) for i in range(count)])  9.74 us
    ppermute x4, starting transfers between devices, body(): pair = [lax.ppermute(w, 'gz', [(i, i ^ 1) for i in range(8)]) for w in mine]  8.77 us
    ppermute x3, starting transfers between devices, around(): lax.ppermute(hi, axis, [(i, (i + 1) % count) for i in range(count)])  7.52 us
    ppermute x3, starting transfers between devices, body(): lax.ppermute(w2, 'gz', [(i, (i + d) % 8) for i in range(8)])  6.48 us
    ppermute x6, starting transfers between devices, beyond(): lax.ppermute(x, axis, [(i, (i + d) % count) for i in range(count)])  6.09 us
    ppermute x3, starting transfers between devices, around(): lax.ppermute(lo, axis, [((i + 1) % count, i) for i in range(count)])  4.64 us
  transfers between devices with their start and end apart: 19, of which 7 were waited for; matrix products, arithmetic and copies ran while one was open for 0% of the time, Pallas kernels for 0%

profile of v6, /device:TPU:1, one launch (start us, length us, event | category | flops | bytes accessed | tf_op | source)
XLA Modules:
  0.0 100.8 jit_solution(17577985813240066490)
XLA Ops:
  1.6 0.9 copy-done.1
  3.3 2.5 %collective-permute-start = (f32[17,32,128]{2,1,0:T(8,128)S(1)}, f32[17,32,128]{2,1,0:T(8,128)S(1)}, u32[]{:S(2)}, u32[]{:S(2)}) collective-permute-start(f32[17,32,128]{2,1,0:T(8,128)S(1)} %get-tuple-element.26), channel_id=1, source_target_pairs={{0,32},{32,64},{64,96},{96,0},{1,33},{33,65},{65,97},{97,1},{2,34}... | collective-permute-start | bytes 835592 | tf_op jit(solution)/shard_map/ppermute | solution.py:677
  5.8 2.2 %collective-permute-start.1 = (f32[17,32,128]{2,1,0:T(8,128)S(1)}, f32[17,32,128]{2,1,0:T(8,128)S(1)}, u32[]{:S(2)}, u32[]{:S(2)}) collective-permute-start(f32[17,32,128]{2,1,0:T(8,128)S(1)} %get-tuple-element.27), channel_id=1, source_target_pairs={{32,0},{64,32},{96,64},{0,96},{33,1},{65,33},{97,65},{1,97},{34,2}... | collective-permute-start | bytes 835592 | tf_op jit(solution)/shard_map/ppermute | solution.py:676
  8.0 2.7 %collective-permute-start.4 = (f32[64,128]{1,0:T(8,128)S(1)}, f32[64,128]{1,0:T(8,128)S(1)}, u32[]{:S(2)}, u32[]{:S(2)}) collective-permute-start(f32[64,128]{1,0:T(8,128)S(1)} %get-tuple-element.28.b0), channel_id=1, source_target_pairs={{0,24},{8,0},{16,8},{24,16},{1,25},{9,1},{17,9},{25,17},{2,26},{10... | collective-permute-start | bytes 98312 | tf_op jit(solution)/shard_map/ppermute | solution.py:683
  11.8 3.3 %collective-permute-done.3.b2 = f32[64,128]{1,0:T(8,128)S(1)} collective-permute-done((f32[64,128]{1,0:T(8,128)S(1)}, f32[64,128]{1,0:T(8,128)S(1)}, u32[]{:S(2)}, u32[]{:S(2)}) %collective-permute-start.3) | collective-permute-done | bytes 32800 | tf_op jit(solution)/shard_map/ppermute | solution.py:683
  15.7 2.4 %collective-permute-start.6 = (f32[66,8,128]{2,1,0:T(8,128)S(1)}, f32[66,8,128]{2,1,0:T(8,128)S(1)}, u32[]{:S(2)}, u32[]{:S(2)}) collective-permute-start(f32[66,8,128]{2,1,0:T(8,128)S(1)} %get-tuple-element.30), channel_id=1, source_target_pairs={{8,0},{16,8},{24,16},{0,24},{9,1},{17,9},{25,17},{1,25},{10,2},{18... | collective-permute-start | bytes 811016 | tf_op jit(solution)/shard_map/ppermute | solution.py:676
  18.2 3.8 %collective-permute-done.5.yl = f32[66,8,128]{2,1,0:T(8,128)S(1)} collective-permute-done((f32[66,8,128]{2,1,0:T(8,128)S(1)}, f32[66,8,128]{2,1,0:T(8,128)S(1)}, u32[]{:S(2)}, u32[]{:S(2)}) %collective-permute-start.5) | collective-permute-done | bytes 270368 | tf_op jit(solution)/shard_map/ppermute | solution.py:677
  22.0 1.1 %pack_lanes.1 = (f32[96,8,128]{2,1,0:T(8,128)S(1)}, f32[96,8,128]{2,1,0:T(8,128)}) custom-call(f32[16,32,128]{2,1,0:T(8,128)S(1)} %get-tuple-element.24.wf, f32[16,32,128]{2,1,0:T(8,128)S(1)} %get-tuple-element.25.wb, f32[17,32,128]{2,1,0:T(8,128)S(1)} %collective-permute-done.xl, f32[17,32,128]{2,1,0:T(8,128)S(1)} %collective-permute-done.1.xu, ...), custom_call_target="tpu_custom_call" | custom-call | tf_op jit(solution)/shard_map/pack_lanes/pallas_call | solution.py:55
  23.1 4.7 %collective-permute-start.7 = (f32[96,8,128]{2,1,0:T(8,128)}, f32[96,8,128]{2,1,0:T(8,128)S(1)}, u32[]{:S(2)}, u32[]{:S(2)}) collective-permute-start(f32[96,8,128]{2,1,0:T(8,128)} %get-tuple-element.31), channel_id=1, source_target_pairs={{0,1},{1,2},{2,3},{3,4},{4,5},{5,6},{6,7},{7,0},{8,9},{9,10},{10,1... | collective-permute-start | bytes 1179656 | tf_op jit(solution)/shard_map/ppermute | solution.py:677
  27.8 1.7 %collective-permute-start.11 = (f32[4,64,128]{2,1,0:T(8,128)S(1)}, f32[4,64,128]{2,1,0:T(8,128)S(1)}, u32[]{:S(2)}, u32[]{:S(2)}) collective-permute-start(f32[4,64,128]{2,1,0:T(8,128)S(1)} %get-tuple-element.37.h0), channel_id=1, source_target_pairs={{0,96},{32,0},{64,32},{96,64},{1,97},{33,1},{65,33},{97,65},{2,98}... | collective-permute-start | bytes 393224 | tf_op jit(solution)/shard_map/ppermute | solution.py:683
  30.2 2.5 %collective-permute-done.11.h3 = f32[4,64,128]{2,1,0:T(8,128)S(1)} collective-permute-done((f32[4,64,128]{2,1,0:T(8,128)S(1)}, f32[4,64,128]{2,1,0:T(8,128)S(1)}, u32[]{:S(2)}, u32[]{:S(2)}) %collective-permute-start.11) | collective-permute-done | bytes 131104 | tf_op jit(solution)/shard_map/ppermute | solution.py:683
  32.7 2.2 %collective-permute-done.10.h2 = f32[4,64,128]{2,1,0:T(8,128)S(1)} collective-permute-done((f32[4,64,128]{2,1,0:T(8,128)S(1)}, f32[4,64,128]{2,1,0:T(8,128)S(1)}, u32[]{:S(2)}, u32[]{:S(2)}) %collective-permute-start.10) | collective-permute-done | bytes 131104 | tf_op jit(solution)/shard_map/ppermute | solution.py:683
  34.9 1.4 %collective-permute-done.9.h1 = f32[4,64,128]{2,1,0:T(8,128)S(1)} collective-permute-done((f32[4,64,128]{2,1,0:T(8,128)S(1)}, f32[4,64,128]{2,1,0:T(8,128)S(1)}, u32[]{:S(2)}, u32[]{:S(2)}) %collective-permute-start.9) | collective-permute-done | bytes 131104 | tf_op jit(solution)/shard_map/ppermute | solution.py:683
  36.4 7.4 %fine_down.1 = (f32[16,128,128]{2,1,0:T(8,128)S(1)}, f32[8,24,48,128]{3,2,1,0:T(8,128)}, f32[9,26,48,128]{3,2,1,0:T(8,128)}) custom-call(s32[3]{0:T(128)S(1)} %pad_add_fusion.at, f32[16,32,128]{2,1,0:T(8,128)S(1)} %get-tuple-element.24.wf, f32[16,32,128]{2,1,0:T(8,128)S(1)} %get-tuple-element.25.wb, f32[17,32,128]{2,1,0:T(8,128)S(1)} %collective-permute-done.xl, ...), custom_call_target="tpu_custom_call" | custom-call | tf_op jit(solution)/shard_map/fine_down/pallas_call | solution.py:55
  43.8 19.1 %all_to_all.5.g = f32[16,128,128]{2,1,0:T(8,128)S(1)} all-to-all(f32[16,128,128]{2,1,0:T(8,128)S(1)} %get-tuple-element.36), channel_id=1, replica_groups=mesh['gx'=4,'gy'=4,'gz'=8] {'gx','gy'}, dimensions={0} | all-to-all | bytes 2097152 | tf_op jit(solution)/shard_map/all_to_all | solution.py:724
  62.9 6.3 %mid_down.1 = (f32[8,32,128]{2,1,0:T(8,128)S(1)}, f32[2,8,16,32,128]{4,3,2,1,0:T(8,128)}, f32[18,32,128]{2,1,0:T(8,128)S(1)}) custom-call(s32[3]{0:T(128)S(1)} %pad_add_fusion.at, f32[16,128,128]{2,1,0:T(8,128)S(1)} %all_to_all.5.g, f32[4,64,128]{2,1,0:T(8,128)S(1)} %get-tuple-element.37.h0, f32[4,64,128]{2,1,0:T(8,128)S(1)} %collective-permute-done.9.h1, ...), custom_call_target="tpu_custom_call" | custom-call | tf_op jit(solution)/shard_map/mid_down/pallas_call | solution.py:55
  69.3 3.7 %collective-permute-start.14 = (f32[8,32,128]{2,1,0:T(8,128)S(1)}, f32[8,32,128]{2,1,0:T(8,128)S(1)}, u32[]{:S(2)}, u32[]{:S(2)}) collective-permute-start(f32[8,32,128]{2,1,0:T(8,128)S(1)} %get-tuple-element.41.m0), channel_id=1, source_target_pairs={{0,6},{1,7},{2,0},{3,1},{4,2},{5,3},{6,4},{7,5},{8,14},{9,15},{10,... | collective-permute-start | bytes 393224 | tf_op jit(solution)/shard_map/ppermute | solution.py:738
  72.9 2.5 %collective-permute-start.13 = (f32[8,32,128]{2,1,0:T(8,128)S(1)}, f32[8,32,128]{2,1,0:T(8,128)S(1)}, u32[]{:S(2)}, u32[]{:S(2)}) collective-permute-start(f32[8,32,128]{2,1,0:T(8,128)S(1)} %get-tuple-element.41.m0), channel_id=1, source_target_pairs={{0,4},{1,5},{2,6},{3,7},{4,0},{5,1},{6,2},{7,3},{8,12},{9,13},{10,... | collective-permute-start | bytes 393224 | tf_op jit(solution)/shard_map/ppermute | solution.py:738
  75.8 3.2 %collective-permute-start.15 = (f32[8,32,128]{2,1,0:T(8,128)S(1)}, f32[8,32,128]{2,1,0:T(8,128)S(1)}, u32[]{:S(2)}, u32[]{:S(2)}) collective-permute-start(f32[8,32,128]{2,1,0:T(8,128)S(1)} %get-tuple-element.41.m0), channel_id=1, source_target_pairs={{0,1},{1,0},{2,3},{3,2},{4,5},{5,4},{6,7},{7,6},{8,9},{9,8},{10,11... | collective-permute-start | bytes 393224 | tf_op jit(solution)/shard_map/ppermute | solution.py:739
  79.0 1.3 %collective-permute-start.18 = (f32[8,32,128]{2,1,0:T(8,128)S(1)}, f32[8,32,128]{2,1,0:T(8,128)S(1)}, u32[]{:S(2)}, u32[]{:S(2)}) collective-permute-start(f32[8,32,128]{2,1,0:T(8,128)S(1)} %collective-permute-done.14.m3), channel_id=1, source_target_pairs={{0,1},{1,0},{2,3},{3,2},{4,5},{5,4},{6,7},{7,6},{8,9},{9,8},{10,11... | collective-permute-start | bytes 393224 | tf_op jit(solution)/shard_map/ppermute | solution.py:739
  80.2 2.4 %collective-permute-start.17 = (f32[8,32,128]{2,1,0:T(8,128)S(1)}, f32[8,32,128]{2,1,0:T(8,128)S(1)}, u32[]{:S(2)}, u32[]{:S(2)}) collective-permute-start(f32[8,32,128]{2,1,0:T(8,128)S(1)} %collective-permute-done.13.m2), channel_id=1, source_target_pairs={{0,1},{1,0},{2,3},{3,2},{4,5},{5,4},{6,7},{7,6},{8,9},{9,8},{10,11... | collective-permute-start | bytes 393224 | tf_op jit(solution)/shard_map/ppermute | solution.py:739
  82.6 1.9 %collective-permute-start.16 = (f32[8,32,128]{2,1,0:T(8,128)S(1)}, f32[8,32,128]{2,1,0:T(8,128)S(1)}, u32[]{:S(2)}, u32[]{:S(2)}) collective-permute-start(f32[8,32,128]{2,1,0:T(8,128)S(1)} %collective-permute-done.12.m1), channel_id=1, source_target_pairs={{0,1},{1,0},{2,3},{3,2},{4,5},{5,4},{6,7},{7,6},{8,9},{9,8},{10,11... | collective-permute-start | bytes 393224 | tf_op jit(solution)/shard_map/ppermute | solution.py:739
  84.6 1.0 collective-permute-done.16.q1
  85.5 15.0 %coarse_up.1 = (f32[16,32,128]{2,1,0:T(8,128)}, f32[16,32,128]{2,1,0:T(8,128)}) custom-call(s32[3]{0:T(128)S(1)} %pad_add_fusion.at, f32[8,32,128]{2,1,0:T(8,128)S(1)} %get-tuple-element.41.m0, f32[8,32,128]{2,1,0:T(8,128)S(1)} %collective-permute-done.12.m1, f32[8,32,128]{2,1,0:T(8,128)S(1)} %collective-permute-done.13.m2, ...), custom_call_target="tpu_custom_call" | custom-call | tf_op jit(solution)/shard_map/coarse_up/pallas_call | solution.py:55
  (26 shorter events, 4.4 us)
Async XLA Ops:
  0.6 1.0 copy-start
  1.6 0.9 copy-start.1
  3.3 12.1 %collective-permute-start = (f32[17,32,128]{2,1,0:T(8,128)S(1)}, f32[17,32,128]{2,1,0:T(8,128)S(1)}, u32[]{:S(2)}, u32[]{:S(2)}) collective-permute-start(f32[17,32,128]{2,1,0:T(8,128)S(1)} %get-tuple-element.26), channel_id=1, source_target_pairs={{0,32},{32,64},{64,96},{96,0},{1,33},{33,65},{65,97},{97,1},{2,34}... | collective-permute-start | bytes 835592 | tf_op jit(solution)/shard_map/ppermute | solution.py:677
  5.8 9.6 %collective-permute-start.1 = (f32[17,32,128]{2,1,0:T(8,128)S(1)}, f32[17,32,128]{2,1,0:T(8,128)S(1)}, u32[]{:S(2)}, u32[]{:S(2)}) collective-permute-start(f32[17,32,128]{2,1,0:T(8,128)S(1)} %get-tuple-element.27), channel_id=1, source_target_pairs={{32,0},{64,32},{96,64},{0,96},{33,1},{65,33},{97,65},{1,97},{34,2}... | collective-permute-start | bytes 835592 | tf_op jit(solution)/shard_map/ppermute | solution.py:676
  8.0 3.8 %collective-permute-start.4 = (f32[64,128]{1,0:T(8,128)S(1)}, f32[64,128]{1,0:T(8,128)S(1)}, u32[]{:S(2)}, u32[]{:S(2)}) collective-permute-start(f32[64,128]{1,0:T(8,128)S(1)} %get-tuple-element.28.b0), channel_id=1, source_target_pairs={{0,24},{8,0},{16,8},{24,16},{1,25},{9,1},{17,9},{25,17},{2,26},{10... | collective-permute-start | bytes 98312 | tf_op jit(solution)/shard_map/ppermute | solution.py:683
  10.7 4.3 %collective-permute-start.3 = (f32[64,128]{1,0:T(8,128)S(1)}, f32[64,128]{1,0:T(8,128)S(1)}, u32[]{:S(2)}, u32[]{:S(2)}) collective-permute-start(f32[64,128]{1,0:T(8,128)S(1)} %get-tuple-element.28.b0), channel_id=1, source_target_pairs={{0,16},{8,24},{16,0},{24,8},{1,17},{9,25},{17,1},{25,9},{2,18},{10... | collective-permute-start | bytes 98312 | tf_op jit(solution)/shard_map/ppermute | solution.py:683
  11.1 4.3 %collective-permute-start.2 = (f32[64,128]{1,0:T(8,128)S(1)}, f32[64,128]{1,0:T(8,128)S(1)}, u32[]{:S(2)}, u32[]{:S(2)}) collective-permute-start(f32[64,128]{1,0:T(8,128)S(1)} %get-tuple-element.28.b0), channel_id=1, source_target_pairs={{0,8},{8,16},{16,24},{24,0},{1,9},{9,17},{17,25},{25,1},{2,10},{10... | collective-permute-start | bytes 98312 | tf_op jit(solution)/shard_map/ppermute | solution.py:683
  15.4 6.6 %collective-permute-start.5 = (f32[66,8,128]{2,1,0:T(8,128)S(1)}, f32[66,8,128]{2,1,0:T(8,128)S(1)}, u32[]{:S(2)}, u32[]{:S(2)}) collective-permute-start(f32[66,8,128]{2,1,0:T(8,128)S(1)} %get-tuple-element.29), channel_id=1, source_target_pairs={{0,8},{8,16},{16,24},{24,0},{1,9},{9,17},{17,25},{25,1},{2,10},{10... | collective-permute-start | bytes 811016 | tf_op jit(solution)/shard_map/ppermute | solution.py:677
  15.7 6.3 %collective-permute-start.6 = (f32[66,8,128]{2,1,0:T(8,128)S(1)}, f32[66,8,128]{2,1,0:T(8,128)S(1)}, u32[]{:S(2)}, u32[]{:S(2)}) collective-permute-start(f32[66,8,128]{2,1,0:T(8,128)S(1)} %get-tuple-element.30), channel_id=1, source_target_pairs={{8,0},{16,8},{24,16},{0,24},{9,1},{17,9},{25,17},{1,25},{10,2},{18... | collective-permute-start | bytes 811016 | tf_op jit(solution)/shard_map/ppermute | solution.py:676
  23.1 13.2 %collective-permute-start.7 = (f32[96,8,128]{2,1,0:T(8,128)}, f32[96,8,128]{2,1,0:T(8,128)S(1)}, u32[]{:S(2)}, u32[]{:S(2)}) collective-permute-start(f32[96,8,128]{2,1,0:T(8,128)} %get-tuple-element.31), channel_id=1, source_target_pairs={{0,1},{1,2},{2,3},{3,4},{4,5},{5,6},{6,7},{7,0},{8,9},{9,10},{10,1... | collective-permute-start | bytes 1179656 | tf_op jit(solution)/shard_map/ppermute | solution.py:677
  27.8 8.6 %collective-permute-start.8 = (f32[96,8,128]{2,1,0:T(8,128)S(1)}, f32[96,8,128]{2,1,0:T(8,128)S(1)}, u32[]{:S(2)}, u32[]{:S(2)}) collective-permute-start(f32[96,8,128]{2,1,0:T(8,128)S(1)} %get-tuple-element.32), channel_id=1, source_target_pairs={{1,0},{2,1},{3,2},{4,3},{5,4},{6,5},{7,6},{0,7},{9,8},{10,9},{11,1... | collective-permute-start | bytes 1179656 | tf_op jit(solution)/shard_map/ppermute | solution.py:676
  27.8 4.9 %collective-permute-start.11 = (f32[4,64,128]{2,1,0:T(8,128)S(1)}, f32[4,64,128]{2,1,0:T(8,128)S(1)}, u32[]{:S(2)}, u32[]{:S(2)}) collective-permute-start(f32[4,64,128]{2,1,0:T(8,128)S(1)} %get-tuple-element.37.h0), channel_id=1, source_target_pairs={{0,96},{32,0},{64,32},{96,64},{1,97},{33,1},{65,33},{97,65},{2,98}... | collective-permute-start | bytes 393224 | tf_op jit(solution)/shard_map/ppermute | solution.py:683
  29.5 5.4 %collective-permute-start.10 = (f32[4,64,128]{2,1,0:T(8,128)S(1)}, f32[4,64,128]{2,1,0:T(8,128)S(1)}, u32[]{:S(2)}, u32[]{:S(2)}) collective-permute-start(f32[4,64,128]{2,1,0:T(8,128)S(1)} %get-tuple-element.37.h0), channel_id=1, source_target_pairs={{0,64},{32,96},{64,0},{96,32},{1,65},{33,97},{65,1},{97,33},{2,66}... | collective-permute-start | bytes 393224 | tf_op jit(solution)/shard_map/ppermute | solution.py:683
  29.5 6.9 %collective-permute-start.9 = (f32[4,64,128]{2,1,0:T(8,128)S(1)}, f32[4,64,128]{2,1,0:T(8,128)S(1)}, u32[]{:S(2)}, u32[]{:S(2)}) collective-permute-start(f32[4,64,128]{2,1,0:T(8,128)S(1)} %get-tuple-element.37.h0), channel_id=1, source_target_pairs={{0,32},{32,64},{64,96},{96,0},{1,33},{33,65},{65,97},{97,1},{2,34}... | collective-permute-start | bytes 393224 | tf_op jit(solution)/shard_map/ppermute | solution.py:683
  69.3 9.7 %collective-permute-start.14 = (f32[8,32,128]{2,1,0:T(8,128)S(1)}, f32[8,32,128]{2,1,0:T(8,128)S(1)}, u32[]{:S(2)}, u32[]{:S(2)}) collective-permute-start(f32[8,32,128]{2,1,0:T(8,128)S(1)} %get-tuple-element.41.m0), channel_id=1, source_target_pairs={{0,6},{1,7},{2,0},{3,1},{4,2},{5,3},{6,4},{7,5},{8,14},{9,15},{10,... | collective-permute-start | bytes 393224 | tf_op jit(solution)/shard_map/ppermute | solution.py:738
  72.9 7.3 %collective-permute-start.13 = (f32[8,32,128]{2,1,0:T(8,128)S(1)}, f32[8,32,128]{2,1,0:T(8,128)S(1)}, u32[]{:S(2)}, u32[]{:S(2)}) collective-permute-start(f32[8,32,128]{2,1,0:T(8,128)S(1)} %get-tuple-element.41.m0), channel_id=1, source_target_pairs={{0,4},{1,5},{2,6},{3,7},{4,0},{5,1},{6,2},{7,3},{8,12},{9,13},{10,... | collective-permute-start | bytes 393224 | tf_op jit(solution)/shard_map/ppermute | solution.py:738
  75.5 7.2 %collective-permute-start.12 = (f32[8,32,128]{2,1,0:T(8,128)S(1)}, f32[8,32,128]{2,1,0:T(8,128)S(1)}, u32[]{:S(2)}, u32[]{:S(2)}) collective-permute-start(f32[8,32,128]{2,1,0:T(8,128)S(1)} %get-tuple-element.41.m0), channel_id=1, source_target_pairs={{0,2},{1,3},{2,4},{3,5},{4,6},{5,7},{6,0},{7,1},{8,10},{9,11},{10,... | collective-permute-start | bytes 393224 | tf_op jit(solution)/shard_map/ppermute | solution.py:738
  75.8 8.8 %collective-permute-start.15 = (f32[8,32,128]{2,1,0:T(8,128)S(1)}, f32[8,32,128]{2,1,0:T(8,128)S(1)}, u32[]{:S(2)}, u32[]{:S(2)}) collective-permute-start(f32[8,32,128]{2,1,0:T(8,128)S(1)} %get-tuple-element.41.m0), channel_id=1, source_target_pairs={{0,1},{1,0},{2,3},{3,2},{4,5},{5,4},{6,7},{7,6},{8,9},{9,8},{10,11... | collective-permute-start | bytes 393224 | tf_op jit(solution)/shard_map/ppermute | solution.py:739
  79.0 5.6 %collective-permute-start.18 = (f32[8,32,128]{2,1,0:T(8,128)S(1)}, f32[8,32,128]{2,1,0:T(8,128)S(1)}, u32[]{:S(2)}, u32[]{:S(2)}) collective-permute-start(f32[8,32,128]{2,1,0:T(8,128)S(1)} %collective-permute-done.14.m3), channel_id=1, source_target_pairs={{0,1},{1,0},{2,3},{3,2},{4,5},{5,4},{6,7},{7,6},{8,9},{9,8},{10,11... | collective-permute-start | bytes 393224 | tf_op jit(solution)/shard_map/ppermute | solution.py:739
  80.2 4.3 %collective-permute-start.17 = (f32[8,32,128]{2,1,0:T(8,128)S(1)}, f32[8,32,128]{2,1,0:T(8,128)S(1)}, u32[]{:S(2)}, u32[]{:S(2)}) collective-permute-start(f32[8,32,128]{2,1,0:T(8,128)S(1)} %collective-permute-done.13.m2), channel_id=1, source_target_pairs={{0,1},{1,0},{2,3},{3,2},{4,5},{5,4},{6,7},{7,6},{8,9},{9,8},{10,11... | collective-permute-start | bytes 393224 | tf_op jit(solution)/shard_map/ppermute | solution.py:739
  82.6 2.9 %collective-permute-start.16 = (f32[8,32,128]{2,1,0:T(8,128)S(1)}, f32[8,32,128]{2,1,0:T(8,128)S(1)}, u32[]{:S(2)}, u32[]{:S(2)}) collective-permute-start(f32[8,32,128]{2,1,0:T(8,128)S(1)} %collective-permute-done.12.m1), channel_id=1, source_target_pairs={{0,1},{1,0},{2,3},{3,2},{4,5},{5,4},{6,7},{7,6},{8,9},{9,8},{10,11... | collective-permute-start | bytes 393224 | tf_op jit(solution)/shard_map/ppermute | solution.py:739

commit v7 on v6

--- a/solution.py
+++ b/solution.py
@@ -11,7 +11,7 @@
 COARSE_ITERS = 20
 MIB = 1 << 20
 GROUP = 64
-LIMIT = 50
+LIMIT_FINE = 50
 LIMIT_MID = 50
 LIMIT_UP = 50
 
@@ -67,20 +67,16 @@
     return jax.ShapeDtypeStruct(shape, F32)
 
 
-def split_fine(f_in, b_in, wf_ref, wb_ref, lo_ref, hi_ref, b1_ref, f_ref, b_ref, tmp, sems):
-    loads = [pltpu.make_async_copy(b_in, b_ref, sems.at[0]), pltpu.make_async_copy(f_in, f_ref, sems.at[1])]
-    for c in loads:
-        c.start()
+def split_fine(both_ref, wf_ref, wb_ref, lo_ref, hi_ref, b1_ref, tmp):
     lane, row = lanes(32), sublanes(32)
     index = []
     for parity in range(2):
         odd = (row + parity) % 2
         index.append(2 * (lane % 64) + jnp.where(lane < 64, odd, 1 - odd))
-    loads[0].wait()
     lane16, row16 = lanes(16), sublanes(16)
     own = []
     for n in range(8):
-        w = [pick(b_ref[2 * n + parity], index[parity]) for parity in range(2)]
+        w = [pick(both_ref[16 + 2 * n + parity], index[parity]) for parity in range(2)]
         for parity in range(2):
             i = 2 * n + parity
             wb_ref[i] = w[parity]
@@ -94,9 +90,8 @@
         own.append(pick(halve_rows(tmp, both + turn(both, 64), 32), cell))
     for n in range(4):
         b1_ref[16 * n : 16 * n + 16] = jnp.where(lane16 < 64, own[n], own[n + 4])
-    loads[1].wait()
     for i in range(16):
-        wf = pick(f_ref[i], index[i % 2])
+        wf = pick(both_ref[i], index[i % 2])
         wf_ref[i] = wf
         if i < 8:
             lo_ref[i] = wf
@@ -689,13 +684,12 @@
     dma = pltpu.SemaphoreType.DMA
 
     block, x_slab = arr(16, 32, 128), arr(17, 32, 128)
-    buffer = pltpu.VMEM((16, 32, 128), F32)
     wf, wb, lo, hi, b1 = call(
         split_fine,
         [(block, block, x_slab, x_slab, arr(64, 128))],
-        (source, conductance),
-        [hbm] * 2,
-        [buffer, buffer, pltpu.VMEM((32, 128), F32), dma((2,))],
+        (jnp.concatenate([source, conductance]),),
+        None,
+        [pltpu.VMEM((32, 128), F32)],
         8,
     )
     xl, xu = around(lo, hi, "gx")
@@ -703,11 +697,9 @@
     y_slab = arr(66, 8, 128)
     lo, hi, b1 = call(pack_rows, [(y_slab, y_slab, arr(4, 64, 128))], (wf, wb, xl, xu, *b1), limit=8)
     yl, yu = around(lo, hi, "gy")
-    b1 = [b1] + beyond(b1, "gx")
+    yl, yu, *b1 = lax.optimization_barrier((yl, yu, b1, *beyond(b1, "gx")))
     lo, hi = call(pack_lanes, [(arr(96, 8, 128),) * 2], (wf, wb, xl, xu, yl, yu), limit=8)
     zl, zu = around(lo, hi, "gz")
-
-    zl, zu, *b1 = lax.optimization_barrier((zl, zu, *b1))
 
     colour0 = pltpu.VMEM((34, 64, 128), F32)
     right0 = pltpu.VMEM((32, 48, 128), F32)
@@ -719,7 +711,7 @@
         (at, wf, wb, xl, xu, yl, yu, zl, zu),
         [smem] + [vmem] * 8,
         [colour0, colour0, right0, right0, coef0, coef0, colour0, colour0, pltpu.VMEM((32, 128), F32), dma((3,))],
-        LIMIT,
+        LIMIT_FINE,
     )
     g = lax.all_to_all(g, ("gx", "gy"), 0, 0, tiled=True)
 

time: 101 us -> 102 us (level)
  waiting for transfers between devices: 14.6 us -> 21.4 us
  starting transfers between devices: 33.5 us -> 28.4 us
  local copies, waits for them, and re-layouts: 1.89 us -> 0 us
  other arithmetic: 0.08 us -> 1.14 us
    ppermute x4, starting transfers between devices: 8.77 us -> 4.58 us  [body(): pair = [lax.ppermute(w, 'gz', [(i, i ^ 1) for i in range(8)]) for w in mine]]
    ppermute x3, waiting for transfers between devices: 0.01 us -> 3.82 us  [body(): lax.ppermute(w2, 'gz', [(i, (i + d) % 8) for i in range(8)])]
    ppermute x3, waiting for transfers between devices: 0.01 us -> 2.17 us  [around(): lax.ppermute(lo, axis, [((i + 1) % count, i) for i in range(count)])]
    unnamed x4 -> x0, local copies, waits for them, and re-layouts: 1.89 us -> none
    ppermute x3, starting transfers between devices: 6.48 us -> 4.89 us  [body(): lax.ppermute(w2, 'gz', [(i, (i + d) % 8) for i in range(8)])]
    ppermute x3, waiting for transfers between devices: 3.85 us -> 4.96 us  [around(): lax.ppermute(hi, axis, [(i, (i + 1) % count) for i in range(count)])]
    concatenate x0 -> x1, other arithmetic: none -> 1.07 us  [body(): jnp.concatenate([source, conductance])]
  transfers between devices with their start and end apart: 19 -> 19, of which waited for: 7 -> 10; matrix products, arithmetic and copies ran while one was open for 0% -> 0% of each run, Pallas kernels for 0% -> 0%
where the time goes in v7:
time: 102 us
  Pallas kernels  30.7 us (30%)
  starting transfers between devices  28.4 us (28%)
  waiting for transfers between devices  21.4 us (21%)
  blocking collectives  19.3 us (19%)
  other arithmetic  1.14 us (1%)
    pallas_call x6, Pallas kernels, call(): pl.pallas_call(kernel, out_shape=out[0], in_specs=specs or [vmem] * len(a...  30.7 us
    all_to_all x1, blocking collectives, body(): g = lax.all_to_all(g, ('gx', 'gy'), 0, 0, tiled=True)  19.3 us
    ppermute x6, waiting for transfers between devices, beyond(): lax.ppermute(x, axis, [(i, (i + d) % count) for i in range(count)])  9.43 us
    ppermute x3, starting transfers between devices, around(): lax.ppermute(hi, axis, [(i, (i + 1) % count) for i in range(count)])  8.29 us
    ppermute x6, starting transfers between devices, beyond(): lax.ppermute(x, axis, [(i, (i + d) % count) for i in range(count)])  6.03 us
    ppermute x3, waiting for transfers between devices, around(): lax.ppermute(hi, axis, [(i, (i + 1) % count) for i in range(count)])  4.96 us
    ppermute x3, starting transfers between devices, body(): lax.ppermute(w2, 'gz', [(i, (i + d) % 8) for i in range(8)])  4.89 us
    ppermute x3, starting transfers between devices, around(): lax.ppermute(lo, axis, [((i + 1) % count, i) for i in range(count)])  4.64 us
  transfers between devices with their start and end apart: 19, of which 10 were waited for; matrix products, arithmetic and copies ran while one was open for 0% of the time, Pallas kernels for 0%

profile of v7, /device:TPU:1, one launch (start us, length us, event | category | flops | bytes accessed | tf_op | source)
XLA Modules:
  0.0 101.8 jit_solution(10616717869588477971)
XLA Ops:
  0.6 1.1 %pad_maximum_fusion.both_ref = f32[32,32,128]{2,1,0:T(8,128)S(1)} fusion(f32[16,32,128]{2,1,0:T(8,128)} %param.3, f32[16,32,128]{2,1,0:T(8,128)} %param.2), kind=kLoop, calls=%fused_computation | loop fusion | flops 131072 | bytes 1048576 | tf_op jit(solution)/shard_map/concatenate | solution.py:690
  2.4 2.5 %collective-permute-start = (f32[17,32,128]{2,1,0:T(8,128)S(1)}, f32[17,32,128]{2,1,0:T(8,128)S(1)}, u32[]{:S(2)}, u32[]{:S(2)}) collective-permute-start(f32[17,32,128]{2,1,0:T(8,128)S(1)} %get-tuple-element.26), channel_id=1, source_target_pairs={{0,32},{32,64},{64,96},{96,0},{1,33},{33,65},{65,97},{97,1},{2,34}... | collective-permute-start | bytes 835592 | tf_op jit(solution)/shard_map/ppermute | solution.py:672
  4.9 2.2 %collective-permute-start.1 = (f32[17,32,128]{2,1,0:T(8,128)S(1)}, f32[17,32,128]{2,1,0:T(8,128)S(1)}, u32[]{:S(2)}, u32[]{:S(2)}) collective-permute-start(f32[17,32,128]{2,1,0:T(8,128)S(1)} %get-tuple-element.27), channel_id=1, source_target_pairs={{32,0},{64,32},{96,64},{0,96},{33,1},{65,33},{97,65},{1,97},{34,2}... | collective-permute-start | bytes 835592 | tf_op jit(solution)/shard_map/ppermute | solution.py:671
  7.1 2.7 %collective-permute-start.4 = (f32[64,128]{1,0:T(8,128)S(1)}, f32[64,128]{1,0:T(8,128)S(1)}, u32[]{:S(2)}, u32[]{:S(2)}) collective-permute-start(f32[64,128]{1,0:T(8,128)S(1)} %get-tuple-element.28.b0), channel_id=1, source_target_pairs={{0,24},{8,0},{16,8},{24,16},{1,25},{9,1},{17,9},{25,17},{2,26},{10... | collective-permute-start | bytes 98312 | tf_op jit(solution)/shard_map/ppermute | solution.py:678
  10.9 3.3 %collective-permute-done.3.b2 = f32[64,128]{1,0:T(8,128)S(1)} collective-permute-done((f32[64,128]{1,0:T(8,128)S(1)}, f32[64,128]{1,0:T(8,128)S(1)}, u32[]{:S(2)}, u32[]{:S(2)}) %collective-permute-start.3) | collective-permute-done | bytes 32800 | tf_op jit(solution)/shard_map/ppermute | solution.py:678
  14.9 2.4 %collective-permute-start.6 = (f32[66,8,128]{2,1,0:T(8,128)S(1)}, f32[66,8,128]{2,1,0:T(8,128)S(1)}, u32[]{:S(2)}, u32[]{:S(2)}) collective-permute-start(f32[66,8,128]{2,1,0:T(8,128)S(1)} %get-tuple-element.30), channel_id=1, source_target_pairs={{8,0},{16,8},{24,16},{0,24},{9,1},{17,9},{25,17},{1,25},{10,2},{18... | collective-permute-start | bytes 811016 | tf_op jit(solution)/shard_map/ppermute | solution.py:671
  17.3 1.7 %collective-permute-start.9 = (f32[4,64,128]{2,1,0:T(8,128)S(1)}, f32[4,64,128]{2,1,0:T(8,128)S(1)}, u32[]{:S(2)}, u32[]{:S(2)}) collective-permute-start(f32[4,64,128]{2,1,0:T(8,128)S(1)} %get-tuple-element.37.h0), channel_id=1, source_target_pairs={{0,96},{32,0},{64,32},{96,64},{1,97},{33,1},{65,33},{97,65},{2,98}... | collective-permute-start | bytes 393224 | tf_op jit(solution)/shard_map/ppermute | solution.py:678
  19.6 2.7 %collective-permute-done.9.h3 = f32[4,64,128]{2,1,0:T(8,128)S(1)} collective-permute-done((f32[4,64,128]{2,1,0:T(8,128)S(1)}, f32[4,64,128]{2,1,0:T(8,128)S(1)}, u32[]{:S(2)}, u32[]{:S(2)}) %collective-permute-start.9) | collective-permute-done | bytes 131104 | tf_op jit(solution)/shard_map/ppermute | solution.py:678
  22.3 2.1 %collective-permute-done.8.h2 = f32[4,64,128]{2,1,0:T(8,128)S(1)} collective-permute-done((f32[4,64,128]{2,1,0:T(8,128)S(1)}, f32[4,64,128]{2,1,0:T(8,128)S(1)}, u32[]{:S(2)}, u32[]{:S(2)}) %collective-permute-start.8) | collective-permute-done | bytes 131104 | tf_op jit(solution)/shard_map/ppermute | solution.py:678
  25.4 1.1 %pack_lanes.1 = (f32[96,8,128]{2,1,0:T(8,128)S(1)}, f32[96,8,128]{2,1,0:T(8,128)}) custom-call(f32[16,32,128]{2,1,0:T(8,128)S(1)} %get-tuple-element.24.wf, f32[16,32,128]{2,1,0:T(8,128)S(1)} %get-tuple-element.25.wb, f32[17,32,128]{2,1,0:T(8,128)S(1)} %collective-permute-done.xl, f32[17,32,128]{2,1,0:T(8,128)S(1)} %collective-permute-done.1.xu, ...), custom_call_target="tpu_custom_call" | custom-call | tf_op jit(solution)/shard_map/pack_lanes/pallas_call | solution.py:55
  26.6 5.5 %collective-permute-start.10 = (f32[96,8,128]{2,1,0:T(8,128)}, f32[96,8,128]{2,1,0:T(8,128)S(1)}, u32[]{:S(2)}, u32[]{:S(2)}) collective-permute-start(f32[96,8,128]{2,1,0:T(8,128)} %get-tuple-element.34), channel_id=1, source_target_pairs={{0,1},{1,2},{2,3},{3,4},{4,5},{5,6},{6,7},{7,0},{8,9},{9,10},{10,1... | collective-permute-start | bytes 1179656 | tf_op jit(solution)/shard_map/ppermute | solution.py:672
  32.1 5.0 %collective-permute-done.10.zl = f32[96,8,128]{2,1,0:T(8,128)S(1)} collective-permute-done((f32[96,8,128]{2,1,0:T(8,128)}, f32[96,8,128]{2,1,0:T(8,128)S(1)}, u32[]{:S(2)}, u32[]{:S(2)}) %collective-permute-start.10) | collective-permute-done | bytes 393248 | tf_op jit(solution)/shard_map/ppermute | solution.py:672
  37.0 2.2 %collective-permute-done.11.zu = f32[96,8,128]{2,1,0:T(8,128)S(1)} collective-permute-done((f32[96,8,128]{2,1,0:T(8,128)S(1)}, f32[96,8,128]{2,1,0:T(8,128)S(1)}, u32[]{:S(2)}, u32[]{:S(2)}) %collective-permute-start.11) | collective-permute-done | bytes 393248 | tf_op jit(solution)/shard_map/ppermute | solution.py:671
  39.2 7.4 %fine_down.1 = (f32[16,128,128]{2,1,0:T(8,128)S(1)}, f32[8,24,48,128]{3,2,1,0:T(8,128)}, f32[9,26,48,128]{3,2,1,0:T(8,128)}) custom-call(s32[3]{0:T(128)S(1)} %pad_add_fusion.at, f32[16,32,128]{2,1,0:T(8,128)S(1)} %get-tuple-element.24.wf, f32[16,32,128]{2,1,0:T(8,128)S(1)} %get-tuple-element.25.wb, f32[17,32,128]{2,1,0:T(8,128)S(1)} %collective-permute-done.xl, ...), custom_call_target="tpu_custom_call" | custom-call | tf_op jit(solution)/shard_map/fine_down/pallas_call | solution.py:55
  46.6 19.3 %all_to_all.5.g = f32[16,128,128]{2,1,0:T(8,128)S(1)} all-to-all(f32[16,128,128]{2,1,0:T(8,128)S(1)} %get-tuple-element.36), channel_id=1, replica_groups=mesh['gx'=4,'gy'=4,'gz'=8] {'gx','gy'}, dimensions={0} | all-to-all | bytes 2097152 | tf_op jit(solution)/shard_map/all_to_all | solution.py:716
  66.0 6.3 %mid_down.1 = (f32[8,32,128]{2,1,0:T(8,128)S(1)}, f32[2,8,16,32,128]{4,3,2,1,0:T(8,128)}, f32[18,32,128]{2,1,0:T(8,128)S(1)}) custom-call(s32[3]{0:T(128)S(1)} %pad_add_fusion.at, f32[16,128,128]{2,1,0:T(8,128)S(1)} %all_to_all.5.g, f32[4,64,128]{2,1,0:T(8,128)S(1)} %get-tuple-element.37.h0, f32[4,64,128]{2,1,0:T(8,128)S(1)} %collective-permute-done.7.h1, ...), custom_call_target="tpu_custom_call" | custom-call | tf_op jit(solution)/shard_map/mid_down/pallas_call | solution.py:55
  72.3 3.1 %collective-permute-start.14 = (f32[8,32,128]{2,1,0:T(8,128)S(1)}, f32[8,32,128]{2,1,0:T(8,128)S(1)}, u32[]{:S(2)}, u32[]{:S(2)}) collective-permute-start(f32[8,32,128]{2,1,0:T(8,128)S(1)} %get-tuple-element.41.m0), channel_id=1, source_target_pairs={{0,6},{1,7},{2,0},{3,1},{4,2},{5,3},{6,4},{7,5},{8,14},{9,15},{10,... | collective-permute-start | bytes 393224 | tf_op jit(solution)/shard_map/ppermute | solution.py:730
  75.4 1.1 %collective-permute-start.13 = (f32[8,32,128]{2,1,0:T(8,128)S(1)}, f32[8,32,128]{2,1,0:T(8,128)S(1)}, u32[]{:S(2)}, u32[]{:S(2)}) collective-permute-start(f32[8,32,128]{2,1,0:T(8,128)S(1)} %get-tuple-element.41.m0), channel_id=1, source_target_pairs={{0,4},{1,5},{2,6},{3,7},{4,0},{5,1},{6,2},{7,3},{8,12},{9,13},{10,... | collective-permute-start | bytes 393224 | tf_op jit(solution)/shard_map/ppermute | solution.py:730
  77.2 1.2 %collective-permute-start.15 = (f32[8,32,128]{2,1,0:T(8,128)S(1)}, f32[8,32,128]{2,1,0:T(8,128)S(1)}, u32[]{:S(2)}, u32[]{:S(2)}) collective-permute-start(f32[8,32,128]{2,1,0:T(8,128)S(1)} %get-tuple-element.41.m0), channel_id=1, source_target_pairs={{0,1},{1,0},{2,3},{3,2},{4,5},{5,4},{6,7},{7,6},{8,9},{9,8},{10,11... | collective-permute-start | bytes 393224 | tf_op jit(solution)/shard_map/ppermute | solution.py:731
  78.4 2.4 %collective-permute-done.14.m3 = f32[8,32,128]{2,1,0:T(8,128)S(1)} collective-permute-done((f32[8,32,128]{2,1,0:T(8,128)S(1)}, f32[8,32,128]{2,1,0:T(8,128)S(1)}, u32[]{:S(2)}, u32[]{:S(2)}) %collective-permute-start.14) | collective-permute-done | bytes 131104 | tf_op jit(solution)/shard_map/ppermute | solution.py:730
  80.8 1.1 %collective-permute-start.18 = (f32[8,32,128]{2,1,0:T(8,128)S(1)}, f32[8,32,128]{2,1,0:T(8,128)S(1)}, u32[]{:S(2)}, u32[]{:S(2)}) collective-permute-start(f32[8,32,128]{2,1,0:T(8,128)S(1)} %collective-permute-done.14.m3), channel_id=1, source_target_pairs={{0,1},{1,0},{2,3},{3,2},{4,5},{5,4},{6,7},{7,6},{8,9},{9,8},{10,11... | collective-permute-start | bytes 393224 | tf_op jit(solution)/shard_map/ppermute | solution.py:731
  81.9 1.7 %collective-permute-start.17 = (f32[8,32,128]{2,1,0:T(8,128)S(1)}, f32[8,32,128]{2,1,0:T(8,128)S(1)}, u32[]{:S(2)}, u32[]{:S(2)}) collective-permute-start(f32[8,32,128]{2,1,0:T(8,128)S(1)} %collective-permute-done.13.m2), channel_id=1, source_target_pairs={{0,1},{1,0},{2,3},{3,2},{4,5},{5,4},{6,7},{7,6},{8,9},{9,8},{10,11... | collective-permute-start | bytes 393224 | tf_op jit(solution)/shard_map/ppermute | solution.py:731
  83.7 1.4 %collective-permute-done.12.m1 = f32[8,32,128]{2,1,0:T(8,128)S(1)} collective-permute-done((f32[8,32,128]{2,1,0:T(8,128)S(1)}, f32[8,32,128]{2,1,0:T(8,128)S(1)}, u32[]{:S(2)}, u32[]{:S(2)}) %collective-permute-start.12) | collective-permute-done | bytes 131104 | tf_op jit(solution)/shard_map/ppermute | solution.py:730
  86.6 15.1 %coarse_up.1 = (f32[16,32,128]{2,1,0:T(8,128)}, f32[16,32,128]{2,1,0:T(8,128)}) custom-call(s32[3]{0:T(128)S(1)} %pad_add_fusion.at, f32[8,32,128]{2,1,0:T(8,128)S(1)} %get-tuple-element.41.m0, f32[8,32,128]{2,1,0:T(8,128)S(1)} %collective-permute-done.12.m1, f32[8,32,128]{2,1,0:T(8,128)S(1)} %collective-permute-done.13.m2, ...), custom_call_target="tpu_custom_call" | custom-call | tf_op jit(solution)/shard_map/coarse_up/pallas_call | solution.py:55
  (23 shorter events, 6.4 us)
Async XLA Ops:
  2.4 12.1 %collective-permute-start = (f32[17,32,128]{2,1,0:T(8,128)S(1)}, f32[17,32,128]{2,1,0:T(8,128)S(1)}, u32[]{:S(2)}, u32[]{:S(2)}) collective-permute-start(f32[17,32,128]{2,1,0:T(8,128)S(1)} %get-tuple-element.26), channel_id=1, source_target_pairs={{0,32},{32,64},{64,96},{96,0},{1,33},{33,65},{65,97},{97,1},{2,34}... | collective-permute-start | bytes 835592 | tf_op jit(solution)/shard_map/ppermute | solution.py:672
  4.9 9.6 %collective-permute-start.1 = (f32[17,32,128]{2,1,0:T(8,128)S(1)}, f32[17,32,128]{2,1,0:T(8,128)S(1)}, u32[]{:S(2)}, u32[]{:S(2)}) collective-permute-start(f32[17,32,128]{2,1,0:T(8,128)S(1)} %get-tuple-element.27), channel_id=1, source_target_pairs={{32,0},{64,32},{96,64},{0,96},{33,1},{65,33},{97,65},{1,97},{34,2}... | collective-permute-start | bytes 835592 | tf_op jit(solution)/shard_map/ppermute | solution.py:671
  7.1 3.8 %collective-permute-start.4 = (f32[64,128]{1,0:T(8,128)S(1)}, f32[64,128]{1,0:T(8,128)S(1)}, u32[]{:S(2)}, u32[]{:S(2)}) collective-permute-start(f32[64,128]{1,0:T(8,128)S(1)} %get-tuple-element.28.b0), channel_id=1, source_target_pairs={{0,24},{8,0},{16,8},{24,16},{1,25},{9,1},{17,9},{25,17},{2,26},{10... | collective-permute-start | bytes 98312 | tf_op jit(solution)/shard_map/ppermute | solution.py:678
  9.9 4.3 %collective-permute-start.3 = (f32[64,128]{1,0:T(8,128)S(1)}, f32[64,128]{1,0:T(8,128)S(1)}, u32[]{:S(2)}, u32[]{:S(2)}) collective-permute-start(f32[64,128]{1,0:T(8,128)S(1)} %get-tuple-element.28.b0), channel_id=1, source_target_pairs={{0,16},{8,24},{16,0},{24,8},{1,17},{9,25},{17,1},{25,9},{2,18},{10... | collective-permute-start | bytes 98312 | tf_op jit(solution)/shard_map/ppermute | solution.py:678
  10.2 4.3 %collective-permute-start.2 = (f32[64,128]{1,0:T(8,128)S(1)}, f32[64,128]{1,0:T(8,128)S(1)}, u32[]{:S(2)}, u32[]{:S(2)}) collective-permute-start(f32[64,128]{1,0:T(8,128)S(1)} %get-tuple-element.28.b0), channel_id=1, source_target_pairs={{0,8},{8,16},{16,24},{24,0},{1,9},{9,17},{17,25},{25,1},{2,10},{10... | collective-permute-start | bytes 98312 | tf_op jit(solution)/shard_map/ppermute | solution.py:678
  14.6 10.9 %collective-permute-start.5 = (f32[66,8,128]{2,1,0:T(8,128)S(1)}, f32[66,8,128]{2,1,0:T(8,128)S(1)}, u32[]{:S(2)}, u32[]{:S(2)}) collective-permute-start(f32[66,8,128]{2,1,0:T(8,128)S(1)} %get-tuple-element.29), channel_id=1, source_target_pairs={{0,8},{8,16},{16,24},{24,0},{1,9},{9,17},{17,25},{25,1},{2,10},{10... | collective-permute-start | bytes 811016 | tf_op jit(solution)/shard_map/ppermute | solution.py:672
  14.9 10.6 %collective-permute-start.6 = (f32[66,8,128]{2,1,0:T(8,128)S(1)}, f32[66,8,128]{2,1,0:T(8,128)S(1)}, u32[]{:S(2)}, u32[]{:S(2)}) collective-permute-start(f32[66,8,128]{2,1,0:T(8,128)S(1)} %get-tuple-element.30), channel_id=1, source_target_pairs={{8,0},{16,8},{24,16},{0,24},{9,1},{17,9},{25,17},{1,25},{10,2},{18... | collective-permute-start | bytes 811016 | tf_op jit(solution)/shard_map/ppermute | solution.py:671
  17.3 5.0 %collective-permute-start.9 = (f32[4,64,128]{2,1,0:T(8,128)S(1)}, f32[4,64,128]{2,1,0:T(8,128)S(1)}, u32[]{:S(2)}, u32[]{:S(2)}) collective-permute-start(f32[4,64,128]{2,1,0:T(8,128)S(1)} %get-tuple-element.37.h0), channel_id=1, source_target_pairs={{0,96},{32,0},{64,32},{96,64},{1,97},{33,1},{65,33},{97,65},{2,98}... | collective-permute-start | bytes 393224 | tf_op jit(solution)/shard_map/ppermute | solution.py:678
  19.0 5.4 %collective-permute-start.8 = (f32[4,64,128]{2,1,0:T(8,128)S(1)}, f32[4,64,128]{2,1,0:T(8,128)S(1)}, u32[]{:S(2)}, u32[]{:S(2)}) collective-permute-start(f32[4,64,128]{2,1,0:T(8,128)S(1)} %get-tuple-element.37.h0), channel_id=1, source_target_pairs={{0,64},{32,96},{64,0},{96,32},{1,65},{33,97},{65,1},{97,33},{2,66}... | collective-permute-start | bytes 393224 | tf_op jit(solution)/shard_map/ppermute | solution.py:678
  19.0 6.4 %collective-permute-start.7 = (f32[4,64,128]{2,1,0:T(8,128)S(1)}, f32[4,64,128]{2,1,0:T(8,128)S(1)}, u32[]{:S(2)}, u32[]{:S(2)}) collective-permute-start(f32[4,64,128]{2,1,0:T(8,128)S(1)} %get-tuple-element.37.h0), channel_id=1, source_target_pairs={{0,32},{32,64},{64,96},{96,0},{1,33},{33,65},{65,97},{97,1},{2,34}... | collective-permute-start | bytes 393224 | tf_op jit(solution)/shard_map/ppermute | solution.py:678
  26.6 10.5 %collective-permute-start.10 = (f32[96,8,128]{2,1,0:T(8,128)}, f32[96,8,128]{2,1,0:T(8,128)S(1)}, u32[]{:S(2)}, u32[]{:S(2)}) collective-permute-start(f32[96,8,128]{2,1,0:T(8,128)} %get-tuple-element.34), channel_id=1, source_target_pairs={{0,1},{1,2},{2,3},{3,4},{4,5},{5,6},{6,7},{7,0},{8,9},{9,10},{10,1... | collective-permute-start | bytes 1179656 | tf_op jit(solution)/shard_map/ppermute | solution.py:672
  32.0 7.2 %collective-permute-start.11 = (f32[96,8,128]{2,1,0:T(8,128)S(1)}, f32[96,8,128]{2,1,0:T(8,128)S(1)}, u32[]{:S(2)}, u32[]{:S(2)}) collective-permute-start(f32[96,8,128]{2,1,0:T(8,128)S(1)} %get-tuple-element.35), channel_id=1, source_target_pairs={{1,0},{2,1},{3,2},{4,3},{5,4},{6,5},{7,6},{0,7},{9,8},{10,9},{11,1... | collective-permute-start | bytes 1179656 | tf_op jit(solution)/shard_map/ppermute | solution.py:671
  72.3 8.5 %collective-permute-start.14 = (f32[8,32,128]{2,1,0:T(8,128)S(1)}, f32[8,32,128]{2,1,0:T(8,128)S(1)}, u32[]{:S(2)}, u32[]{:S(2)}) collective-permute-start(f32[8,32,128]{2,1,0:T(8,128)S(1)} %get-tuple-element.41.m0), channel_id=1, source_target_pairs={{0,6},{1,7},{2,0},{3,1},{4,2},{5,3},{6,4},{7,5},{8,14},{9,15},{10,... | collective-permute-start | bytes 393224 | tf_op jit(solution)/shard_map/ppermute | solution.py:730
  75.4 6.6 %collective-permute-start.13 = (f32[8,32,128]{2,1,0:T(8,128)S(1)}, f32[8,32,128]{2,1,0:T(8,128)S(1)}, u32[]{:S(2)}, u32[]{:S(2)}) collective-permute-start(f32[8,32,128]{2,1,0:T(8,128)S(1)} %get-tuple-element.41.m0), channel_id=1, source_target_pairs={{0,4},{1,5},{2,6},{3,7},{4,0},{5,1},{6,2},{7,3},{8,12},{9,13},{10,... | collective-permute-start | bytes 393224 | tf_op jit(solution)/shard_map/ppermute | solution.py:730
  76.4 8.7 %collective-permute-start.12 = (f32[8,32,128]{2,1,0:T(8,128)S(1)}, f32[8,32,128]{2,1,0:T(8,128)S(1)}, u32[]{:S(2)}, u32[]{:S(2)}) collective-permute-start(f32[8,32,128]{2,1,0:T(8,128)S(1)} %get-tuple-element.41.m0), channel_id=1, source_target_pairs={{0,2},{1,3},{2,4},{3,5},{4,6},{5,7},{6,0},{7,1},{8,10},{9,11},{10,... | collective-permute-start | bytes 393224 | tf_op jit(solution)/shard_map/ppermute | solution.py:730
  77.2 8.4 %collective-permute-start.15 = (f32[8,32,128]{2,1,0:T(8,128)S(1)}, f32[8,32,128]{2,1,0:T(8,128)S(1)}, u32[]{:S(2)}, u32[]{:S(2)}) collective-permute-start(f32[8,32,128]{2,1,0:T(8,128)S(1)} %get-tuple-element.41.m0), channel_id=1, source_target_pairs={{0,1},{1,0},{2,3},{3,2},{4,5},{5,4},{6,7},{7,6},{8,9},{9,8},{10,11... | collective-permute-start | bytes 393224 | tf_op jit(solution)/shard_map/ppermute | solution.py:731
  80.8 4.8 %collective-permute-start.18 = (f32[8,32,128]{2,1,0:T(8,128)S(1)}, f32[8,32,128]{2,1,0:T(8,128)S(1)}, u32[]{:S(2)}, u32[]{:S(2)}) collective-permute-start(f32[8,32,128]{2,1,0:T(8,128)S(1)} %collective-permute-done.14.m3), channel_id=1, source_target_pairs={{0,1},{1,0},{2,3},{3,2},{4,5},{5,4},{6,7},{7,6},{8,9},{9,8},{10,11... | collective-permute-start | bytes 393224 | tf_op jit(solution)/shard_map/ppermute | solution.py:731
  81.9 3.7 %collective-permute-start.17 = (f32[8,32,128]{2,1,0:T(8,128)S(1)}, f32[8,32,128]{2,1,0:T(8,128)S(1)}, u32[]{:S(2)}, u32[]{:S(2)}) collective-permute-start(f32[8,32,128]{2,1,0:T(8,128)S(1)} %collective-permute-done.13.m2), channel_id=1, source_target_pairs={{0,1},{1,0},{2,3},{3,2},{4,5},{5,4},{6,7},{7,6},{8,9},{9,8},{10,11... | collective-permute-start | bytes 393224 | tf_op jit(solution)/shard_map/ppermute | solution.py:731
  85.1 1.5 %collective-permute-start.16 = (f32[8,32,128]{2,1,0:T(8,128)S(1)}, f32[8,32,128]{2,1,0:T(8,128)S(1)}, u32[]{:S(2)}, u32[]{:S(2)}) collective-permute-start(f32[8,32,128]{2,1,0:T(8,128)S(1)} %collective-permute-done.12.m1), channel_id=1, source_target_pairs={{0,1},{1,0},{2,3},{3,2},{4,5},{5,4},{6,7},{7,6},{8,9},{9,8},{10,11... | collective-permute-start | bytes 393224 | tf_op jit(solution)/shard_map/ppermute | solution.py:731

commit v8 on v7

--- a/solution.py
+++ b/solution.py
@@ -502,7 +502,7 @@
 
 
 def coarse_up(
-    at, m0, m1, m2, m3, q0, q1, q2, q3, c1_in, v1b_in, c0r_in, c0b_in, u_ref, res_ref,
+    at, m0, m1, m2, m3, q0, q123, c1_in, v1b_in, c0r_in, c0b_in, u_ref, res_ref,
     b2r, b2b, v2r, v2b, c2r, c2b, f2,
     b3r, b3b, v3r, v3b, c3r, c3b, f3,
     b4r, b4b, v4r, v4b, c4r, c4b, f4,
@@ -527,6 +527,7 @@
 
     chip = gz // 2
     first = gz % 2 == 0
+    q1, q2, q3 = (q123.at[pl.ds(8 * n, 8)] for n in range(3))
     for n in range(8):
         near = [(jnp.where(first, a[n], b[n]), jnp.where(first, b[n], a[n])) for a, b in ((m0, q0), (m1, q1), (m2, q2), (m3, q3))]
         blocks = []
@@ -728,7 +729,9 @@
         LIMIT_MID,
     )
     mine = [w2] + [lax.ppermute(w2, "gz", [(i, (i + d) % 8) for i in range(8)]) for d in (2, 4, 6)]
-    pair = [lax.ppermute(w, "gz", [(i, i ^ 1) for i in range(8)]) for w in mine]
+    swap = [(i, i ^ 1) for i in range(8)]
+    near, *mine = lax.optimization_barrier((lax.ppermute(w2, "gz", swap), *mine))
+    pair = [near, lax.ppermute(jnp.concatenate(mine[1:]), "gz", swap)]
 
     scratch = []
     for planes, rows in ((16, 32), (8, 16), (4, 8)):
@@ -740,7 +743,7 @@
         coarse_up,
         [(block, block)],
         (at, *mine, *pair, c1, v1b, c0r, c0b),
-        [smem] + [vmem] * 8 + [hbm] * 4,
+        [smem] + [vmem] * 6 + [hbm] * 4,
         scratch,
         LIMIT_UP,
     )

time: 102 us -> 102 us (level)
  waiting for transfers between devices: 21.4 us -> 24.6 us
  starting transfers between devices: 28.4 us -> 25.7 us
    ppermute x3, waiting for transfers between devices: 3.82 us -> 6.67 us  [body(): lax.ppermute(w2, 'gz', [(i, (i + d) % 8) for i in range(8)])]
    ppermute x4 -> x2, starting transfers between devices: 4.58 us -> 1.81 us  [the longest x1 1.23 us: body(): lax.ppermute(w2, 'gz', swap)]
  transfers between devices with their start and end apart: 19 -> 17, of which waited for: 10 -> 11; matrix products, arithmetic and copies ran while one was open for 0% -> 0% of each run, Pallas kernels for 0% -> 0%
where the time goes in v8:
time: 102 us
  Pallas kernels  30.7 us (30%)
  starting transfers between devices  25.7 us (25%)
  waiting for transfers between devices  24.6 us (24%)
  blocking collectives  19.3 us (19%)
  other arithmetic  1.17 us (1%)
    pallas_call x6, Pallas kernels, call(): pl.pallas_call(kernel, out_shape=out[0], in_specs=specs or [vmem] * len(a...  30.7 us
    all_to_all x1, blocking collectives, body(): g = lax.all_to_all(g, ('gx', 'gy'), 0, 0, tiled=True)  19.3 us
    ppermute x6, waiting for transfers between devices, beyond(): lax.ppermute(x, axis, [(i, (i + d) % count) for i in range(count)])  9.43 us
    ppermute x3, starting transfers between devices, around(): lax.ppermute(hi, axis, [(i, (i + 1) % count) for i in range(count)])  8.29 us
    ppermute x3, waiting for transfers between devices, body(): lax.ppermute(w2, 'gz', [(i, (i + d) % 8) for i in range(8)])  6.67 us
    ppermute x6, starting transfers between devices, beyond(): lax.ppermute(x, axis, [(i, (i + d) % count) for i in range(count)])  6.03 us
    ppermute x3, waiting for transfers between devices, around(): lax.ppermute(hi, axis, [(i, (i + 1) % count) for i in range(count)])  4.96 us
    ppermute x3, starting transfers between devices, body(): lax.ppermute(w2, 'gz', [(i, (i + d) % 8) for i in range(8)])  4.89 us
  transfers between devices with their start and end apart: 17, of which 11 were waited for; matrix products, arithmetic and copies ran while one was open for 0% of the time, Pallas kernels for 0%

profile of v8, /device:TPU:1, one launch (start us, length us, event | category | flops | bytes accessed | tf_op | source)
XLA Modules:
  0.0 102.3 jit_solution(125177040669349658)
XLA Ops:
  0.6 1.1 %pad_maximum_fusion.both_ref = f32[32,32,128]{2,1,0:T(8,128)S(1)} fusion(f32[16,32,128]{2,1,0:T(8,128)} %param.3, f32[16,32,128]{2,1,0:T(8,128)} %param.2), kind=kLoop, calls=%fused_computation | loop fusion | flops 131072 | bytes 1048576 | tf_op jit(solution)/shard_map/concatenate | solution.py:691
  2.4 2.5 %collective-permute-start = (f32[17,32,128]{2,1,0:T(8,128)S(1)}, f32[17,32,128]{2,1,0:T(8,128)S(1)}, u32[]{:S(2)}, u32[]{:S(2)}) collective-permute-start(f32[17,32,128]{2,1,0:T(8,128)S(1)} %get-tuple-element.31), channel_id=1, source_target_pairs={{0,32},{32,64},{64,96},{96,0},{1,33},{33,65},{65,97},{97,1},{2,34}... | collective-permute-start | bytes 835592 | tf_op jit(solution)/shard_map/ppermute | solution.py:673
  4.9 2.2 %collective-permute-start.1 = (f32[17,32,128]{2,1,0:T(8,128)S(1)}, f32[17,32,128]{2,1,0:T(8,128)S(1)}, u32[]{:S(2)}, u32[]{:S(2)}) collective-permute-start(f32[17,32,128]{2,1,0:T(8,128)S(1)} %get-tuple-element.32), channel_id=1, source_target_pairs={{32,0},{64,32},{96,64},{0,96},{33,1},{65,33},{97,65},{1,97},{34,2}... | collective-permute-start | bytes 835592 | tf_op jit(solution)/shard_map/ppermute | solution.py:672
  7.1 2.7 %collective-permute-start.4 = (f32[64,128]{1,0:T(8,128)S(1)}, f32[64,128]{1,0:T(8,128)S(1)}, u32[]{:S(2)}, u32[]{:S(2)}) collective-permute-start(f32[64,128]{1,0:T(8,128)S(1)} %get-tuple-element.33.b0), channel_id=1, source_target_pairs={{0,24},{8,0},{16,8},{24,16},{1,25},{9,1},{17,9},{25,17},{2,26},{10... | collective-permute-start | bytes 98312 | tf_op jit(solution)/shard_map/ppermute | solution.py:679
  10.9 3.3 %collective-permute-done.3.b2 = f32[64,128]{1,0:T(8,128)S(1)} collective-permute-done((f32[64,128]{1,0:T(8,128)S(1)}, f32[64,128]{1,0:T(8,128)S(1)}, u32[]{:S(2)}, u32[]{:S(2)}) %collective-permute-start.3) | collective-permute-done | bytes 32800 | tf_op jit(solution)/shard_map/ppermute | solution.py:679
  14.9 2.4 %collective-permute-start.6 = (f32[66,8,128]{2,1,0:T(8,128)S(1)}, f32[66,8,128]{2,1,0:T(8,128)S(1)}, u32[]{:S(2)}, u32[]{:S(2)}) collective-permute-start(f32[66,8,128]{2,1,0:T(8,128)S(1)} %get-tuple-element.35), channel_id=1, source_target_pairs={{8,0},{16,8},{24,16},{0,24},{9,1},{17,9},{25,17},{1,25},{10,2},{18... | collective-permute-start | bytes 811016 | tf_op jit(solution)/shard_map/ppermute | solution.py:672
  17.3 1.7 %collective-permute-start.9 = (f32[4,64,128]{2,1,0:T(8,128)S(1)}, f32[4,64,128]{2,1,0:T(8,128)S(1)}, u32[]{:S(2)}, u32[]{:S(2)}) collective-permute-start(f32[4,64,128]{2,1,0:T(8,128)S(1)} %get-tuple-element.42.h0), channel_id=1, source_target_pairs={{0,96},{32,0},{64,32},{96,64},{1,97},{33,1},{65,33},{97,65},{2,98}... | collective-permute-start | bytes 393224 | tf_op jit(solution)/shard_map/ppermute | solution.py:679
  19.6 2.7 %collective-permute-done.9.h3 = f32[4,64,128]{2,1,0:T(8,128)S(1)} collective-permute-done((f32[4,64,128]{2,1,0:T(8,128)S(1)}, f32[4,64,128]{2,1,0:T(8,128)S(1)}, u32[]{:S(2)}, u32[]{:S(2)}) %collective-permute-start.9) | collective-permute-done | bytes 131104 | tf_op jit(solution)/shard_map/ppermute | solution.py:679
  22.3 2.1 %collective-permute-done.8.h2 = f32[4,64,128]{2,1,0:T(8,128)S(1)} collective-permute-done((f32[4,64,128]{2,1,0:T(8,128)S(1)}, f32[4,64,128]{2,1,0:T(8,128)S(1)}, u32[]{:S(2)}, u32[]{:S(2)}) %collective-permute-start.8) | collective-permute-done | bytes 131104 | tf_op jit(solution)/shard_map/ppermute | solution.py:679
  24.4 1.0 collective-permute-done.7.h1
  25.4 1.1 %pack_lanes.1 = (f32[96,8,128]{2,1,0:T(8,128)S(1)}, f32[96,8,128]{2,1,0:T(8,128)}) custom-call(f32[16,32,128]{2,1,0:T(8,128)S(1)} %get-tuple-element.29.wf, f32[16,32,128]{2,1,0:T(8,128)S(1)} %get-tuple-element.30.wb, f32[17,32,128]{2,1,0:T(8,128)S(1)} %collective-permute-done.xl, f32[17,32,128]{2,1,0:T(8,128)S(1)} %collective-permute-done.1.xu, ...), custom_call_target="tpu_custom_call" | custom-call | tf_op jit(solution)/shard_map/pack_lanes/pallas_call | solution.py:55
  26.6 5.5 %collective-permute-start.10 = (f32[96,8,128]{2,1,0:T(8,128)}, f32[96,8,128]{2,1,0:T(8,128)S(1)}, u32[]{:S(2)}, u32[]{:S(2)}) collective-permute-start(f32[96,8,128]{2,1,0:T(8,128)} %get-tuple-element.39), channel_id=1, source_target_pairs={{0,1},{1,2},{2,3},{3,4},{4,5},{5,6},{6,7},{7,0},{8,9},{9,10},{10,1... | collective-permute-start | bytes 1179656 | tf_op jit(solution)/shard_map/ppermute | solution.py:673
  32.1 5.0 %collective-permute-done.10.zl = f32[96,8,128]{2,1,0:T(8,128)S(1)} collective-permute-done((f32[96,8,128]{2,1,0:T(8,128)}, f32[96,8,128]{2,1,0:T(8,128)S(1)}, u32[]{:S(2)}, u32[]{:S(2)}) %collective-permute-start.10) | collective-permute-done | bytes 393248 | tf_op jit(solution)/shard_map/ppermute | solution.py:673
  37.1 2.2 %collective-permute-done.11.zu = f32[96,8,128]{2,1,0:T(8,128)S(1)} collective-permute-done((f32[96,8,128]{2,1,0:T(8,128)S(1)}, f32[96,8,128]{2,1,0:T(8,128)S(1)}, u32[]{:S(2)}, u32[]{:S(2)}) %collective-permute-start.11) | collective-permute-done | bytes 393248 | tf_op jit(solution)/shard_map/ppermute | solution.py:672
  39.2 7.4 %fine_down.1 = (f32[16,128,128]{2,1,0:T(8,128)S(1)}, f32[8,24,48,128]{3,2,1,0:T(8,128)}, f32[9,26,48,128]{3,2,1,0:T(8,128)}) custom-call(s32[3]{0:T(128)S(1)} %pad_add_fusion.at, f32[16,32,128]{2,1,0:T(8,128)S(1)} %get-tuple-element.29.wf, f32[16,32,128]{2,1,0:T(8,128)S(1)} %get-tuple-element.30.wb, f32[17,32,128]{2,1,0:T(8,128)S(1)} %collective-permute-done.xl, ...), custom_call_target="tpu_custom_call" | custom-call | tf_op jit(solution)/shard_map/fine_down/pallas_call | solution.py:55
  46.7 19.3 %all_to_all.5.g = f32[16,128,128]{2,1,0:T(8,128)S(1)} all-to-all(f32[16,128,128]{2,1,0:T(8,128)S(1)} %get-tuple-element.41), channel_id=1, replica_groups=mesh['gx'=4,'gy'=4,'gz'=8] {'gx','gy'}, dimensions={0} | all-to-all | bytes 2097152 | tf_op jit(solution)/shard_map/all_to_all | solution.py:717
  66.0 6.3 %mid_down.1 = (f32[8,32,128]{2,1,0:T(8,128)S(1)}, f32[2,8,16,32,128]{4,3,2,1,0:T(8,128)}, f32[18,32,128]{2,1,0:T(8,128)S(1)}) custom-call(s32[3]{0:T(128)S(1)} %pad_add_fusion.at, f32[16,128,128]{2,1,0:T(8,128)S(1)} %all_to_all.5.g, f32[4,64,128]{2,1,0:T(8,128)S(1)} %get-tuple-element.42.h0, f32[4,64,128]{2,1,0:T(8,128)S(1)} %collective-permute-done.7.h1, ...), custom_call_target="tpu_custom_call" | custom-call | tf_op jit(solution)/shard_map/mid_down/pallas_call | solution.py:55
  72.3 3.1 %collective-permute-start.15 = (f32[8,32,128]{2,1,0:T(8,128)S(1)}, f32[8,32,128]{2,1,0:T(8,128)S(1)}, u32[]{:S(2)}, u32[]{:S(2)}) collective-permute-start(f32[8,32,128]{2,1,0:T(8,128)S(1)} %get-tuple-element.47.m0), channel_id=1, source_target_pairs={{0,6},{1,7},{2,0},{3,1},{4,2},{5,3},{6,4},{7,5},{8,14},{9,15},{10,... | collective-permute-start | bytes 393224 | tf_op jit(solution)/shard_map/ppermute | solution.py:731
  75.4 1.1 %collective-permute-start.14 = (f32[8,32,128]{2,1,0:T(8,128)S(1)}, f32[8,32,128]{2,1,0:T(8,128)S(1)}, u32[]{:S(2)}, u32[]{:S(2)}) collective-permute-start(f32[8,32,128]{2,1,0:T(8,128)S(1)} %get-tuple-element.47.m0), channel_id=1, source_target_pairs={{0,4},{1,5},{2,6},{3,7},{4,0},{5,1},{6,2},{7,3},{8,12},{9,13},{10,... | collective-permute-start | bytes 393224 | tf_op jit(solution)/shard_map/ppermute | solution.py:731
  77.2 1.2 %collective-permute-start.12 = (f32[8,32,128]{2,1,0:T(8,128)S(1)}, f32[8,32,128]{2,1,0:T(8,128)S(1)}, u32[]{:S(2)}, u32[]{:S(2)}) collective-permute-start(f32[8,32,128]{2,1,0:T(8,128)S(1)} %get-tuple-element.47.m0), channel_id=1, source_target_pairs={{0,1},{1,0},{2,3},{3,2},{4,5},{5,4},{6,7},{7,6},{8,9},{9,8},{10,11... | collective-permute-start | bytes 393224 | tf_op jit(solution)/shard_map/ppermute | solution.py:733
  78.5 2.4 %collective-permute-done.15.m3 = f32[8,32,128]{2,1,0:T(8,128)S(1)} collective-permute-done((f32[8,32,128]{2,1,0:T(8,128)S(1)}, f32[8,32,128]{2,1,0:T(8,128)S(1)}, u32[]{:S(2)}, u32[]{:S(2)}) %collective-permute-start.15) | collective-permute-done | bytes 131104 | tf_op jit(solution)/shard_map/ppermute | solution.py:731
  81.6 3.6 %collective-permute-done.13.m1 = f32[8,32,128]{2,1,0:T(8,128)S(1)} collective-permute-done((f32[8,32,128]{2,1,0:T(8,128)S(1)}, f32[8,32,128]{2,1,0:T(8,128)S(1)}, u32[]{:S(2)}, u32[]{:S(2)}) %collective-permute-start.13) | collective-permute-done | bytes 131104 | tf_op jit(solution)/shard_map/ppermute | solution.py:731
  85.7 1.3 %collective-permute-done.16.q123 = f32[24,32,128]{2,1,0:T(8,128)S(1)} collective-permute-done((f32[24,32,128]{2,1,0:T(8,128)S(1)}, f32[24,32,128]{2,1,0:T(8,128)S(1)}, u32[]{:S(2)}, u32[]{:S(2)}) %collective-permute-start.16) | collective-permute-done | bytes 393248 | tf_op jit(solution)/shard_map/ppermute | solution.py:734
  87.1 15.1 %coarse_up.1 = (f32[16,32,128]{2,1,0:T(8,128)}, f32[16,32,128]{2,1,0:T(8,128)}) custom-call(s32[3]{0:T(128)S(1)} %pad_add_fusion.at, f32[8,32,128]{2,1,0:T(8,128)S(1)} %get-tuple-element.47.m0, f32[8,32,128]{2,1,0:T(8,128)S(1)} %collective-permute-done.13.m1, f32[8,32,128]{2,1,0:T(8,128)S(1)} %collective-permute-done.14.m2, ...), custom_call_target="tpu_custom_call" | custom-call | tf_op jit(solution)/shard_map/coarse_up/pallas_call | solution.py:55
  (20 shorter events, 5.2 us)
Async XLA Ops:
  2.4 12.1 %collective-permute-start = (f32[17,32,128]{2,1,0:T(8,128)S(1)}, f32[17,32,128]{2,1,0:T(8,128)S(1)}, u32[]{:S(2)}, u32[]{:S(2)}) collective-permute-start(f32[17,32,128]{2,1,0:T(8,128)S(1)} %get-tuple-element.31), channel_id=1, source_target_pairs={{0,32},{32,64},{64,96},{96,0},{1,33},{33,65},{65,97},{97,1},{2,34}... | collective-permute-start | bytes 835592 | tf_op jit(solution)/shard_map/ppermute | solution.py:673
  4.9 9.6 %collective-permute-start.1 = (f32[17,32,128]{2,1,0:T(8,128)S(1)}, f32[17,32,128]{2,1,0:T(8,128)S(1)}, u32[]{:S(2)}, u32[]{:S(2)}) collective-permute-start(f32[17,32,128]{2,1,0:T(8,128)S(1)} %get-tuple-element.32), channel_id=1, source_target_pairs={{32,0},{64,32},{96,64},{0,96},{33,1},{65,33},{97,65},{1,97},{34,2}... | collective-permute-start | bytes 835592 | tf_op jit(solution)/shard_map/ppermute | solution.py:672
  7.1 3.8 %collective-permute-start.4 = (f32[64,128]{1,0:T(8,128)S(1)}, f32[64,128]{1,0:T(8,128)S(1)}, u32[]{:S(2)}, u32[]{:S(2)}) collective-permute-start(f32[64,128]{1,0:T(8,128)S(1)} %get-tuple-element.33.b0), channel_id=1, source_target_pairs={{0,24},{8,0},{16,8},{24,16},{1,25},{9,1},{17,9},{25,17},{2,26},{10... | collective-permute-start | bytes 98312 | tf_op jit(solution)/shard_map/ppermute | solution.py:679
  9.9 4.3 %collective-permute-start.3 = (f32[64,128]{1,0:T(8,128)S(1)}, f32[64,128]{1,0:T(8,128)S(1)}, u32[]{:S(2)}, u32[]{:S(2)}) collective-permute-start(f32[64,128]{1,0:T(8,128)S(1)} %get-tuple-element.33.b0), channel_id=1, source_target_pairs={{0,16},{8,24},{16,0},{24,8},{1,17},{9,25},{17,1},{25,9},{2,18},{10... | collective-permute-start | bytes 98312 | tf_op jit(solution)/shard_map/ppermute | solution.py:679
  10.2 4.3 %collective-permute-start.2 = (f32[64,128]{1,0:T(8,128)S(1)}, f32[64,128]{1,0:T(8,128)S(1)}, u32[]{:S(2)}, u32[]{:S(2)}) collective-permute-start(f32[64,128]{1,0:T(8,128)S(1)} %get-tuple-element.33.b0), channel_id=1, source_target_pairs={{0,8},{8,16},{16,24},{24,0},{1,9},{9,17},{17,25},{25,1},{2,10},{10... | collective-permute-start | bytes 98312 | tf_op jit(solution)/shard_map/ppermute | solution.py:679
  14.6 10.9 %collective-permute-start.5 = (f32[66,8,128]{2,1,0:T(8,128)S(1)}, f32[66,8,128]{2,1,0:T(8,128)S(1)}, u32[]{:S(2)}, u32[]{:S(2)}) collective-permute-start(f32[66,8,128]{2,1,0:T(8,128)S(1)} %get-tuple-element.34), channel_id=1, source_target_pairs={{0,8},{8,16},{16,24},{24,0},{1,9},{9,17},{17,25},{25,1},{2,10},{10... | collective-permute-start | bytes 811016 | tf_op jit(solution)/shard_map/ppermute | solution.py:673
  14.9 10.6 %collective-permute-start.6 = (f32[66,8,128]{2,1,0:T(8,128)S(1)}, f32[66,8,128]{2,1,0:T(8,128)S(1)}, u32[]{:S(2)}, u32[]{:S(2)}) collective-permute-start(f32[66,8,128]{2,1,0:T(8,128)S(1)} %get-tuple-element.35), channel_id=1, source_target_pairs={{8,0},{16,8},{24,16},{0,24},{9,1},{17,9},{25,17},{1,25},{10,2},{18... | collective-permute-start | bytes 811016 | tf_op jit(solution)/shard_map/ppermute | solution.py:672
  17.3 5.0 %collective-permute-start.9 = (f32[4,64,128]{2,1,0:T(8,128)S(1)}, f32[4,64,128]{2,1,0:T(8,128)S(1)}, u32[]{:S(2)}, u32[]{:S(2)}) collective-permute-start(f32[4,64,128]{2,1,0:T(8,128)S(1)} %get-tuple-element.42.h0), channel_id=1, source_target_pairs={{0,96},{32,0},{64,32},{96,64},{1,97},{33,1},{65,33},{97,65},{2,98}... | collective-permute-start | bytes 393224 | tf_op jit(solution)/shard_map/ppermute | solution.py:679
  19.0 5.4 %collective-permute-start.8 = (f32[4,64,128]{2,1,0:T(8,128)S(1)}, f32[4,64,128]{2,1,0:T(8,128)S(1)}, u32[]{:S(2)}, u32[]{:S(2)}) collective-permute-start(f32[4,64,128]{2,1,0:T(8,128)S(1)} %get-tuple-element.42.h0), channel_id=1, source_target_pairs={{0,64},{32,96},{64,0},{96,32},{1,65},{33,97},{65,1},{97,33},{2,66}... | collective-permute-start | bytes 393224 | tf_op jit(solution)/shard_map/ppermute | solution.py:679
  19.0 6.4 %collective-permute-start.7 = (f32[4,64,128]{2,1,0:T(8,128)S(1)}, f32[4,64,128]{2,1,0:T(8,128)S(1)}, u32[]{:S(2)}, u32[]{:S(2)}) collective-permute-start(f32[4,64,128]{2,1,0:T(8,128)S(1)} %get-tuple-element.42.h0), channel_id=1, source_target_pairs={{0,32},{32,64},{64,96},{96,0},{1,33},{33,65},{65,97},{97,1},{2,34}... | collective-permute-start | bytes 393224 | tf_op jit(solution)/shard_map/ppermute | solution.py:679
  26.6 10.5 %collective-permute-start.10 = (f32[96,8,128]{2,1,0:T(8,128)}, f32[96,8,128]{2,1,0:T(8,128)S(1)}, u32[]{:S(2)}, u32[]{:S(2)}) collective-permute-start(f32[96,8,128]{2,1,0:T(8,128)} %get-tuple-element.39), channel_id=1, source_target_pairs={{0,1},{1,2},{2,3},{3,4},{4,5},{5,6},{6,7},{7,0},{8,9},{9,10},{10,1... | collective-permute-start | bytes 1179656 | tf_op jit(solution)/shard_map/ppermute | solution.py:673
  32.0 7.2 %collective-permute-start.11 = (f32[96,8,128]{2,1,0:T(8,128)S(1)}, f32[96,8,128]{2,1,0:T(8,128)S(1)}, u32[]{:S(2)}, u32[]{:S(2)}) collective-permute-start(f32[96,8,128]{2,1,0:T(8,128)S(1)} %get-tuple-element.40), channel_id=1, source_target_pairs={{1,0},{2,1},{3,2},{4,3},{5,4},{6,5},{7,6},{0,7},{9,8},{10,9},{11,1... | collective-permute-start | bytes 1179656 | tf_op jit(solution)/shard_map/ppermute | solution.py:672
  72.3 8.5 %collective-permute-start.15 = (f32[8,32,128]{2,1,0:T(8,128)S(1)}, f32[8,32,128]{2,1,0:T(8,128)S(1)}, u32[]{:S(2)}, u32[]{:S(2)}) collective-permute-start(f32[8,32,128]{2,1,0:T(8,128)S(1)} %get-tuple-element.47.m0), channel_id=1, source_target_pairs={{0,6},{1,7},{2,0},{3,1},{4,2},{5,3},{6,4},{7,5},{8,14},{9,15},{10,... | collective-permute-start | bytes 393224 | tf_op jit(solution)/shard_map/ppermute | solution.py:731
  75.4 6.1 %collective-permute-start.14 = (f32[8,32,128]{2,1,0:T(8,128)S(1)}, f32[8,32,128]{2,1,0:T(8,128)S(1)}, u32[]{:S(2)}, u32[]{:S(2)}) collective-permute-start(f32[8,32,128]{2,1,0:T(8,128)S(1)} %get-tuple-element.47.m0), channel_id=1, source_target_pairs={{0,4},{1,5},{2,6},{3,7},{4,0},{5,1},{6,2},{7,3},{8,12},{9,13},{10,... | collective-permute-start | bytes 393224 | tf_op jit(solution)/shard_map/ppermute | solution.py:731
  76.5 8.7 %collective-permute-start.13 = (f32[8,32,128]{2,1,0:T(8,128)S(1)}, f32[8,32,128]{2,1,0:T(8,128)S(1)}, u32[]{:S(2)}, u32[]{:S(2)}) collective-permute-start(f32[8,32,128]{2,1,0:T(8,128)S(1)} %get-tuple-element.47.m0), channel_id=1, source_target_pairs={{0,2},{1,3},{2,4},{3,5},{4,6},{5,7},{6,0},{7,1},{8,10},{9,11},{10,... | collective-permute-start | bytes 393224 | tf_op jit(solution)/shard_map/ppermute | solution.py:731
  77.2 7.9 %collective-permute-start.12 = (f32[8,32,128]{2,1,0:T(8,128)S(1)}, f32[8,32,128]{2,1,0:T(8,128)S(1)}, u32[]{:S(2)}, u32[]{:S(2)}) collective-permute-start(f32[8,32,128]{2,1,0:T(8,128)S(1)} %get-tuple-element.47.m0), channel_id=1, source_target_pairs={{0,1},{1,0},{2,3},{3,2},{4,5},{5,4},{6,7},{7,6},{8,9},{9,8},{10,11... | collective-permute-start | bytes 393224 | tf_op jit(solution)/shard_map/ppermute | solution.py:733
  85.2 1.9 %collective-permute-start.16 = (f32[24,32,128]{2,1,0:T(8,128)S(1)}, f32[24,32,128]{2,1,0:T(8,128)S(1)}, u32[]{:S(2)}, u32[]{:S(2)}) collective-permute-start(f32[24,32,128]{2,1,0:T(8,128)S(1)} %pad_maximum_fusion.1), channel_id=1, source_target_pairs={{0,1},{1,0},{2,3},{3,2},{4,5},{5,4},{6,7},{7,6},{8,9},{9,8},{10,11... | collective-permute-start | bytes 1179656 | tf_op jit(solution)/shard_map/ppermute | solution.py:734

commit v9 on v7

--- a/solution.py
+++ b/solution.py
@@ -697,9 +697,10 @@
     y_slab = arr(66, 8, 128)
     lo, hi, b1 = call(pack_rows, [(y_slab, y_slab, arr(4, 64, 128))], (wf, wb, xl, xu, *b1), limit=8)
     yl, yu = around(lo, hi, "gy")
-    yl, yu, *b1 = lax.optimization_barrier((yl, yu, b1, *beyond(b1, "gx")))
+    b1 = [b1] + beyond(b1, "gx")
     lo, hi = call(pack_lanes, [(arr(96, 8, 128),) * 2], (wf, wb, xl, xu, yl, yu), limit=8)
     zl, zu = around(lo, hi, "gz")
+    zl, zu, *b1 = lax.optimization_barrier((zl, zu, *b1))
 
     colour0 = pltpu.VMEM((34, 64, 128), F32)
     right0 = pltpu.VMEM((32, 48, 128), F32)

time: 102 us -> 100 us (0.980)
  waiting for transfers between devices: 21.4 us -> 14.6 us
  starting transfers between devices: 28.4 us -> 33.5 us
    ppermute x4, starting transfers between devices: 4.58 us -> 8.77 us  [body(): pair = [lax.ppermute(w, 'gz', [(i, i ^ 1) for i in range(8)]) for w in mine]]
    ppermute x3, waiting for transfers between devices: 3.82 us -> 0.01 us  [body(): lax.ppermute(w2, 'gz', [(i, (i + d) % 8) for i in range(8)])]
    ppermute x3, waiting for transfers between devices: 2.17 us -> 0.01 us  [around(): lax.ppermute(lo, axis, [((i + 1) % count, i) for i in range(count)])]
    ppermute x3, starting transfers between devices: 4.89 us -> 6.48 us  [body(): lax.ppermute(w2, 'gz', [(i, (i + d) % 8) for i in range(8)])]
    ppermute x3, waiting for transfers between devices: 4.96 us -> 3.85 us  [around(): lax.ppermute(hi, axis, [(i, (i + 1) % count) for i in range(count)])]
  transfers between devices with their start and end apart: 19 -> 19, of which waited for: 10 -> 7; matrix products, arithmetic and copies ran while one was open for 0% -> 0% of each run, Pallas kernels for 0% -> 0%
where the time goes in v9:
time: 100 us; the launch traced here: 99.9 us
  starting transfers between devices  33.5 us (34%)
  Pallas kernels  30.7 us (31%)
  blocking collectives  19.1 us (19%)
  waiting for transfers between devices  14.6 us (15%)
  other arithmetic  1.14 us (1%)
    pallas_call x6, Pallas kernels, call(): pl.pallas_call(kernel, out_shape=out[0], in_specs=specs or [vmem] * len(a...  30.7 us
    all_to_all x1, blocking collectives, body(): g = lax.all_to_all(g, ('gx', 'gy'), 0, 0, tiled=True)  19.1 us
    ppermute x6, waiting for transfers between devices, beyond(): lax.ppermute(x, axis, [(i, (i + d) % count) for i in range(count)])  9.74 us
    ppermute x4, starting transfers between devices, body(): pair = [lax.ppermute(w, 'gz', [(i, i ^ 1) for i in range(8)]) for w in mine]  8.77 us
    ppermute x3, starting transfers between devices, around(): lax.ppermute(hi, axis, [(i, (i + 1) % count) for i in range(count)])  7.51 us
    ppermute x3, starting transfers between devices, body(): lax.ppermute(w2, 'gz', [(i, (i + d) % 8) for i in range(8)])  6.48 us
    ppermute x6, starting transfers between devices, beyond(): lax.ppermute(x, axis, [(i, (i + d) % count) for i in range(count)])  6.09 us
    ppermute x3, starting transfers between devices, around(): lax.ppermute(lo, axis, [((i + 1) % count, i) for i in range(count)])  4.64 us
  transfers between devices with their start and end apart: 19, of which 7 were waited for; matrix products, arithmetic and copies ran while one was open for 0% of the time, Pallas kernels for 0%

profile of v9, /device:TPU:1, one launch (start us, length us, event | category | flops | bytes accessed | tf_op | source)
XLA Modules:
  0.0 99.9 jit_solution(9057718582731804003)
XLA Ops:
  0.6 1.1 %pad_maximum_fusion.both_ref = f32[32,32,128]{2,1,0:T(8,128)S(1)} fusion(f32[16,32,128]{2,1,0:T(8,128)} %param.3, f32[16,32,128]{2,1,0:T(8,128)} %param.2), kind=kLoop, calls=%fused_computation | loop fusion | flops 131072 | bytes 1048576 | tf_op jit(solution)/shard_map/concatenate | solution.py:690
  2.4 2.5 %collective-permute-start = (f32[17,32,128]{2,1,0:T(8,128)S(1)}, f32[17,32,128]{2,1,0:T(8,128)S(1)}, u32[]{:S(2)}, u32[]{:S(2)}) collective-permute-start(f32[17,32,128]{2,1,0:T(8,128)S(1)} %get-tuple-element.26), channel_id=1, source_target_pairs={{0,32},{32,64},{64,96},{96,0},{1,33},{33,65},{65,97},{97,1},{2,34}... | collective-permute-start | bytes 835592 | tf_op jit(solution)/shard_map/ppermute | solution.py:672
  4.9 2.2 %collective-permute-start.1 = (f32[17,32,128]{2,1,0:T(8,128)S(1)}, f32[17,32,128]{2,1,0:T(8,128)S(1)}, u32[]{:S(2)}, u32[]{:S(2)}) collective-permute-start(f32[17,32,128]{2,1,0:T(8,128)S(1)} %get-tuple-element.27), channel_id=1, source_target_pairs={{32,0},{64,32},{96,64},{0,96},{33,1},{65,33},{97,65},{1,97},{34,2}... | collective-permute-start | bytes 835592 | tf_op jit(solution)/shard_map/ppermute | solution.py:671
  7.1 2.7 %collective-permute-start.4 = (f32[64,128]{1,0:T(8,128)S(1)}, f32[64,128]{1,0:T(8,128)S(1)}, u32[]{:S(2)}, u32[]{:S(2)}) collective-permute-start(f32[64,128]{1,0:T(8,128)S(1)} %get-tuple-element.28.b0), channel_id=1, source_target_pairs={{0,24},{8,0},{16,8},{24,16},{1,25},{9,1},{17,9},{25,17},{2,26},{10... | collective-permute-start | bytes 98312 | tf_op jit(solution)/shard_map/ppermute | solution.py:678
  10.9 3.3 %collective-permute-done.3.b2 = f32[64,128]{1,0:T(8,128)S(1)} collective-permute-done((f32[64,128]{1,0:T(8,128)S(1)}, f32[64,128]{1,0:T(8,128)S(1)}, u32[]{:S(2)}, u32[]{:S(2)}) %collective-permute-start.3) | collective-permute-done | bytes 32800 | tf_op jit(solution)/shard_map/ppermute | solution.py:678
  14.9 2.4 %collective-permute-start.6 = (f32[66,8,128]{2,1,0:T(8,128)S(1)}, f32[66,8,128]{2,1,0:T(8,128)S(1)}, u32[]{:S(2)}, u32[]{:S(2)}) collective-permute-start(f32[66,8,128]{2,1,0:T(8,128)S(1)} %get-tuple-element.30), channel_id=1, source_target_pairs={{8,0},{16,8},{24,16},{0,24},{9,1},{17,9},{25,17},{1,25},{10,2},{18... | collective-permute-start | bytes 811016 | tf_op jit(solution)/shard_map/ppermute | solution.py:671
  17.3 3.8 %collective-permute-done.5.yl = f32[66,8,128]{2,1,0:T(8,128)S(1)} collective-permute-done((f32[66,8,128]{2,1,0:T(8,128)S(1)}, f32[66,8,128]{2,1,0:T(8,128)S(1)}, u32[]{:S(2)}, u32[]{:S(2)}) %collective-permute-start.5) | collective-permute-done | bytes 270368 | tf_op jit(solution)/shard_map/ppermute | solution.py:672
  21.2 1.1 %pack_lanes.1 = (f32[96,8,128]{2,1,0:T(8,128)S(1)}, f32[96,8,128]{2,1,0:T(8,128)}) custom-call(f32[16,32,128]{2,1,0:T(8,128)S(1)} %get-tuple-element.24.wf, f32[16,32,128]{2,1,0:T(8,128)S(1)} %get-tuple-element.25.wb, f32[17,32,128]{2,1,0:T(8,128)S(1)} %collective-permute-done.xl, f32[17,32,128]{2,1,0:T(8,128)S(1)} %collective-permute-done.1.xu, ...), custom_call_target="tpu_custom_call" | custom-call | tf_op jit(solution)/shard_map/pack_lanes/pallas_call | solution.py:55
  22.3 4.7 %collective-permute-start.7 = (f32[96,8,128]{2,1,0:T(8,128)}, f32[96,8,128]{2,1,0:T(8,128)S(1)}, u32[]{:S(2)}, u32[]{:S(2)}) collective-permute-start(f32[96,8,128]{2,1,0:T(8,128)} %get-tuple-element.31), channel_id=1, source_target_pairs={{0,1},{1,2},{2,3},{3,4},{4,5},{5,6},{6,7},{7,0},{8,9},{9,10},{10,1... | collective-permute-start | bytes 1179656 | tf_op jit(solution)/shard_map/ppermute | solution.py:672
  27.0 1.7 %collective-permute-start.11 = (f32[4,64,128]{2,1,0:T(8,128)S(1)}, f32[4,64,128]{2,1,0:T(8,128)S(1)}, u32[]{:S(2)}, u32[]{:S(2)}) collective-permute-start(f32[4,64,128]{2,1,0:T(8,128)S(1)} %get-tuple-element.37.h0), channel_id=1, source_target_pairs={{0,96},{32,0},{64,32},{96,64},{1,97},{33,1},{65,33},{97,65},{2,98}... | collective-permute-start | bytes 393224 | tf_op jit(solution)/shard_map/ppermute | solution.py:678
  29.4 2.5 %collective-permute-done.11.h3 = f32[4,64,128]{2,1,0:T(8,128)S(1)} collective-permute-done((f32[4,64,128]{2,1,0:T(8,128)S(1)}, f32[4,64,128]{2,1,0:T(8,128)S(1)}, u32[]{:S(2)}, u32[]{:S(2)}) %collective-permute-start.11) | collective-permute-done | bytes 131104 | tf_op jit(solution)/shard_map/ppermute | solution.py:678
  31.9 2.2 %collective-permute-done.10.h2 = f32[4,64,128]{2,1,0:T(8,128)S(1)} collective-permute-done((f32[4,64,128]{2,1,0:T(8,128)S(1)}, f32[4,64,128]{2,1,0:T(8,128)S(1)}, u32[]{:S(2)}, u32[]{:S(2)}) %collective-permute-start.10) | collective-permute-done | bytes 131104 | tf_op jit(solution)/shard_map/ppermute | solution.py:678
  34.1 1.4 %collective-permute-done.9.h1 = f32[4,64,128]{2,1,0:T(8,128)S(1)} collective-permute-done((f32[4,64,128]{2,1,0:T(8,128)S(1)}, f32[4,64,128]{2,1,0:T(8,128)S(1)}, u32[]{:S(2)}, u32[]{:S(2)}) %collective-permute-start.9) | collective-permute-done | bytes 131104 | tf_op jit(solution)/shard_map/ppermute | solution.py:678
  35.5 7.4 %fine_down.1 = (f32[16,128,128]{2,1,0:T(8,128)S(1)}, f32[8,24,48,128]{3,2,1,0:T(8,128)}, f32[9,26,48,128]{3,2,1,0:T(8,128)}) custom-call(s32[3]{0:T(128)S(1)} %pad_add_fusion.at, f32[16,32,128]{2,1,0:T(8,128)S(1)} %get-tuple-element.24.wf, f32[16,32,128]{2,1,0:T(8,128)S(1)} %get-tuple-element.25.wb, f32[17,32,128]{2,1,0:T(8,128)S(1)} %collective-permute-done.xl, ...), custom_call_target="tpu_custom_call" | custom-call | tf_op jit(solution)/shard_map/fine_down/pallas_call | solution.py:55
  43.0 19.1 %all_to_all.5.g = f32[16,128,128]{2,1,0:T(8,128)S(1)} all-to-all(f32[16,128,128]{2,1,0:T(8,128)S(1)} %get-tuple-element.36), channel_id=1, replica_groups=mesh['gx'=4,'gy'=4,'gz'=8] {'gx','gy'}, dimensions={0} | all-to-all | bytes 2097152 | tf_op jit(solution)/shard_map/all_to_all | solution.py:717
  62.1 6.3 %mid_down.1 = (f32[8,32,128]{2,1,0:T(8,128)S(1)}, f32[2,8,16,32,128]{4,3,2,1,0:T(8,128)}, f32[18,32,128]{2,1,0:T(8,128)S(1)}) custom-call(s32[3]{0:T(128)S(1)} %pad_add_fusion.at, f32[16,128,128]{2,1,0:T(8,128)S(1)} %all_to_all.5.g, f32[4,64,128]{2,1,0:T(8,128)S(1)} %get-tuple-element.37.h0, f32[4,64,128]{2,1,0:T(8,128)S(1)} %collective-permute-done.9.h1, ...), custom_call_target="tpu_custom_call" | custom-call | tf_op jit(solution)/shard_map/mid_down/pallas_call | solution.py:55
  68.4 3.7 %collective-permute-start.14 = (f32[8,32,128]{2,1,0:T(8,128)S(1)}, f32[8,32,128]{2,1,0:T(8,128)S(1)}, u32[]{:S(2)}, u32[]{:S(2)}) collective-permute-start(f32[8,32,128]{2,1,0:T(8,128)S(1)} %get-tuple-element.41.m0), channel_id=1, source_target_pairs={{0,6},{1,7},{2,0},{3,1},{4,2},{5,3},{6,4},{7,5},{8,14},{9,15},{10,... | collective-permute-start | bytes 393224 | tf_op jit(solution)/shard_map/ppermute | solution.py:731
  72.1 2.5 %collective-permute-start.13 = (f32[8,32,128]{2,1,0:T(8,128)S(1)}, f32[8,32,128]{2,1,0:T(8,128)S(1)}, u32[]{:S(2)}, u32[]{:S(2)}) collective-permute-start(f32[8,32,128]{2,1,0:T(8,128)S(1)} %get-tuple-element.41.m0), channel_id=1, source_target_pairs={{0,4},{1,5},{2,6},{3,7},{4,0},{5,1},{6,2},{7,3},{8,12},{9,13},{10,... | collective-permute-start | bytes 393224 | tf_op jit(solution)/shard_map/ppermute | solution.py:731
  74.9 3.2 %collective-permute-start.15 = (f32[8,32,128]{2,1,0:T(8,128)S(1)}, f32[8,32,128]{2,1,0:T(8,128)S(1)}, u32[]{:S(2)}, u32[]{:S(2)}) collective-permute-start(f32[8,32,128]{2,1,0:T(8,128)S(1)} %get-tuple-element.41.m0), channel_id=1, source_target_pairs={{0,1},{1,0},{2,3},{3,2},{4,5},{5,4},{6,7},{7,6},{8,9},{9,8},{10,11... | collective-permute-start | bytes 393224 | tf_op jit(solution)/shard_map/ppermute | solution.py:732
  78.1 1.3 %collective-permute-start.18 = (f32[8,32,128]{2,1,0:T(8,128)S(1)}, f32[8,32,128]{2,1,0:T(8,128)S(1)}, u32[]{:S(2)}, u32[]{:S(2)}) collective-permute-start(f32[8,32,128]{2,1,0:T(8,128)S(1)} %collective-permute-done.14.m3), channel_id=1, source_target_pairs={{0,1},{1,0},{2,3},{3,2},{4,5},{5,4},{6,7},{7,6},{8,9},{9,8},{10,11... | collective-permute-start | bytes 393224 | tf_op jit(solution)/shard_map/ppermute | solution.py:732
  79.3 2.4 %collective-permute-start.17 = (f32[8,32,128]{2,1,0:T(8,128)S(1)}, f32[8,32,128]{2,1,0:T(8,128)S(1)}, u32[]{:S(2)}, u32[]{:S(2)}) collective-permute-start(f32[8,32,128]{2,1,0:T(8,128)S(1)} %collective-permute-done.13.m2), channel_id=1, source_target_pairs={{0,1},{1,0},{2,3},{3,2},{4,5},{5,4},{6,7},{7,6},{8,9},{9,8},{10,11... | collective-permute-start | bytes 393224 | tf_op jit(solution)/shard_map/ppermute | solution.py:732
  81.8 1.9 %collective-permute-start.16 = (f32[8,32,128]{2,1,0:T(8,128)S(1)}, f32[8,32,128]{2,1,0:T(8,128)S(1)}, u32[]{:S(2)}, u32[]{:S(2)}) collective-permute-start(f32[8,32,128]{2,1,0:T(8,128)S(1)} %collective-permute-done.12.m1), channel_id=1, source_target_pairs={{0,1},{1,0},{2,3},{3,2},{4,5},{5,4},{6,7},{7,6},{8,9},{9,8},{10,11... | collective-permute-start | bytes 393224 | tf_op jit(solution)/shard_map/ppermute | solution.py:732
  83.7 1.0 collective-permute-done.16.q1
  84.7 15.0 %coarse_up.1 = (f32[16,32,128]{2,1,0:T(8,128)}, f32[16,32,128]{2,1,0:T(8,128)}) custom-call(s32[3]{0:T(128)S(1)} %pad_add_fusion.at, f32[8,32,128]{2,1,0:T(8,128)S(1)} %get-tuple-element.41.m0, f32[8,32,128]{2,1,0:T(8,128)S(1)} %collective-permute-done.12.m1, f32[8,32,128]{2,1,0:T(8,128)S(1)} %collective-permute-done.13.m2, ...), custom_call_target="tpu_custom_call" | custom-call | tf_op jit(solution)/shard_map/coarse_up/pallas_call | solution.py:55
  (23 shorter events, 3.5 us)
Async XLA Ops:
  2.4 12.1 %collective-permute-start = (f32[17,32,128]{2,1,0:T(8,128)S(1)}, f32[17,32,128]{2,1,0:T(8,128)S(1)}, u32[]{:S(2)}, u32[]{:S(2)}) collective-permute-start(f32[17,32,128]{2,1,0:T(8,128)S(1)} %get-tuple-element.26), channel_id=1, source_target_pairs={{0,32},{32,64},{64,96},{96,0},{1,33},{33,65},{65,97},{97,1},{2,34}... | collective-permute-start | bytes 835592 | tf_op jit(solution)/shard_map/ppermute | solution.py:672
  4.9 9.6 %collective-permute-start.1 = (f32[17,32,128]{2,1,0:T(8,128)S(1)}, f32[17,32,128]{2,1,0:T(8,128)S(1)}, u32[]{:S(2)}, u32[]{:S(2)}) collective-permute-start(f32[17,32,128]{2,1,0:T(8,128)S(1)} %get-tuple-element.27), channel_id=1, source_target_pairs={{32,0},{64,32},{96,64},{0,96},{33,1},{65,33},{97,65},{1,97},{34,2}... | collective-permute-start | bytes 835592 | tf_op jit(solution)/shard_map/ppermute | solution.py:671
  7.1 3.8 %collective-permute-start.4 = (f32[64,128]{1,0:T(8,128)S(1)}, f32[64,128]{1,0:T(8,128)S(1)}, u32[]{:S(2)}, u32[]{:S(2)}) collective-permute-start(f32[64,128]{1,0:T(8,128)S(1)} %get-tuple-element.28.b0), channel_id=1, source_target_pairs={{0,24},{8,0},{16,8},{24,16},{1,25},{9,1},{17,9},{25,17},{2,26},{10... | collective-permute-start | bytes 98312 | tf_op jit(solution)/shard_map/ppermute | solution.py:678
  9.9 4.3 %collective-permute-start.3 = (f32[64,128]{1,0:T(8,128)S(1)}, f32[64,128]{1,0:T(8,128)S(1)}, u32[]{:S(2)}, u32[]{:S(2)}) collective-permute-start(f32[64,128]{1,0:T(8,128)S(1)} %get-tuple-element.28.b0), channel_id=1, source_target_pairs={{0,16},{8,24},{16,0},{24,8},{1,17},{9,25},{17,1},{25,9},{2,18},{10... | collective-permute-start | bytes 98312 | tf_op jit(solution)/shard_map/ppermute | solution.py:678
  10.2 4.3 %collective-permute-start.2 = (f32[64,128]{1,0:T(8,128)S(1)}, f32[64,128]{1,0:T(8,128)S(1)}, u32[]{:S(2)}, u32[]{:S(2)}) collective-permute-start(f32[64,128]{1,0:T(8,128)S(1)} %get-tuple-element.28.b0), channel_id=1, source_target_pairs={{0,8},{8,16},{16,24},{24,0},{1,9},{9,17},{17,25},{25,1},{2,10},{10... | collective-permute-start | bytes 98312 | tf_op jit(solution)/shard_map/ppermute | solution.py:678
  14.6 6.6 %collective-permute-start.5 = (f32[66,8,128]{2,1,0:T(8,128)S(1)}, f32[66,8,128]{2,1,0:T(8,128)S(1)}, u32[]{:S(2)}, u32[]{:S(2)}) collective-permute-start(f32[66,8,128]{2,1,0:T(8,128)S(1)} %get-tuple-element.29), channel_id=1, source_target_pairs={{0,8},{8,16},{16,24},{24,0},{1,9},{9,17},{17,25},{25,1},{2,10},{10... | collective-permute-start | bytes 811016 | tf_op jit(solution)/shard_map/ppermute | solution.py:672
  14.9 6.3 %collective-permute-start.6 = (f32[66,8,128]{2,1,0:T(8,128)S(1)}, f32[66,8,128]{2,1,0:T(8,128)S(1)}, u32[]{:S(2)}, u32[]{:S(2)}) collective-permute-start(f32[66,8,128]{2,1,0:T(8,128)S(1)} %get-tuple-element.30), channel_id=1, source_target_pairs={{8,0},{16,8},{24,16},{0,24},{9,1},{17,9},{25,17},{1,25},{10,2},{18... | collective-permute-start | bytes 811016 | tf_op jit(solution)/shard_map/ppermute | solution.py:671
  22.3 13.2 %collective-permute-start.7 = (f32[96,8,128]{2,1,0:T(8,128)}, f32[96,8,128]{2,1,0:T(8,128)S(1)}, u32[]{:S(2)}, u32[]{:S(2)}) collective-permute-start(f32[96,8,128]{2,1,0:T(8,128)} %get-tuple-element.31), channel_id=1, source_target_pairs={{0,1},{1,2},{2,3},{3,4},{4,5},{5,6},{6,7},{7,0},{8,9},{9,10},{10,1... | collective-permute-start | bytes 1179656 | tf_op jit(solution)/shard_map/ppermute | solution.py:672
  27.0 8.6 %collective-permute-start.8 = (f32[96,8,128]{2,1,0:T(8,128)S(1)}, f32[96,8,128]{2,1,0:T(8,128)S(1)}, u32[]{:S(2)}, u32[]{:S(2)}) collective-permute-start(f32[96,8,128]{2,1,0:T(8,128)S(1)} %get-tuple-element.32), channel_id=1, source_target_pairs={{1,0},{2,1},{3,2},{4,3},{5,4},{6,5},{7,6},{0,7},{9,8},{10,9},{11,1... | collective-permute-start | bytes 1179656 | tf_op jit(solution)/shard_map/ppermute | solution.py:671
  27.0 4.9 %collective-permute-start.11 = (f32[4,64,128]{2,1,0:T(8,128)S(1)}, f32[4,64,128]{2,1,0:T(8,128)S(1)}, u32[]{:S(2)}, u32[]{:S(2)}) collective-permute-start(f32[4,64,128]{2,1,0:T(8,128)S(1)} %get-tuple-element.37.h0), channel_id=1, source_target_pairs={{0,96},{32,0},{64,32},{96,64},{1,97},{33,1},{65,33},{97,65},{2,98}... | collective-permute-start | bytes 393224 | tf_op jit(solution)/shard_map/ppermute | solution.py:678
  28.6 5.4 %collective-permute-start.10 = (f32[4,64,128]{2,1,0:T(8,128)S(1)}, f32[4,64,128]{2,1,0:T(8,128)S(1)}, u32[]{:S(2)}, u32[]{:S(2)}) collective-permute-start(f32[4,64,128]{2,1,0:T(8,128)S(1)} %get-tuple-element.37.h0), channel_id=1, source_target_pairs={{0,64},{32,96},{64,0},{96,32},{1,65},{33,97},{65,1},{97,33},{2,66}... | collective-permute-start | bytes 393224 | tf_op jit(solution)/shard_map/ppermute | solution.py:678
  28.6 6.9 %collective-permute-start.9 = (f32[4,64,128]{2,1,0:T(8,128)S(1)}, f32[4,64,128]{2,1,0:T(8,128)S(1)}, u32[]{:S(2)}, u32[]{:S(2)}) collective-permute-start(f32[4,64,128]{2,1,0:T(8,128)S(1)} %get-tuple-element.37.h0), channel_id=1, source_target_pairs={{0,32},{32,64},{64,96},{96,0},{1,33},{33,65},{65,97},{97,1},{2,34}... | collective-permute-start | bytes 393224 | tf_op jit(solution)/shard_map/ppermute | solution.py:678
  68.4 9.7 %collective-permute-start.14 = (f32[8,32,128]{2,1,0:T(8,128)S(1)}, f32[8,32,128]{2,1,0:T(8,128)S(1)}, u32[]{:S(2)}, u32[]{:S(2)}) collective-permute-start(f32[8,32,128]{2,1,0:T(8,128)S(1)} %get-tuple-element.41.m0), channel_id=1, source_target_pairs={{0,6},{1,7},{2,0},{3,1},{4,2},{5,3},{6,4},{7,5},{8,14},{9,15},{10,... | collective-permute-start | bytes 393224 | tf_op jit(solution)/shard_map/ppermute | solution.py:731
  72.1 7.3 %collective-permute-start.13 = (f32[8,32,128]{2,1,0:T(8,128)S(1)}, f32[8,32,128]{2,1,0:T(8,128)S(1)}, u32[]{:S(2)}, u32[]{:S(2)}) collective-permute-start(f32[8,32,128]{2,1,0:T(8,128)S(1)} %get-tuple-element.41.m0), channel_id=1, source_target_pairs={{0,4},{1,5},{2,6},{3,7},{4,0},{5,1},{6,2},{7,3},{8,12},{9,13},{10,... | collective-permute-start | bytes 393224 | tf_op jit(solution)/shard_map/ppermute | solution.py:731
  74.6 7.2 %collective-permute-start.12 = (f32[8,32,128]{2,1,0:T(8,128)S(1)}, f32[8,32,128]{2,1,0:T(8,128)S(1)}, u32[]{:S(2)}, u32[]{:S(2)}) collective-permute-start(f32[8,32,128]{2,1,0:T(8,128)S(1)} %get-tuple-element.41.m0), channel_id=1, source_target_pairs={{0,2},{1,3},{2,4},{3,5},{4,6},{5,7},{6,0},{7,1},{8,10},{9,11},{10,... | collective-permute-start | bytes 393224 | tf_op jit(solution)/shard_map/ppermute | solution.py:731
  74.9 8.8 %collective-permute-start.15 = (f32[8,32,128]{2,1,0:T(8,128)S(1)}, f32[8,32,128]{2,1,0:T(8,128)S(1)}, u32[]{:S(2)}, u32[]{:S(2)}) collective-permute-start(f32[8,32,128]{2,1,0:T(8,128)S(1)} %get-tuple-element.41.m0), channel_id=1, source_target_pairs={{0,1},{1,0},{2,3},{3,2},{4,5},{5,4},{6,7},{7,6},{8,9},{9,8},{10,11... | collective-permute-start | bytes 393224 | tf_op jit(solution)/shard_map/ppermute | solution.py:732
  78.1 5.6 %collective-permute-start.18 = (f32[8,32,128]{2,1,0:T(8,128)S(1)}, f32[8,32,128]{2,1,0:T(8,128)S(1)}, u32[]{:S(2)}, u32[]{:S(2)}) collective-permute-start(f32[8,32,128]{2,1,0:T(8,128)S(1)} %collective-permute-done.14.m3), channel_id=1, source_target_pairs={{0,1},{1,0},{2,3},{3,2},{4,5},{5,4},{6,7},{7,6},{8,9},{9,8},{10,11... | collective-permute-start | bytes 393224 | tf_op jit(solution)/shard_map/ppermute | solution.py:732
  79.3 4.3 %collective-permute-start.17 = (f32[8,32,128]{2,1,0:T(8,128)S(1)}, f32[8,32,128]{2,1,0:T(8,128)S(1)}, u32[]{:S(2)}, u32[]{:S(2)}) collective-permute-start(f32[8,32,128]{2,1,0:T(8,128)S(1)} %collective-permute-done.13.m2), channel_id=1, source_target_pairs={{0,1},{1,0},{2,3},{3,2},{4,5},{5,4},{6,7},{7,6},{8,9},{9,8},{10,11... | collective-permute-start | bytes 393224 | tf_op jit(solution)/shard_map/ppermute | solution.py:732
  81.8 2.9 %collective-permute-start.16 = (f32[8,32,128]{2,1,0:T(8,128)S(1)}, f32[8,32,128]{2,1,0:T(8,128)S(1)}, u32[]{:S(2)}, u32[]{:S(2)}) collective-permute-start(f32[8,32,128]{2,1,0:T(8,128)S(1)} %collective-permute-done.12.m1), channel_id=1, source_target_pairs={{0,1},{1,0},{2,3},{3,2},{4,5},{5,4},{6,7},{7,6},{8,9},{9,8},{10,11... | collective-permute-start | bytes 393224 | tf_op jit(solution)/shard_map/ppermute | solution.py:732

commit v10 on v9

--- a/solution.py
+++ b/solution.py
@@ -245,8 +245,7 @@
     above = jnp.where(gx < 3, 1.0, 0.0).astype(F32)
     left = jnp.where(gy > 0, 1.0, 0.0).astype(F32)
     right = jnp.where(gy < 3, 1.0, 0.0).astype(F32)
-    vr[...] = jnp.zeros_like(vr)
-    vb[...] = jnp.zeros_like(vb)
+    clear((vr, vb))
     edge = jnp.zeros((8, 128), F32)
     for b in (br, bb):
         for q in range(34):
@@ -370,8 +369,7 @@
     keep = own | ((lane % 64 < 48) & (gz < 7)) | ((lane % 64 >= 48) & (gz > 0))
     kept = jnp.where(keep, 1.0, 0.0).astype(F32)
     halo = (lane + jnp.where(lane % 64 < 48, 6, -6)) % 128
-    for v in (vr, vb):
-        v[...] = jnp.zeros_like(v)
+    clear((vr, vb))
     for b in (br, bb):
         b[:, 0:8] = jnp.zeros((18, 8, 128), F32)
         b[:, 72:80] = jnp.zeros((18, 8, 128), F32)
@@ -446,9 +444,13 @@
     return [pltpu.VMEM((planes + 2, rows + 16, 128), F32)] * 4 + [pltpu.VMEM((8, planes, rows, 128), F32)] * 2
 
 
-def clear(refs):
+def clear(refs, ends=1):
     for v in refs:
-        v[...] = jnp.zeros_like(v)
+        planes, rows, _ = v.shape
+        v[:, 0:8] = jnp.zeros((planes, 8, 128), F32)
+        v[:, rows - 8 : rows] = jnp.zeros((planes, 8, 128), F32)
+        v[0:ends] = jnp.zeros((ends, rows, 128), F32)
+        v[planes - ends : planes] = jnp.zeros((ends, rows, 128), F32)
 
 
 def smooth_down(br, bb, vr, vb, cr, cb, f_of, index, scale, planes, rows, inside):
@@ -519,7 +521,8 @@
     ]
     for c in copies:
         c.start()
-    clear((b2r, b2b, v2r, v2b, b3r, b3b, v3r, v3b, b4r, b4b, v4r, v4b, v1r, v0r))
+    clear((b2r, b2b, v2r, v2b, b3r, b3b, v3r, v3b, b4r, b4b, v4r, v4b, v1r))
+    clear((v0r,), 5)
     v0b[:, 0:8] = jnp.zeros((34, 8, 128), F32)
     v0b[:, 56:64] = jnp.zeros((34, 8, 128), F32)
     v1b[:, 0:8] = jnp.zeros((18, 8, 128), F32)

time: 100 us -> 99.9 us (level)
  no operation moved by 1% of the time
where the time goes in v10:
time: 99.9 us; the launch traced here: 99.7 us
  starting transfers between devices  33.5 us (34%)
  Pallas kernels  30.5 us (31%)
  blocking collectives  19.1 us (19%)
  waiting for transfers between devices  14.6 us (15%)
  other arithmetic  1.14 us (1%)
    pallas_call x6, Pallas kernels, call(): pl.pallas_call(kernel, out_shape=out[0], in_specs=specs or [vmem] * len(a...  30.5 us
    all_to_all x1, blocking collectives, body(): g = lax.all_to_all(g, ('gx', 'gy'), 0, 0, tiled=True)  19.1 us
    ppermute x6, waiting for transfers between devices, beyond(): lax.ppermute(x, axis, [(i, (i + d) % count) for i in range(count)])  9.74 us
    ppermute x4, starting transfers between devices, body(): pair = [lax.ppermute(w, 'gz', [(i, i ^ 1) for i in range(8)]) for w in mine]  8.77 us
    ppermute x3, starting transfers between devices, around(): lax.ppermute(hi, axis, [(i, (i + 1) % count) for i in range(count)])  7.51 us
    ppermute x3, starting transfers between devices, body(): lax.ppermute(w2, 'gz', [(i, (i + d) % 8) for i in range(8)])  6.48 us
    ppermute x6, starting transfers between devices, beyond(): lax.ppermute(x, axis, [(i, (i + d) % count) for i in range(count)])  6.09 us
    ppermute x3, starting transfers between devices, around(): lax.ppermute(lo, axis, [((i + 1) % count, i) for i in range(count)])  4.64 us
  transfers between devices with their start and end apart: 19, of which 7 were waited for; matrix products, arithmetic and copies ran while one was open for 0% of the time, Pallas kernels for 0%

profile of v10, /device:TPU:1, one launch (start us, length us, event | category | flops | bytes accessed | tf_op | source)
XLA Modules:
  0.0 99.7 jit_solution(14790630411910691998)
XLA Ops:
  0.6 1.1 %pad_maximum_fusion.both_ref = f32[32,32,128]{2,1,0:T(8,128)S(1)} fusion(f32[16,32,128]{2,1,0:T(8,128)} %param.3, f32[16,32,128]{2,1,0:T(8,128)} %param.2), kind=kLoop, calls=%fused_computation | loop fusion | flops 131072 | bytes 1048576 | tf_op jit(solution)/shard_map/concatenate | solution.py:693
  2.4 2.5 %collective-permute-start = (f32[17,32,128]{2,1,0:T(8,128)S(1)}, f32[17,32,128]{2,1,0:T(8,128)S(1)}, u32[]{:S(2)}, u32[]{:S(2)}) collective-permute-start(f32[17,32,128]{2,1,0:T(8,128)S(1)} %get-tuple-element.26), channel_id=1, source_target_pairs={{0,32},{32,64},{64,96},{96,0},{1,33},{33,65},{65,97},{97,1},{2,34}... | collective-permute-start | bytes 835592 | tf_op jit(solution)/shard_map/ppermute | solution.py:675
  4.9 2.2 %collective-permute-start.1 = (f32[17,32,128]{2,1,0:T(8,128)S(1)}, f32[17,32,128]{2,1,0:T(8,128)S(1)}, u32[]{:S(2)}, u32[]{:S(2)}) collective-permute-start(f32[17,32,128]{2,1,0:T(8,128)S(1)} %get-tuple-element.27), channel_id=1, source_target_pairs={{32,0},{64,32},{96,64},{0,96},{33,1},{65,33},{97,65},{1,97},{34,2}... | collective-permute-start | bytes 835592 | tf_op jit(solution)/shard_map/ppermute | solution.py:674
  7.1 2.7 %collective-permute-start.4 = (f32[64,128]{1,0:T(8,128)S(1)}, f32[64,128]{1,0:T(8,128)S(1)}, u32[]{:S(2)}, u32[]{:S(2)}) collective-permute-start(f32[64,128]{1,0:T(8,128)S(1)} %get-tuple-element.28.b0), channel_id=1, source_target_pairs={{0,24},{8,0},{16,8},{24,16},{1,25},{9,1},{17,9},{25,17},{2,26},{10... | collective-permute-start | bytes 98312 | tf_op jit(solution)/shard_map/ppermute | solution.py:681
  10.9 3.3 %collective-permute-done.3.b2 = f32[64,128]{1,0:T(8,128)S(1)} collective-permute-done((f32[64,128]{1,0:T(8,128)S(1)}, f32[64,128]{1,0:T(8,128)S(1)}, u32[]{:S(2)}, u32[]{:S(2)}) %collective-permute-start.3) | collective-permute-done | bytes 32800 | tf_op jit(solution)/shard_map/ppermute | solution.py:681
  14.9 2.4 %collective-permute-start.6 = (f32[66,8,128]{2,1,0:T(8,128)S(1)}, f32[66,8,128]{2,1,0:T(8,128)S(1)}, u32[]{:S(2)}, u32[]{:S(2)}) collective-permute-start(f32[66,8,128]{2,1,0:T(8,128)S(1)} %get-tuple-element.30), channel_id=1, source_target_pairs={{8,0},{16,8},{24,16},{0,24},{9,1},{17,9},{25,17},{1,25},{10,2},{18... | collective-permute-start | bytes 811016 | tf_op jit(solution)/shard_map/ppermute | solution.py:674
  17.3 3.8 %collective-permute-done.5.yl = f32[66,8,128]{2,1,0:T(8,128)S(1)} collective-permute-done((f32[66,8,128]{2,1,0:T(8,128)S(1)}, f32[66,8,128]{2,1,0:T(8,128)S(1)}, u32[]{:S(2)}, u32[]{:S(2)}) %collective-permute-start.5) | collective-permute-done | bytes 270368 | tf_op jit(solution)/shard_map/ppermute | solution.py:675
  21.2 1.1 %pack_lanes.1 = (f32[96,8,128]{2,1,0:T(8,128)S(1)}, f32[96,8,128]{2,1,0:T(8,128)}) custom-call(f32[16,32,128]{2,1,0:T(8,128)S(1)} %get-tuple-element.24.wf, f32[16,32,128]{2,1,0:T(8,128)S(1)} %get-tuple-element.25.wb, f32[17,32,128]{2,1,0:T(8,128)S(1)} %collective-permute-done.xl, f32[17,32,128]{2,1,0:T(8,128)S(1)} %collective-permute-done.1.xu, ...), custom_call_target="tpu_custom_call" | custom-call | tf_op jit(solution)/shard_map/pack_lanes/pallas_call | solution.py:55
  22.3 4.7 %collective-permute-start.7 = (f32[96,8,128]{2,1,0:T(8,128)}, f32[96,8,128]{2,1,0:T(8,128)S(1)}, u32[]{:S(2)}, u32[]{:S(2)}) collective-permute-start(f32[96,8,128]{2,1,0:T(8,128)} %get-tuple-element.31), channel_id=1, source_target_pairs={{0,1},{1,2},{2,3},{3,4},{4,5},{5,6},{6,7},{7,0},{8,9},{9,10},{10,1... | collective-permute-start | bytes 1179656 | tf_op jit(solution)/shard_map/ppermute | solution.py:675
  27.0 1.7 %collective-permute-start.11 = (f32[4,64,128]{2,1,0:T(8,128)S(1)}, f32[4,64,128]{2,1,0:T(8,128)S(1)}, u32[]{:S(2)}, u32[]{:S(2)}) collective-permute-start(f32[4,64,128]{2,1,0:T(8,128)S(1)} %get-tuple-element.37.h0), channel_id=1, source_target_pairs={{0,96},{32,0},{64,32},{96,64},{1,97},{33,1},{65,33},{97,65},{2,98}... | collective-permute-start | bytes 393224 | tf_op jit(solution)/shard_map/ppermute | solution.py:681
  29.4 2.5 %collective-permute-done.11.h3 = f32[4,64,128]{2,1,0:T(8,128)S(1)} collective-permute-done((f32[4,64,128]{2,1,0:T(8,128)S(1)}, f32[4,64,128]{2,1,0:T(8,128)S(1)}, u32[]{:S(2)}, u32[]{:S(2)}) %collective-permute-start.11) | collective-permute-done | bytes 131104 | tf_op jit(solution)/shard_map/ppermute | solution.py:681
  31.9 2.2 %collective-permute-done.10.h2 = f32[4,64,128]{2,1,0:T(8,128)S(1)} collective-permute-done((f32[4,64,128]{2,1,0:T(8,128)S(1)}, f32[4,64,128]{2,1,0:T(8,128)S(1)}, u32[]{:S(2)}, u32[]{:S(2)}) %collective-permute-start.10) | collective-permute-done | bytes 131104 | tf_op jit(solution)/shard_map/ppermute | solution.py:681
  34.1 1.4 %collective-permute-done.9.h1 = f32[4,64,128]{2,1,0:T(8,128)S(1)} collective-permute-done((f32[4,64,128]{2,1,0:T(8,128)S(1)}, f32[4,64,128]{2,1,0:T(8,128)S(1)}, u32[]{:S(2)}, u32[]{:S(2)}) %collective-permute-start.9) | collective-permute-done | bytes 131104 | tf_op jit(solution)/shard_map/ppermute | solution.py:681
  35.5 7.3 %fine_down.1 = (f32[16,128,128]{2,1,0:T(8,128)S(1)}, f32[8,24,48,128]{3,2,1,0:T(8,128)}, f32[9,26,48,128]{3,2,1,0:T(8,128)}) custom-call(s32[3]{0:T(128)S(1)} %pad_add_fusion.at, f32[16,32,128]{2,1,0:T(8,128)S(1)} %get-tuple-element.24.wf, f32[16,32,128]{2,1,0:T(8,128)S(1)} %get-tuple-element.25.wb, f32[17,32,128]{2,1,0:T(8,128)S(1)} %collective-permute-done.xl, ...), custom_call_target="tpu_custom_call" | custom-call | tf_op jit(solution)/shard_map/fine_down/pallas_call | solution.py:55
  42.9 19.1 %all_to_all.5.g = f32[16,128,128]{2,1,0:T(8,128)S(1)} all-to-all(f32[16,128,128]{2,1,0:T(8,128)S(1)} %get-tuple-element.36), channel_id=1, replica_groups=mesh['gx'=4,'gy'=4,'gz'=8] {'gx','gy'}, dimensions={0} | all-to-all | bytes 2097152 | tf_op jit(solution)/shard_map/all_to_all | solution.py:720
  62.0 6.3 %mid_down.1 = (f32[8,32,128]{2,1,0:T(8,128)S(1)}, f32[2,8,16,32,128]{4,3,2,1,0:T(8,128)}, f32[18,32,128]{2,1,0:T(8,128)S(1)}) custom-call(s32[3]{0:T(128)S(1)} %pad_add_fusion.at, f32[16,128,128]{2,1,0:T(8,128)S(1)} %all_to_all.5.g, f32[4,64,128]{2,1,0:T(8,128)S(1)} %get-tuple-element.37.h0, f32[4,64,128]{2,1,0:T(8,128)S(1)} %collective-permute-done.9.h1, ...), custom_call_target="tpu_custom_call" | custom-call | tf_op jit(solution)/shard_map/mid_down/pallas_call | solution.py:55
  68.3 3.7 %collective-permute-start.14 = (f32[8,32,128]{2,1,0:T(8,128)S(1)}, f32[8,32,128]{2,1,0:T(8,128)S(1)}, u32[]{:S(2)}, u32[]{:S(2)}) collective-permute-start(f32[8,32,128]{2,1,0:T(8,128)S(1)} %get-tuple-element.41.m0), channel_id=1, source_target_pairs={{0,6},{1,7},{2,0},{3,1},{4,2},{5,3},{6,4},{7,5},{8,14},{9,15},{10,... | collective-permute-start | bytes 393224 | tf_op jit(solution)/shard_map/ppermute | solution.py:734
  72.0 2.5 %collective-permute-start.13 = (f32[8,32,128]{2,1,0:T(8,128)S(1)}, f32[8,32,128]{2,1,0:T(8,128)S(1)}, u32[]{:S(2)}, u32[]{:S(2)}) collective-permute-start(f32[8,32,128]{2,1,0:T(8,128)S(1)} %get-tuple-element.41.m0), channel_id=1, source_target_pairs={{0,4},{1,5},{2,6},{3,7},{4,0},{5,1},{6,2},{7,3},{8,12},{9,13},{10,... | collective-permute-start | bytes 393224 | tf_op jit(solution)/shard_map/ppermute | solution.py:734
  74.8 3.2 %collective-permute-start.15 = (f32[8,32,128]{2,1,0:T(8,128)S(1)}, f32[8,32,128]{2,1,0:T(8,128)S(1)}, u32[]{:S(2)}, u32[]{:S(2)}) collective-permute-start(f32[8,32,128]{2,1,0:T(8,128)S(1)} %get-tuple-element.41.m0), channel_id=1, source_target_pairs={{0,1},{1,0},{2,3},{3,2},{4,5},{5,4},{6,7},{7,6},{8,9},{9,8},{10,11... | collective-permute-start | bytes 393224 | tf_op jit(solution)/shard_map/ppermute | solution.py:735
  78.0 1.3 %collective-permute-start.18 = (f32[8,32,128]{2,1,0:T(8,128)S(1)}, f32[8,32,128]{2,1,0:T(8,128)S(1)}, u32[]{:S(2)}, u32[]{:S(2)}) collective-permute-start(f32[8,32,128]{2,1,0:T(8,128)S(1)} %collective-permute-done.14.m3), channel_id=1, source_target_pairs={{0,1},{1,0},{2,3},{3,2},{4,5},{5,4},{6,7},{7,6},{8,9},{9,8},{10,11... | collective-permute-start | bytes 393224 | tf_op jit(solution)/shard_map/ppermute | solution.py:735
  79.2 2.4 %collective-permute-start.17 = (f32[8,32,128]{2,1,0:T(8,128)S(1)}, f32[8,32,128]{2,1,0:T(8,128)S(1)}, u32[]{:S(2)}, u32[]{:S(2)}) collective-permute-start(f32[8,32,128]{2,1,0:T(8,128)S(1)} %collective-permute-done.13.m2), channel_id=1, source_target_pairs={{0,1},{1,0},{2,3},{3,2},{4,5},{5,4},{6,7},{7,6},{8,9},{9,8},{10,11... | collective-permute-start | bytes 393224 | tf_op jit(solution)/shard_map/ppermute | solution.py:735
  81.7 1.9 %collective-permute-start.16 = (f32[8,32,128]{2,1,0:T(8,128)S(1)}, f32[8,32,128]{2,1,0:T(8,128)S(1)}, u32[]{:S(2)}, u32[]{:S(2)}) collective-permute-start(f32[8,32,128]{2,1,0:T(8,128)S(1)} %collective-permute-done.12.m1), channel_id=1, source_target_pairs={{0,1},{1,0},{2,3},{3,2},{4,5},{5,4},{6,7},{7,6},{8,9},{9,8},{10,11... | collective-permute-start | bytes 393224 | tf_op jit(solution)/shard_map/ppermute | solution.py:735
  83.6 1.0 collective-permute-done.16.q1
  84.6 15.0 %coarse_up.1 = (f32[16,32,128]{2,1,0:T(8,128)}, f32[16,32,128]{2,1,0:T(8,128)}) custom-call(s32[3]{0:T(128)S(1)} %pad_add_fusion.at, f32[8,32,128]{2,1,0:T(8,128)S(1)} %get-tuple-element.41.m0, f32[8,32,128]{2,1,0:T(8,128)S(1)} %collective-permute-done.12.m1, f32[8,32,128]{2,1,0:T(8,128)S(1)} %collective-permute-done.13.m2, ...), custom_call_target="tpu_custom_call" | custom-call | tf_op jit(solution)/shard_map/coarse_up/pallas_call | solution.py:55
  (23 shorter events, 3.5 us)
Async XLA Ops:
  2.4 12.1 %collective-permute-start = (f32[17,32,128]{2,1,0:T(8,128)S(1)}, f32[17,32,128]{2,1,0:T(8,128)S(1)}, u32[]{:S(2)}, u32[]{:S(2)}) collective-permute-start(f32[17,32,128]{2,1,0:T(8,128)S(1)} %get-tuple-element.26), channel_id=1, source_target_pairs={{0,32},{32,64},{64,96},{96,0},{1,33},{33,65},{65,97},{97,1},{2,34}... | collective-permute-start | bytes 835592 | tf_op jit(solution)/shard_map/ppermute | solution.py:675
  4.9 9.6 %collective-permute-start.1 = (f32[17,32,128]{2,1,0:T(8,128)S(1)}, f32[17,32,128]{2,1,0:T(8,128)S(1)}, u32[]{:S(2)}, u32[]{:S(2)}) collective-permute-start(f32[17,32,128]{2,1,0:T(8,128)S(1)} %get-tuple-element.27), channel_id=1, source_target_pairs={{32,0},{64,32},{96,64},{0,96},{33,1},{65,33},{97,65},{1,97},{34,2}... | collective-permute-start | bytes 835592 | tf_op jit(solution)/shard_map/ppermute | solution.py:674
  7.1 3.8 %collective-permute-start.4 = (f32[64,128]{1,0:T(8,128)S(1)}, f32[64,128]{1,0:T(8,128)S(1)}, u32[]{:S(2)}, u32[]{:S(2)}) collective-permute-start(f32[64,128]{1,0:T(8,128)S(1)} %get-tuple-element.28.b0), channel_id=1, source_target_pairs={{0,24},{8,0},{16,8},{24,16},{1,25},{9,1},{17,9},{25,17},{2,26},{10... | collective-permute-start | bytes 98312 | tf_op jit(solution)/shard_map/ppermute | solution.py:681
  9.9 4.3 %collective-permute-start.3 = (f32[64,128]{1,0:T(8,128)S(1)}, f32[64,128]{1,0:T(8,128)S(1)}, u32[]{:S(2)}, u32[]{:S(2)}) collective-permute-start(f32[64,128]{1,0:T(8,128)S(1)} %get-tuple-element.28.b0), channel_id=1, source_target_pairs={{0,16},{8,24},{16,0},{24,8},{1,17},{9,25},{17,1},{25,9},{2,18},{10... | collective-permute-start | bytes 98312 | tf_op jit(solution)/shard_map/ppermute | solution.py:681
  10.2 4.3 %collective-permute-start.2 = (f32[64,128]{1,0:T(8,128)S(1)}, f32[64,128]{1,0:T(8,128)S(1)}, u32[]{:S(2)}, u32[]{:S(2)}) collective-permute-start(f32[64,128]{1,0:T(8,128)S(1)} %get-tuple-element.28.b0), channel_id=1, source_target_pairs={{0,8},{8,16},{16,24},{24,0},{1,9},{9,17},{17,25},{25,1},{2,10},{10... | collective-permute-start | bytes 98312 | tf_op jit(solution)/shard_map/ppermute | solution.py:681
  14.6 6.6 %collective-permute-start.5 = (f32[66,8,128]{2,1,0:T(8,128)S(1)}, f32[66,8,128]{2,1,0:T(8,128)S(1)}, u32[]{:S(2)}, u32[]{:S(2)}) collective-permute-start(f32[66,8,128]{2,1,0:T(8,128)S(1)} %get-tuple-element.29), channel_id=1, source_target_pairs={{0,8},{8,16},{16,24},{24,0},{1,9},{9,17},{17,25},{25,1},{2,10},{10... | collective-permute-start | bytes 811016 | tf_op jit(solution)/shard_map/ppermute | solution.py:675
  14.9 6.3 %collective-permute-start.6 = (f32[66,8,128]{2,1,0:T(8,128)S(1)}, f32[66,8,128]{2,1,0:T(8,128)S(1)}, u32[]{:S(2)}, u32[]{:S(2)}) collective-permute-start(f32[66,8,128]{2,1,0:T(8,128)S(1)} %get-tuple-element.30), channel_id=1, source_target_pairs={{8,0},{16,8},{24,16},{0,24},{9,1},{17,9},{25,17},{1,25},{10,2},{18... | collective-permute-start | bytes 811016 | tf_op jit(solution)/shard_map/ppermute | solution.py:674
  22.3 13.2 %collective-permute-start.7 = (f32[96,8,128]{2,1,0:T(8,128)}, f32[96,8,128]{2,1,0:T(8,128)S(1)}, u32[]{:S(2)}, u32[]{:S(2)}) collective-permute-start(f32[96,8,128]{2,1,0:T(8,128)} %get-tuple-element.31), channel_id=1, source_target_pairs={{0,1},{1,2},{2,3},{3,4},{4,5},{5,6},{6,7},{7,0},{8,9},{9,10},{10,1... | collective-permute-start | bytes 1179656 | tf_op jit(solution)/shard_map/ppermute | solution.py:675
  27.0 8.6 %collective-permute-start.8 = (f32[96,8,128]{2,1,0:T(8,128)S(1)}, f32[96,8,128]{2,1,0:T(8,128)S(1)}, u32[]{:S(2)}, u32[]{:S(2)}) collective-permute-start(f32[96,8,128]{2,1,0:T(8,128)S(1)} %get-tuple-element.32), channel_id=1, source_target_pairs={{1,0},{2,1},{3,2},{4,3},{5,4},{6,5},{7,6},{0,7},{9,8},{10,9},{11,1... | collective-permute-start | bytes 1179656 | tf_op jit(solution)/shard_map/ppermute | solution.py:674
  27.0 4.9 %collective-permute-start.11 = (f32[4,64,128]{2,1,0:T(8,128)S(1)}, f32[4,64,128]{2,1,0:T(8,128)S(1)}, u32[]{:S(2)}, u32[]{:S(2)}) collective-permute-start(f32[4,64,128]{2,1,0:T(8,128)S(1)} %get-tuple-element.37.h0), channel_id=1, source_target_pairs={{0,96},{32,0},{64,32},{96,64},{1,97},{33,1},{65,33},{97,65},{2,98}... | collective-permute-start | bytes 393224 | tf_op jit(solution)/shard_map/ppermute | solution.py:681
  28.6 5.4 %collective-permute-start.10 = (f32[4,64,128]{2,1,0:T(8,128)S(1)}, f32[4,64,128]{2,1,0:T(8,128)S(1)}, u32[]{:S(2)}, u32[]{:S(2)}) collective-permute-start(f32[4,64,128]{2,1,0:T(8,128)S(1)} %get-tuple-element.37.h0), channel_id=1, source_target_pairs={{0,64},{32,96},{64,0},{96,32},{1,65},{33,97},{65,1},{97,33},{2,66}... | collective-permute-start | bytes 393224 | tf_op jit(solution)/shard_map/ppermute | solution.py:681
  28.6 6.9 %collective-permute-start.9 = (f32[4,64,128]{2,1,0:T(8,128)S(1)}, f32[4,64,128]{2,1,0:T(8,128)S(1)}, u32[]{:S(2)}, u32[]{:S(2)}) collective-permute-start(f32[4,64,128]{2,1,0:T(8,128)S(1)} %get-tuple-element.37.h0), channel_id=1, source_target_pairs={{0,32},{32,64},{64,96},{96,0},{1,33},{33,65},{65,97},{97,1},{2,34}... | collective-permute-start | bytes 393224 | tf_op jit(solution)/shard_map/ppermute | solution.py:681
  68.3 9.7 %collective-permute-start.14 = (f32[8,32,128]{2,1,0:T(8,128)S(1)}, f32[8,32,128]{2,1,0:T(8,128)S(1)}, u32[]{:S(2)}, u32[]{:S(2)}) collective-permute-start(f32[8,32,128]{2,1,0:T(8,128)S(1)} %get-tuple-element.41.m0), channel_id=1, source_target_pairs={{0,6},{1,7},{2,0},{3,1},{4,2},{5,3},{6,4},{7,5},{8,14},{9,15},{10,... | collective-permute-start | bytes 393224 | tf_op jit(solution)/shard_map/ppermute | solution.py:734
  72.0 7.3 %collective-permute-start.13 = (f32[8,32,128]{2,1,0:T(8,128)S(1)}, f32[8,32,128]{2,1,0:T(8,128)S(1)}, u32[]{:S(2)}, u32[]{:S(2)}) collective-permute-start(f32[8,32,128]{2,1,0:T(8,128)S(1)} %get-tuple-element.41.m0), channel_id=1, source_target_pairs={{0,4},{1,5},{2,6},{3,7},{4,0},{5,1},{6,2},{7,3},{8,12},{9,13},{10,... | collective-permute-start | bytes 393224 | tf_op jit(solution)/shard_map/ppermute | solution.py:734
  74.5 7.2 %collective-permute-start.12 = (f32[8,32,128]{2,1,0:T(8,128)S(1)}, f32[8,32,128]{2,1,0:T(8,128)S(1)}, u32[]{:S(2)}, u32[]{:S(2)}) collective-permute-start(f32[8,32,128]{2,1,0:T(8,128)S(1)} %get-tuple-element.41.m0), channel_id=1, source_target_pairs={{0,2},{1,3},{2,4},{3,5},{4,6},{5,7},{6,0},{7,1},{8,10},{9,11},{10,... | collective-permute-start | bytes 393224 | tf_op jit(solution)/shard_map/ppermute | solution.py:734
  74.8 8.8 %collective-permute-start.15 = (f32[8,32,128]{2,1,0:T(8,128)S(1)}, f32[8,32,128]{2,1,0:T(8,128)S(1)}, u32[]{:S(2)}, u32[]{:S(2)}) collective-permute-start(f32[8,32,128]{2,1,0:T(8,128)S(1)} %get-tuple-element.41.m0), channel_id=1, source_target_pairs={{0,1},{1,0},{2,3},{3,2},{4,5},{5,4},{6,7},{7,6},{8,9},{9,8},{10,11... | collective-permute-start | bytes 393224 | tf_op jit(solution)/shard_map/ppermute | solution.py:735
  78.0 5.6 %collective-permute-start.18 = (f32[8,32,128]{2,1,0:T(8,128)S(1)}, f32[8,32,128]{2,1,0:T(8,128)S(1)}, u32[]{:S(2)}, u32[]{:S(2)}) collective-permute-start(f32[8,32,128]{2,1,0:T(8,128)S(1)} %collective-permute-done.14.m3), channel_id=1, source_target_pairs={{0,1},{1,0},{2,3},{3,2},{4,5},{5,4},{6,7},{7,6},{8,9},{9,8},{10,11... | collective-permute-start | bytes 393224 | tf_op jit(solution)/shard_map/ppermute | solution.py:735
  79.2 4.3 %collective-permute-start.17 = (f32[8,32,128]{2,1,0:T(8,128)S(1)}, f32[8,32,128]{2,1,0:T(8,128)S(1)}, u32[]{:S(2)}, u32[]{:S(2)}) collective-permute-start(f32[8,32,128]{2,1,0:T(8,128)S(1)} %collective-permute-done.13.m2), channel_id=1, source_target_pairs={{0,1},{1,0},{2,3},{3,2},{4,5},{5,4},{6,7},{7,6},{8,9},{9,8},{10,11... | collective-permute-start | bytes 393224 | tf_op jit(solution)/shard_map/ppermute | solution.py:735
  81.7 2.9 %collective-permute-start.16 = (f32[8,32,128]{2,1,0:T(8,128)S(1)}, f32[8,32,128]{2,1,0:T(8,128)S(1)}, u32[]{:S(2)}, u32[]{:S(2)}) collective-permute-start(f32[8,32,128]{2,1,0:T(8,128)S(1)} %collective-permute-done.12.m1), channel_id=1, source_target_pairs={{0,1},{1,0},{2,3},{3,2},{4,5},{5,4},{6,7},{7,6},{8,9},{9,8},{10,11... | collective-permute-start | bytes 393224 | tf_op jit(solution)/shard_map/ppermute | solution.py:735
